TPU v7x, 128 devices: a whole 4x4x4 slice. The times are simulated.
128 devices in a mesh: gx: 32 (over z, x_hi, y), gy: 4 (over x_lo, core).
Axes of the slice: x: 4 (x_hi: 2, x_lo: 2; x = x_hi * 2 + x_lo), y: 4, z: 4, core: 2. Of those that a mesh axis runs over, the one named last changes fastest.
Arguments:
- temp_start: float32 [8, 2048, 4096], P(None, 'gx', 'gy'), may hold values from -6 to 6
- conduct: float32 [2048, 4096], P('gx', 'gy'), may hold values from 0.2 to 1
- adjoint_in: float32 [8, 2048, 4096], P(None, 'gx', 'gy'), may hold values from -6 to 6
- grad_in: float32 [2048, 4096], P('gx', 'gy'), may hold values from -6 to 6
- observed: float32 [4, 8192, 1024], P(None, ('gx', 'gy')), may hold values from -6 to 6
- frame_index: int32 [8192], P(('gx', 'gy')), may hold values from 0 to 3
- source_map: int32 [8192, 4], P(('gx', 'gy')), may hold values from 0 to 8191, as said below
- source_weight: float32 [8192, 4], P(('gx', 'gy')), may hold values from 0.2 to 0.6
Outputs:
- misfit: float32 [8192, 1024], P(('gx', 'gy'))
- adjoint_out: float32 [8, 2048, 4096], P(None, 'gx', 'gy')
- grad_out: float32 [2048, 4096], P('gx', 'gy')
Inputs may be any that keep to these rules, and one draw needn't show every extreme that they name: `source_map`: each camera tile's blocks lie in plate tiles of devices with the same gy index as the device that holds the camera tile. Of the 256 blocks of one device's camera tiles, at most 16 lie on any one plate device, and exactly 16 on each of 8 of them.
All inputs are finite; a program needn't handle non-finite values.
Results may differ from a plain program's by a relative error of at most 0.00008.
Values sent between devices are 32-bit elements; how exact they have to be, the bound alone decides.
A program may use at most 64 MiB of HBM per device.

v0:
```python
import jax
import jax.numpy as jnp
from jax import lax
from jax.sharding import PartitionSpec as P

TR = 8
TC = 128


RATE_PLANE = 0.2
RATE_VERTICAL = 0.08


def extended(block, sides, width):
    for axis, dim in sides:
        count = lax.axis_size(axis)
        forward = [(i, i + 1) for i in range(count - 1)]
        backward = [(target, source) for source, target in forward]
        low = lax.ppermute(
            lax.slice_in_dim(block, block.shape[dim] - width, None, axis=dim), axis, forward
        )
        high = lax.ppermute(lax.slice_in_dim(block, 0, width, axis=dim), axis, backward)
        block = jnp.concatenate([low, block, high], axis=dim)
    return block


def plane_term(fpad, kpad):
    centre = fpad[..., 1:-1, 1:-1]
    kcentre = kpad[1:-1, 1:-1]
    total = 0.5 * (kcentre + kpad[2:, 1:-1]) * (fpad[..., 2:, 1:-1] - centre)
    total = total + 0.5 * (kcentre + kpad[:-2, 1:-1]) * (fpad[..., :-2, 1:-1] - centre)
    total = total + 0.5 * (kcentre + kpad[1:-1, 2:]) * (fpad[..., 1:-1, 2:] - centre)
    total = total + 0.5 * (kcentre + kpad[1:-1, :-2]) * (fpad[..., 1:-1, :-2] - centre)
    return total


def vertical(field):
    zero_layer = jnp.zeros(field[:1].shape, jnp.float32)
    lower = jnp.concatenate([field[1:] - field[:-1], zero_layer], axis=0)
    upper = jnp.concatenate([zero_layer, field[:-1] - field[1:]], axis=0)
    return RATE_VERTICAL * (lower + upper)


def face_grad(tpad, lpad):
    tcen = tpad[:, 1:-1, 1:-1]
    lcen = lpad[:, 1:-1, 1:-1]
    total = 0.5 * (tpad[:, 2:, 1:-1] - tcen) * (lcen - lpad[:, 2:, 1:-1])
    total = total + 0.5 * (tpad[:, :-2, 1:-1] - tcen) * (lcen - lpad[:, :-2, 1:-1])
    total = total + 0.5 * (tpad[:, 1:-1, 2:] - tcen) * (lcen - lpad[:, 1:-1, 2:])
    total = total + 0.5 * (tpad[:, 1:-1, :-2] - tcen) * (lcen - lpad[:, 1:-1, :-2])
    return jnp.sum(total, axis=0)


def local_tiles(plane):
    rows, cols = plane.shape
    shaped = plane.reshape(rows // TR, TR, cols // TC, TC)
    return shaped.transpose(0, 2, 1, 3).reshape(rows // TR * (cols // TC), TR * TC)


def local_plane(tiles, rows, cols):
    shaped = tiles.reshape(rows // TR, cols // TC, TR, TC)
    return shaped.transpose(0, 2, 1, 3).reshape(rows, cols)


def local(
    temp_start, conduct, adjoint_in, grad_in, observed, frame_index, source_map, source_weight
):
    layers, rows, cols = temp_start.shape
    tiles = rows // TR * (cols // TC)
    n_cols = lax.axis_size("gy")
    stacked = jnp.concatenate([temp_start, conduct[None]], axis=0)
    padded = extended(stacked, (("gx", 1), ("gy", 2)), 1)
    temp_pad = padded[:layers]
    kpad = padded[layers]
    top_now = temp_start[-1]
    top_next = (
        top_now
        + RATE_PLANE * plane_term(temp_pad[-1], kpad)
        + RATE_VERTICAL * (temp_start[-2] - top_now)
    )
    top_tiles = local_tiles(top_next)
    frames = observed.shape[0]
    picks = frame_index[None, :, None] == jnp.arange(frames, dtype=jnp.int32)[:, None, None]
    frame_obs = jnp.sum(jnp.where(picks, observed, 0.0), axis=0)
    plate_row = source_map // tiles // n_cols
    local_index = source_map % tiles
    column_index = plate_row * tiles + local_index

    def select_block(count):
        hits = column_index[:, :, None] == jnp.arange(count, dtype=jnp.int32)[None, None, :]
        return jnp.sum(jnp.where(hits, source_weight[:, :, None], 0.0), axis=1)

    piece = lax.all_gather(top_tiles, "gx", axis=0, tiled=True)
    select = select_block(piece.shape[0])
    predicted = jnp.dot(
        select, piece, precision=lax.Precision.HIGHEST, preferred_element_type=jnp.float32
    )
    misfit = predicted - frame_obs
    select = select_block(tiles * lax.axis_size("gx"))
    added_tiles = lax.psum_scatter(
        jnp.dot(
            select.T, misfit, precision=lax.Precision.HIGHEST, preferred_element_type=jnp.float32
        ),
        "gx",
        scatter_dimension=0,
        tiled=True,
    )
    added = local_plane(added_tiles, rows, cols)
    adjoint_next = adjoint_in.at[-1].add(added)
    adj_pad = extended(adjoint_next, (("gx", 1), ("gy", 2)), 1)
    adjoint_out = adjoint_next + RATE_PLANE * plane_term(adj_pad, kpad) + vertical(adjoint_next)
    grad_out = grad_in + RATE_PLANE * face_grad(temp_pad, adj_pad)
    return (misfit, adjoint_out, grad_out)


def solution(mesh):
    placed = (
        P(None, "gx", "gy"),
        P("gx", "gy"),
        P(None, "gx", "gy"),
        P("gx", "gy"),
        P(None, ("gx", "gy"), None),
        P(("gx", "gy")),
        P(("gx", "gy"), None),
        P(("gx", "gy"), None),
    )
    return jax.shard_map(
        local,
        mesh=mesh,
        in_specs=placed,
        out_specs=(P(("gx", "gy"), None), P(None, "gx", "gy"), P("gx", "gy")),
        check_vma=False,
    )
```

profile of v0, /device:TPU:0, one launch (start us, length us, event | category | flops | bytes accessed | tf_op | source)
XLA Modules:
  0.0 402.5 jit_solution(11395471040664376536)
XLA Ops:
  7.2 0.0 copy-start.1
  7.2 0.0 all-gather.2.cloned.1.call-start
  7.2 1.5 copy-done.1
  8.8 0.1 pad_maximum_fusion.25
  8.8 3.6 collective-permute-start
  12.4 1.3 collective-permute-start.1
  13.7 0.3 collective-permute-done
  14.0 4.2 %collective-permute-done.1 = f32[9,1,1024]{2,1,0:T(1,128)S(1)} collective-permute-done((f32[9,1,1024]{2,1,0:T(1,128)S(1)}, f32[9,1,1024]{2,1,0:T(1,128)S(1)}, u32[]{:S(2)}, u32[]{:S(2)}) %collective-permute-start.1) | collective-permute-done | bytes 36896 | tf_op jit(solution)/shard_map/ppermute | solution.py:22
  18.2 0.4 pad_maximum_fusion
  18.6 0.2 copy-done.12
  18.9 1.5 copy-done.3
  20.4 0.2 fusion.59
  20.6 1.3 collective-permute-start.2
  21.9 1.3 collective-permute-start.3
  23.2 3.9 collective-permute-done.3
  27.1 4.6 %concatenate.47 = f32[9,66,1026]{2,1,0:T(8,128)} concatenate(f32[9,66,1]{2,1,0:T(8,128)S(1)} %collective-permute-done.2, f32[9,66,1024]{2,1,0:T(8,128)} %copy-done.3, f32[9,66,1]{2,1,0:T(8,128)S(1)} %collective-permute-done.3), dimensions={2} | concatenate | bytes 4875552 | tf_op jit(solution)/shard_map/concatenate | solution.py:23
  31.7 1.1 slice_bitcast_fusion.1
  32.8 0.0 copy-start.16
  32.9 1.5 fusion.39
  34.3 0.8 copy.15
  35.1 0.0 all-gather.2.cloned.1.call-update
  35.1 0.0 reduce-scatter.2.cloned.1.call-start
  35.2 1.4 select_reduce_fusion.1
  36.6 0.3 select_reduce_fusion
  37.0 114.0 %all-gather.2.cloned.1.call-done = f32[2048,1024]{1,0:T(8,128)} async-done(((f32[64,1024]{1,0:T(8,128)}), f32[2048,1024]{1,0:T(8,128)}) %all-gather.2.cloned.1.call-update) | async-done | bytes 8388624 | tf_op jit(solution)/shard_map/all_gather | solution.py:93
  151.0 7.5 %convolution_subtract_fusion = f32[64,1024]{1,0:T(8,128)S(1)} fusion(f32[64,1024]{1,0:T(8,128)S(1)} %select_reduce_fusion.1, f32[64,2048]{1,0:T(8,128)S(1)} %select_reduce_fusion, f32[2048,1024]{1,0:T(8,128)} %all-gather.2.cloned.1.call-done), kind=kOutput, calls=%fused_computation.59 | convolution fusion | flops 1610678272 | bytes 9437184 | tf_op jit(solution)/shard_map/dot_general | solution.py:95
  158.5 0.0 copy-start.5
  158.5 9.0 %fusion.61 = f32[2048,1024]{1,0:T(8,128)} fusion(f32[64,2048]{1,0:T(8,128)S(1)} %select_reduce_fusion, f32[64,1024]{1,0:T(8,128)S(1)} %convolution_subtract_fusion), kind=kOutput, calls=%fused_computation.115 | convolution fusion | flops 1610612736 | bytes 9175040 | tf_op jit(solution)/shard_map/dot_general | solution.py:101
  167.5 0.0 reduce-scatter.2.cloned.1.call-update
  167.6 201.5 %reduce-scatter.2.cloned.1.call-done = f32[64,1024]{1,0:T(8,128)} async-done(((f32[2048,1024]{1,0:T(8,128)}), f32[64,1024]{1,0:T(8,128)}) %reduce-scatter.2.cloned.1.call-update) | async-done | bytes 262160 | tf_op jit(solution)/shard_map/reduce_scatter | solution.py:100
  369.1 1.0 reshape.79
  370.1 0.1 add_dynamic-update-slice_fusion
  370.2 0.1 fusion.60
  370.2 1.3 collective-permute-start.4
  371.5 4.5 %collective-permute-start.5 = (f32[8,1,1024]{2,1,0:T(1,128)S(1)}, f32[8,1,1024]{2,1,0:T(1,128)S(1)}, u32[]{:S(2)}, u32[]{:S(2)}) collective-permute-start(f32[8,1,1024]{2,1,0:T(1,128)S(1)} %get-tuple-element.30), channel_id=1, source_target_pairs={{0,4},{4,8},{8,12},{12,16},{16,20},{20,24},{24,28},{28,32},{32,36}... | collective-permute-start | bytes 98312 | tf_op jit(solution)/shard_map/ppermute | solution.py:19
  376.1 0.0 collective-permute-done.4
  376.1 1.6 collective-permute-done.5
  377.7 0.2 pad_maximum_fusion.23
  377.8 1.3 collective-permute-start.6
  379.1 0.0 copy-start.2
  379.2 3.4 collective-permute-start.7
  382.5 0.6 slice_subtract_fusion.1
  383.1 0.0 copy-start.9
  383.1 0.0 copy-start.6
  383.2 0.4 collective-permute-done.7
  383.5 6.9 %fusion.4 = f32[64,1024]{1,0:T(8,128)S(1)} fusion(f32[8,64,1024]{2,1,0:T(8,128)S(1)} %copy-done.2, f32[9,66,1]{2,1,0:T(8,128)S(1)} %collective-permute-done.2, f32[9,1,1024]{2,1,0:T(1,128)S(1)} %copy-done.13, f32[9,1,1024]{2,1,0:T(1,128)S(1)} %copy-done.11, f32[1,64,1024]{2,1,0:T(8,128)S(1)} %bitcast.33, f32[9,66,1]{2,1,0:T(8,128)S(1)} %collective-permute-done.3, ...), kind=kLoop, calls=%fused_computation.6 | loop fusion | flops 20905984 | bytes 4866832 | tf_op jit(solution)/shard_map/reduce_sum | solution.py:51
  390.5 0.7 multiply_add_fusion
  391.2 4.4 %fusion.22 = f32[8,64,1024]{2,1,0:T(8,128)} fusion(f32[8,64,1024]{2,1,0:T(8,128)S(1)} %add_dynamic-update-slice_fusion, f32[8,1,1024]{2,1,0:T(1,128)S(1)} %collective-permute-done.4, f32[8,1,1024]{2,1,0:T(1,128)S(1)} %collective-permute-done.5, f32[8,66,1]{2,1,0:T(8,128)S(1)} %collective-permute-done.7, f32[8,66,1]{2,1,0:T(8,128)S(1)} %collective-permute-done.6, ...), kind=kLoop, calls=%fused_computation.38 | loop fusion | flops 12582912 | bytes 8982656 | tf_op jit(solution)/shard_map/add | solution.py:111
  (29 shorter events, 0.1 us)
Async XLA Ops:
  7.2 1.6 copy-start.1
  7.2 1.6 copy-start.4
  7.2 143.8 %all-gather.2.cloned.1.call-start = ((), (), s32[]{:S(2)}) async-start(), calls=%async_computation.1 | async-start | bytes 8650752 | tf_op jit(solution)/shard_map/all_gather | solution.py:93
  8.8 5.2 %collective-permute-start = (f32[9,1,1024]{2,1,0:T(1,128)S(1)}, f32[9,1,1024]{2,1,0:T(1,128)S(1)}, u32[]{:S(2)}, u32[]{:S(2)}) collective-permute-start(f32[9,1,1024]{2,1,0:T(1,128)S(1)} %get-tuple-element.24), channel_id=1, source_target_pairs={{0,4},{4,8},{8,12},{12,16},{16,20},{20,24},{24,28},{28,32},{32,36}... | collective-permute-start | bytes 110600 | tf_op jit(solution)/shard_map/ppermute | solution.py:19
  12.4 5.9 %collective-permute-start.1 = (f32[9,1,1024]{2,1,0:T(1,128)S(1)}, f32[9,1,1024]{2,1,0:T(1,128)S(1)}, u32[]{:S(2)}, u32[]{:S(2)}) collective-permute-start(f32[9,1,1024]{2,1,0:T(1,128)S(1)} %get-tuple-element.25), channel_id=1, source_target_pairs={{4,0},{8,4},{12,8},{16,12},{20,16},{24,20},{28,24},{32,28},{36,32}... | collective-permute-start | bytes 110600 | tf_op jit(solution)/shard_map/ppermute | solution.py:22
  14.0 4.6 %copy-start.10 = (f32[9,1,1024]{2,1,0:T(1,128)}, f32[9,1,1024]{2,1,0:T(1,128)S(1)}, u32[]{:S(2)}) copy-start(f32[9,1,1024]{2,1,0:T(1,128)S(1)} %collective-permute-done) | copy-start | bytes 110596
  18.2 0.6 copy-start.12
  18.9 1.5 copy-start.3
  20.6 2.6 collective-permute-start.2
  21.9 5.2 %collective-permute-start.3 = (f32[9,66,1]{2,1,0:T(8,128)S(1)}, f32[9,66,1]{2,1,0:T(8,128)S(1)}, u32[]{:S(2)}, u32[]{:S(2)}) collective-permute-start(f32[9,66,1]{2,1,0:T(8,128)S(1)} %get-tuple-element.22), channel_id=1, source_target_pairs={{1,0},{2,1},{3,2},{5,4},{6,5},{7,6},{9,8},{10,9},{11,10},{13,12},{... | collective-permute-start | bytes 7136 | tf_op jit(solution)/shard_map/ppermute | solution.py:22
  32.8 2.3 copy-start.16
  34.3 2.3 copy-start.15
  34.3 2.3 copy-start.14
  35.1 334.0 %reduce-scatter.2.cloned.1.call-start = ((), (), s32[]{:S(2)}) async-start(), calls=%async_computation.2 | async-start | bytes 8650752 | tf_op jit(solution)/shard_map/reduce_scatter | solution.py:100
  158.5 9.0 %copy-start.5 = (f32[64,1024]{1,0:T(8,128)}, f32[64,1024]{1,0:T(8,128)S(1)}, u32[]{:S(2)}) copy-start(f32[64,1024]{1,0:T(8,128)S(1)} %convolution_subtract_fusion) | copy-start | bytes 786436
  167.5 202.6 %copy-start = (f32[8,64,1024]{2,1,0:T(8,128)S(1)}, f32[8,64,1024]{2,1,0:T(8,128)}, u32[]{:S(2)}) copy-start(f32[8,64,1024]{2,1,0:T(8,128)} %param.12) | copy-start | bytes 6291460
  370.2 5.9 %collective-permute-start.4 = (f32[8,1,1024]{2,1,0:T(1,128)S(1)}, f32[8,1,1024]{2,1,0:T(1,128)S(1)}, u32[]{:S(2)}, u32[]{:S(2)}) collective-permute-start(f32[8,1,1024]{2,1,0:T(1,128)S(1)} %get-tuple-element.31), channel_id=1, source_target_pairs={{4,0},{8,4},{12,8},{16,12},{20,16},{24,20},{28,24},{32,28},{36,32}... | collective-permute-start | bytes 98312 | tf_op jit(solution)/shard_map/ppermute | solution.py:22
  371.5 6.1 %collective-permute-start.5 = (f32[8,1,1024]{2,1,0:T(1,128)S(1)}, f32[8,1,1024]{2,1,0:T(1,128)S(1)}, u32[]{:S(2)}, u32[]{:S(2)}) collective-permute-start(f32[8,1,1024]{2,1,0:T(1,128)S(1)} %get-tuple-element.30), channel_id=1, source_target_pairs={{0,4},{4,8},{8,12},{12,16},{16,20},{20,24},{24,28},{28,32},{32,36}... | collective-permute-start | bytes 98312 | tf_op jit(solution)/shard_map/ppermute | solution.py:19
  377.8 5.3 %collective-permute-start.6 = (f32[8,66,1]{2,1,0:T(8,128)S(1)}, f32[8,66,1]{2,1,0:T(8,128)S(1)}, u32[]{:S(2)}, u32[]{:S(2)}) collective-permute-start(f32[8,66,1]{2,1,0:T(8,128)S(1)} %get-tuple-element.26), channel_id=1, source_target_pairs={{1,0},{2,1},{3,2},{5,4},{6,5},{7,6},{9,8},{10,9},{11,10},{13,12},{... | collective-permute-start | bytes 6344 | tf_op jit(solution)/shard_map/ppermute | solution.py:22
  379.1 4.4 %copy-start.2 = (f32[8,64,1024]{2,1,0:T(8,128)S(1)}, f32[8,64,1024]{2,1,0:T(8,128)}, u32[]{:S(2)}) copy-start(f32[8,64,1024]{2,1,0:T(8,128)} %param.10) | copy-start | bytes 6291460
  379.1 4.4 %copy-start.11 = (f32[9,1,1024]{2,1,0:T(1,128)S(1)}, f32[9,1,1024]{2,1,0:T(1,128)}, u32[]{:S(2)}) copy-start(f32[9,1,1024]{2,1,0:T(1,128)} %copy-done.10) | copy-start | bytes 110596
  379.2 4.4 %copy-start.13 = (f32[9,1,1024]{2,1,0:T(1,128)S(1)}, f32[9,1,1024]{2,1,0:T(1,128)}, u32[]{:S(2)}) copy-start(f32[9,1,1024]{2,1,0:T(1,128)} %copy-done.12) | copy-start | bytes 110596
  379.2 4.4 %collective-permute-start.7 = (f32[8,66,1]{2,1,0:T(8,128)S(1)}, f32[8,66,1]{2,1,0:T(8,128)S(1)}, u32[]{:S(2)}, u32[]{:S(2)}) collective-permute-start(f32[8,66,1]{2,1,0:T(8,128)S(1)} %get-tuple-element.27), channel_id=1, source_target_pairs={{0,1},{1,2},{2,3},{4,5},{5,6},{6,7},{8,9},{9,10},{10,11},{12,13},{... | collective-permute-start | bytes 6344 | tf_op jit(solution)/shard_map/ppermute | solution.py:19
  383.1 7.3 %copy-start.9 = (f32[64,1024]{1,0:T(8,128)S(1)}, f32[64,1024]{1,0:T(8,128)}, u32[]{:S(2)}) copy-start(f32[64,1024]{1,0:T(8,128)} %param.13) | copy-start | bytes 786436
  383.1 8.1 %copy-start.6 = (f32[64,1024]{1,0:T(8,128)S(1)}, f32[64,1024]{1,0:T(8,128)}, u32[]{:S(2)}) copy-start(f32[64,1024]{1,0:T(8,128)} %get-tuple-element.17) | copy-start | bytes 786436
  383.1 8.1 %copy-start.7 = (f32[64,1024]{1,0:T(8,128)S(1)}, f32[64,1024]{1,0:T(8,128)}, u32[]{:S(2)}) copy-start(f32[64,1024]{1,0:T(8,128)} %get-tuple-element.18) | copy-start | bytes 786436
  383.1 8.1 %copy-start.8 = (f32[64,1024]{1,0:T(8,128)S(1)}, f32[64,1024]{1,0:T(8,128)}, u32[]{:S(2)}) copy-start(f32[64,1024]{1,0:T(8,128)} %get-tuple-element.19) | copy-start | bytes 786436
Sparse Core Ops, SparseCore 0:
  35.2 115.6 all-gather.1
  167.7 201.3 reduce-scatter.1
where the time goes:
time: 407 us; the launch traced here: 402 us
  waiting for transfers between devices  326 us (80%)
  starting transfers between devices  18 us (4%)
  other arithmetic  16.5 us (4%)
  matrix products  16.5 us (4%)
  between operations  14.4 us (4%)
  local copies, waits for them, and re-layouts  11 us (3%)
    reduce_scatter x1, waiting for transfers between devices, local(): lax.psum_scatter(jnp.dot(select.T, misfit, precision=lax.Precision.HIGHES...  202 us
    all_gather x1, waiting for transfers between devices, local(): piece = lax.all_gather(top_tiles, 'gx', axis=0, tiled=True)  114 us
    ppermute x4, starting transfers between devices, extended(): lax.ppermute(lax.slice_in_dim(block, block.shape[dim] - width, None, axis...  12.8 us
    dot_general x1, matrix products, local(): jnp.dot(select.T, misfit, precision=lax.Precision.HIGHEST, preferred_elem...  8.99 us
    ppermute x4, waiting for transfers between devices, extended(): lax.ppermute(lax.slice_in_dim(block, 0, width, axis=dim), axis, backward)  8.16 us
  transfers between devices with their start and end apart: 10, of which 7 were waited for; matrix products, arithmetic and copies ran while one was open for 1% of the time, Pallas kernels for 0%

commit v1 on v0

v1 whole, which is shorter than its diff:
```python
import jax
import jax.numpy as jnp
from jax import lax
from jax.experimental import pallas as pl
from jax.experimental.pallas import tpu as pltpu
from jax.sharding import PartitionSpec as P

TR = 8
TC = 128
CAP = 16
LANES = 128
RATE_PLANE = 0.2
RATE_VERTICAL = 0.08
MESH = pl.DeviceIdType.MESH
F32 = jnp.float32
BF16 = jnp.bfloat16


def iota(shape, dim):
    return lax.broadcasted_iota(jnp.int32, shape, dim)


def two_parts(x):
    hi = x.astype(BF16)
    lo = (x - hi.astype(F32)).astype(BF16)
    return hi, lo


def three_parts(x):
    hi = x.astype(BF16)
    rest = x - hi.astype(F32)
    mid = rest.astype(BF16)
    lo = (rest - mid.astype(F32)).astype(BF16)
    return hi, mid, lo


RING = 4
PLANE = RING * RING
ORDER = (
    ((2, 2), (2, 2)), ((2, 0), (0, 2)), ((0, 2), (2, 0)),
    ((2, 1), (2, 3)), ((1, 2), (3, 2)), ((2, 3), (2, 1)), ((3, 2), (1, 2)),
    ((1, 1), (3, 3)), ((1, 3), (3, 1)), ((3, 3), (1, 1)), ((3, 1), (1, 3)),
    ((0, 1), (0, 3)), ((1, 0), (3, 0)), ((0, 3), (0, 1)), ((3, 0), (1, 0)),
)


def make_kernel(n_gx, n_gy, layers, rows, cols, frames, k_blocks):
    tiles = (rows // TR) * (cols // TC)
    half = PLANE * CAP
    n_slots = 2 * half
    row0, col0 = TR, LANES
    row1, col1 = row0 + rows, col0 + cols
    strips = rows // TR
    tile_cols = cols // TC
    top = layers - 1
    per_group = LANES // CAP
    groups = PLANE // per_group
    order = [tuple(dz * RING + dy for dz, dy in pair) for pair in ORDER]
    others = range(1, PLANE)

    def kernel(
        temp, cond, adj, grad, obs, frame_ref, map_ref, weight_ref,
        misfit_out, adj_out, grad_out,
        tpad, apad, kpad, gin, obs_v, coef, gacc, outv, misv, gradv,
        ns0_send, ns0_recv, ew0_send, ew0_recv,
        ns_send, ns_recv, ew_send, ew_recv,
        ns2_send, ns2_recv, ew2_send, ew2_recv,
        req_send, req_recv, tiles3, wsel, onehot, lhs1, lhs2, rhs,
        x_send, x_recv, xa_send, xa_recv,
        send1, recv1, send2, recv2,
        in_sem, out_sem,
        rim0_ss, rim0_rs, rim_ss, rim_rs, rim2_ss, rim2_rs, x_ss, x_rs,
        req_ss, req_rs, a1_ss, a1_rs, a2_ss, a2_rs,
    ):
        gx = lax.axis_index("gx")
        gy = lax.axis_index("gy")
        gx_y = lax.rem(gx, RING)
        gx_x = lax.rem(gx // RING, 2)
        gx_z = gx // (2 * RING)
        north, south = lax.rem(gx + n_gx - 1, n_gx), lax.rem(gx + 1, n_gx)
        west, east = lax.rem(gy + n_gy - 1, n_gy), lax.rem(gy + 1, n_gy)
        sides = ({"gx": north}, {"gx": south}, {"gy": west}, {"gy": east})
        partner = {"gx": gx + RING - 2 * RING * gx_x}

        core = lax.rem(gy, 2)

        def peer(q, sign):
            dz, dy = q // RING, lax.rem(q, RING)
            if sign < 0:
                dz, dy = RING - dz, RING - dy
            z = lax.rem(gx_z + dz, RING)
            y = lax.rem(gx_y + dy, RING)
            return {"gx": z * (2 * RING) + gx_x * RING + y}

        barrier = pltpu.get_barrier_semaphore()
        greeted = [peer(q, 1) for q in others] + [partner] + list(sides)
        for device in greeted:
            pl.semaphore_signal(barrier, inc=1, device_id=device, device_id_type=MESH)

        body_at = (slice(row0, row1), slice(col0, col1))
        loads = [
            pltpu.make_async_copy(
                temp.at[top - 1 : layers],
                tpad.at[(slice(top - 1, layers), *body_at)],
                in_sem.at[0],
            ),
            pltpu.make_async_copy(cond, kpad.at[body_at], in_sem.at[1]),
            pltpu.make_async_copy(
                temp.at[0 : top - 1], tpad.at[(slice(0, top - 1), *body_at)], in_sem.at[2]
            ),
            pltpu.make_async_copy(adj, apad.at[(slice(None), *body_at)], in_sem.at[3]),
            pltpu.make_async_copy(grad, gin, in_sem.at[4]),
            pltpu.make_async_copy(obs, obs_v, in_sem.at[5]),
        ]
        for load in loads:
            load.start()

        eye = iota((tiles, tiles), 0) == iota((tiles, tiles), 1)

        def as_column(line):
            spread = jnp.where(eye, jnp.broadcast_to(line, (tiles, tiles)), 0)
            return jnp.sum(spread, axis=1, keepdims=True)

        lane = iota((tiles, LANES), 1)
        lane_slot = iota((tiles, n_slots), 1)
        below = jnp.where(iota((tiles, tiles), 0) > iota((tiles, tiles), 1), 1.0, 0.0)
        base = jnp.zeros((1, LANES), F32)
        weights = jnp.zeros((tiles, n_slots), F32)
        wanted = jnp.zeros((tiles, n_slots), F32)
        for k in range(k_blocks):
            code = as_column(map_ref[k : k + 1, :].astype(F32)).astype(jnp.int32)
            weight = as_column(weight_ref[k : k + 1, :])
            plate = code >> ((tiles * n_gy).bit_length() - 1)
            far = ((plate ^ gx) >> 2) & 1
            dz = ((plate >> 3) - gx_z) & 3
            dy = (plate - gx) & 3
            block = far * PLANE + dz * RING + dy
            local = code & (tiles - 1)
            hit = jnp.where(block == lane, 1.0, 0.0)
            before = jnp.dot(below, hit, preferred_element_type=F32) + base
            base = base + jnp.sum(hit, axis=0, keepdims=True)
            rank = jnp.sum(hit * before, axis=1, keepdims=True)
            here = block * CAP + rank.astype(jnp.int32) == lane_slot
            weights = weights + jnp.where(here, weight, 0.0)
            wanted = wanted + jnp.where(here, (local + 1).astype(F32), 0.0)
        wsel[...] = weights
        asked = jnp.sum(wanted, axis=0, keepdims=True)
        for g in range(groups):
            for f in range(2):
                at = f * half + g * LANES
                req_send[g, f : f + 1] = asked[:, at : at + LANES]

        for load in loads[:2]:
            load.wait()
        first, last = row0, row1 - 1
        rim_lane = iota((rows, LANES), 1)
        for side, row in ((0, first), (1, last)):
            ns0_send[side, 0:1] = tpad[top, row : row + 1, col0:col1]
            ns0_send[side, 1:2] = kpad[row : row + 1, col0:col1]
        for side, col in ((0, col0), (1, col1 - 1)):
            ew0_send[side] = jnp.where(
                rim_lane == 0,
                tpad[top, row0:row1, col : col + 1],
                kpad[row0:row1, col : col + 1],
            )

        pl.semaphore_wait(barrier, len(greeted))

        def rim_copies(ns_s, ns_r, ew_s, ew_r, ss, rs):
            copies = []
            for i in range(4):
                src, dst = (ns_s, ns_r) if i < 2 else (ew_s, ew_r)
                copies.append(
                    pltpu.make_async_remote_copy(
                        src_ref=src.at[i % 2],
                        dst_ref=dst.at[1 - i % 2],
                        send_sem=ss.at[i],
                        recv_sem=rs.at[i],
                        device_id=sides[i],
                        device_id_type=MESH,
                    )
                )
            return copies

        rims0 = rim_copies(ns0_send, ns0_recv, ew0_send, ew0_recv, rim0_ss, rim0_rs)
        for copy in rims0:
            copy.start()

        req_copies = []
        for q in others:
            copy = pltpu.make_async_remote_copy(
                src_ref=req_send.at[q // per_group],
                dst_ref=req_recv.at[q],
                send_sem=req_ss.at[q],
                recv_sem=req_rs.at[q],
                device_id=peer(q, 1),
                device_id_type=MESH,
            )
            copy.start()
            req_copies.append(copy)
        req_recv[0] = req_send[0]

        has_north = jnp.where(gx > 0, 1.0, 0.0)
        has_south = jnp.where(gx < n_gx - 1, 1.0, 0.0)
        has_west = jnp.where(gy > 0, 1.0, 0.0)
        has_east = jnp.where(gy < n_gy - 1, 1.0, 0.0)

        def column_rims(pad, index, source, lane_at):
            for side, has, at in ((0, has_west, 0), (1, has_east, col1)):
                value = source[side, :, lane_at : lane_at + 1] * has
                pad[(*index, slice(row0, row1), slice(at, at + LANES))] = jnp.broadcast_to(
                    value, (rows, LANES)
                )

        for copy in rims0:
            copy.wait_recv()
        kpad[first - 1 : first, col0:col1] = ns0_recv[0, 1:2] * has_north
        kpad[last + 1 : last + 2, col0:col1] = ns0_recv[1, 1:2] * has_south
        column_rims(kpad, (), ew0_recv, 1)
        tpad[top, first - 1 : first, col0:col1] = ns0_recv[0, 0:1] * has_north
        tpad[top, last + 1 : last + 2, col0:col1] = ns0_recv[1, 0:1] * has_south
        column_rims(tpad, (top,), ew0_recv, 0)

        def around(pad, index, r):
            a, b = row0 + r * TR, row0 + (r + 1) * TR
            return (
                pad[(*index, slice(a, b), slice(col0, col1))],
                pad[(*index, slice(a, b), slice(col0 + 1, col1 + 1))],
                pad[(*index, slice(a, b), slice(col0 - 1, col1 - 1))],
                pad[(*index, slice(a - 1, b - 1), slice(col0, col1))],
                pad[(*index, slice(a + 1, b + 1), slice(col0, col1))],
            )

        for r in range(strips):
            kc, ke, kw, kn, ks = around(kpad, (), r)
            strip = slice(r * TR, (r + 1) * TR)
            faces = [0.5 * RATE_PLANE * (kc + other) for other in (ke, kw, kn, ks)]
            for i in range(4):
                coef[i, strip] = faces[i]
            tc, te, tw, tn, ts = around(tpad, (top,), r)
            under = tpad[top - 1, row0 + r * TR : row0 + (r + 1) * TR, col0:col1]
            value = tc + RATE_VERTICAL * (under - tc)
            for face, other in zip(faces, (te, tw, tn, ts)):
                value = value + face * (other - tc)
            for u in range(tile_cols):
                tiles3[r * tile_cols + u] = value[:, u * TC : (u + 1) * TC]

        def partner_copy(src, dst, i):
            return pltpu.make_async_remote_copy(
                src_ref=src,
                dst_ref=dst,
                send_sem=x_ss.at[i],
                recv_sem=x_rs.at[i],
                device_id=partner,
                device_id_type=MESH,
            )

        for rr in range(TR):
            x_send[:, rr * TC : (rr + 1) * TC] = tiles3[:, rr, :]
        x_copy = partner_copy(x_send, x_recv, 0)
        x_copy.start()

        for copy in req_copies:
            copy.wait_recv()
        group_lane = iota((per_group, LANES), 1) // CAP
        group_row = iota((per_group, LANES), 0)
        tile_row = iota((tiles, LANES), 0).astype(F32)
        for f in range(2):
            picks = []
            for g in range(groups):
                block = req_recv[g * per_group : (g + 1) * per_group, f, :]
                line = jnp.sum(
                    jnp.where(group_lane == group_row, block, 0.0), axis=0, keepdims=True
                )
                picks.append(jnp.where(line - 1.0 == tile_row, 1.0, 0.0))
            pick = jnp.concatenate(picks, axis=1)
            onehot[:, f * half : (f + 1) * half] = pick
            turned = jnp.transpose(jnp.concatenate([pick, pick], axis=0)).astype(BF16)
            lhs1[f * half : (f + 1) * half, 0 : 2 * tiles] = turned
            lhs1[f * half : (f + 1) * half, 2 * tiles : 4 * tiles] = turned

        def block_copy(src, dst, ss, rs, sign, f, q):
            b = f * PLANE + q
            at = pl.ds(pl.multiple_of(b * CAP, CAP), CAP)
            return pltpu.make_async_remote_copy(
                src_ref=src.at[at],
                dst_ref=dst.at[at],
                send_sem=ss.at[b],
                recv_sem=rs.at[b],
                device_id=peer(q, sign),
                device_id_type=MESH,
            )

        def exchange(*args):
            starts, waits = [[], []], [[], []]
            for f in range(2):
                for one, two in order:
                    starts[f].append(block_copy(*args, f, one + core * (two - one)))
                for q in others:
                    waits[f].append(block_copy(*args, f, q))
            return starts, waits

        def pack_and_send(lhs, src, dst, copies, f):
            at = slice(f * half, (f + 1) * half)
            src[at] = jnp.dot(lhs[at], rhs[...], preferred_element_type=F32)
            for copy in copies[f]:
                copy.start()
            dst[f * half : f * half + CAP] = src[f * half : f * half + CAP]

        def fill_tiles(source):
            for i, part in enumerate(three_parts(source)):
                rhs[i * tiles : (i + 1) * tiles] = part
            rhs[3 * tiles : 4 * tiles] = jnp.zeros((tiles, cols), BF16)

        starts1, copies1 = exchange(send1, recv1, a1_ss, a1_rs, -1)
        fill_tiles(x_send[...])
        pack_and_send(lhs1, send1, recv1, starts1, 0)

        for load in loads[2:4]:
            load.wait()
        for side, row in ((0, first), (1, last)):
            ns_send[side, 0:top] = tpad[0:top, row, col0:col1]
            ns_send[side, layers : layers + top] = apad[0:top, row, col0:col1]
        for side, col in ((0, col0), (1, col1 - 1)):
            packed = jnp.zeros((rows, LANES), F32)
            for l in range(top):
                packed = jnp.where(rim_lane == l, tpad[l, row0:row1, col : col + 1], packed)
                packed = jnp.where(
                    rim_lane == layers + l, apad[l, row0:row1, col : col + 1], packed
                )
            ew_send[side] = packed
        rims = rim_copies(ns_send, ns_recv, ew_send, ew_recv, rim_ss, rim_rs)
        for copy in rims:
            copy.start()

        halves = jnp.concatenate(two_parts(wsel[...]), axis=0).astype(F32)
        turned = jnp.transpose(halves).astype(BF16)
        lhs2[:, 0 : 2 * tiles] = turned
        lhs2[:, 2 * tiles : 4 * tiles] = turned

        for copy in rims:
            copy.wait_recv()
        for l in range(top):
            column_rims(tpad, (l,), ew_recv, l)
            column_rims(apad, (l,), ew_recv, layers + l)
        tpad[0:top, first - 1, col0:col1] = ns_recv[0, 0:top] * has_north
        tpad[0:top, last + 1, col0:col1] = ns_recv[1, 0:top] * has_south
        apad[0:top, first - 1, col0:col1] = ns_recv[0, layers : layers + top] * has_north
        apad[0:top, last + 1, col0:col1] = ns_recv[1, layers : layers + top] * has_south

        def layer_step(l, r, total):
            strip = slice(r * TR, (r + 1) * TR)
            tc, *t_near = around(tpad, (l,), r)
            ac, *a_near = around(apad, (l,), r)
            flow = jnp.zeros_like(ac)
            for i in range(4):
                step = a_near[i] - ac
                flow = flow + coef[i, strip] * step
                total = total + (t_near[i] - tc) * step
            return ac + flow, ac, total

        def inner_layers(r):
            strip = slice(r * TR, (r + 1) * TR)
            inner = slice(row0 + r * TR, row0 + (r + 1) * TR)

            def body(l, total):
                value, ac, total = layer_step(l, r, total)
                above = apad[l + 1, inner, col0:col1]
                under = apad[jnp.maximum(l - 1, 0), inner, col0:col1]
                outv[l, strip] = value + RATE_VERTICAL * ((above - ac) + (under - ac))
                return total

            gacc[strip] = lax.fori_loop(0, top, body, jnp.zeros((TR, cols), F32))

        for r in range(strips // 2):
            inner_layers(r)

        x_copy.wait_recv()
        fill_tiles(x_recv[...])
        pack_and_send(lhs1, send1, recv1, starts1, 1)

        for r in range(strips // 2, strips):
            inner_layers(r)
        early = pltpu.make_async_copy(
            outv.at[0 : top - 1], adj_out.at[0 : top - 1], out_sem.at[0]
        )
        early.start()

        loads[4].wait()
        loads[5].wait()
        frame = as_column(frame_ref[...].astype(F32)).astype(jnp.int32)
        seen = jnp.zeros((tiles, cols), F32)
        for f in range(frames):
            seen = jnp.where(frame == f, obs_v[f], seen)
        misv[...] = -seen

        for f in range(2):
            for copy in copies1[f]:
                copy.wait_recv()
            at = slice(f * half, (f + 1) * half)
            wh, wl = two_parts(wsel[:, at])
            rh, rl = two_parts(recv1[at])
            misv[...] += jnp.dot(
                jnp.concatenate([wh, wl, wh], axis=1),
                jnp.concatenate([rh, rh, rl], axis=0),
                preferred_element_type=F32,
            )
        mis_copy = pltpu.make_async_copy(misv, misfit_out, out_sem.at[1])
        mis_copy.start()

        mh, ml = two_parts(misv[...])
        rhs[0:tiles] = mh
        rhs[tiles : 2 * tiles] = mh
        rhs[2 * tiles : 3 * tiles] = ml
        rhs[3 * tiles : 4 * tiles] = ml
        starts2, copies2 = exchange(send2, recv2, a2_ss, a2_rs, 1)
        for f in (1, 0):
            pack_and_send(lhs2, send2, recv2, starts2, f)

        def gathered(f):
            for copy in copies2[f]:
                copy.wait_recv()
            at = slice(f * half, (f + 1) * half)
            pick = onehot[:, at].astype(BF16)
            return jnp.dot(
                jnp.concatenate([pick, pick, pick], axis=1),
                jnp.concatenate(three_parts(recv2[at]), axis=0),
                preferred_element_type=F32,
            )

        xa_send[...] = gathered(1)
        xa_copy = partner_copy(xa_send, xa_recv, 1)
        xa_copy.start()
        added = gathered(0)
        xa_copy.wait_recv()
        added = added + xa_recv[...]
        for rr in range(TR):
            tiles3[:, rr, :] = added[:, rr * TC : (rr + 1) * TC]
        for r in range(strips):
            strip = slice(r * TR, (r + 1) * TR)
            inner = slice(row0 + r * TR, row0 + (r + 1) * TR)
            extra = jnp.concatenate(
                [tiles3[r * tile_cols + u] for u in range(tile_cols)], axis=1
            )
            apad[top, inner, col0:col1] += extra
            outv[top - 1, strip] += RATE_VERTICAL * extra

        for side, row in ((0, first), (1, last)):
            ns2_send[side] = apad[top, row : row + 1, col0:col1]
        for side, col in ((0, col0), (1, col1 - 1)):
            ew2_send[side] = jnp.broadcast_to(
                apad[top, row0:row1, col : col + 1], (rows, LANES)
            )
        rims2 = rim_copies(ns2_send, ns2_recv, ew2_send, ew2_recv, rim2_ss, rim2_rs)
        for copy in rims2:
            copy.start()
        late = pltpu.make_async_copy(
            outv.at[top - 1], adj_out.at[top - 1], out_sem.at[2]
        )
        late.start()
        for copy in rims2:
            copy.wait_recv()
        apad[top, first - 1 : first, col0:col1] = ns2_recv[0] * has_north
        apad[top, last + 1 : last + 2, col0:col1] = ns2_recv[1] * has_south
        apad[top, row0:row1, 0:col0] = ew2_recv[0] * has_west
        apad[top, row0:row1, col1 : col1 + LANES] = ew2_recv[1] * has_east

        for r in range(strips):
            strip = slice(r * TR, (r + 1) * TR)
            inner = slice(row0 + r * TR, row0 + (r + 1) * TR)
            value, ac, total = layer_step(top, r, gacc[strip])
            under = apad[top - 1, inner, col0:col1]
            outv[top, strip] = value + RATE_VERTICAL * (under - ac)
            gradv[strip] = gin[strip] - (0.5 * RATE_PLANE) * total

        last_copies = [
            pltpu.make_async_copy(outv.at[top], adj_out.at[top], out_sem.at[3]),
            pltpu.make_async_copy(gradv, grad_out, out_sem.at[4]),
        ]
        for copy in last_copies:
            copy.start()
        sent = rims0 + rims + rims2 + req_copies + [x_copy, xa_copy]
        for copy in sent + copies1[0] + copies1[1] + copies2[0] + copies2[1]:
            copy.wait_send()
        for copy in [early, mis_copy, late] + last_copies:
            copy.wait()

    dma = pltpu.SemaphoreType.DMA

    def vmem(*shape, dtype=F32):
        return pltpu.VMEM(shape, dtype)

    def pair(*shape):
        return [vmem(*shape), vmem(*shape)]

    tile = TR * TC
    scratch = [
        vmem(layers, rows + 2 * TR, cols + 2 * LANES),
        vmem(layers, rows + 2 * TR, cols + 2 * LANES),
        vmem(rows + 2 * TR, cols + 2 * LANES),
        vmem(rows, cols),
        vmem(frames, tiles, tile),
        vmem(4, rows, cols),
        vmem(rows, cols),
        vmem(layers, rows, cols),
        vmem(tiles, tile),
        vmem(rows, cols),
        *pair(2, 2, cols),
        *pair(2, rows, LANES),
        *pair(2, 2 * layers, cols),
        *pair(2, rows, LANES),
        *pair(2, 1, cols),
        *pair(2, rows, LANES),
        vmem(groups, 8, LANES),
        vmem(PLANE, 8, LANES),
        vmem(tiles, TR, TC),
        *pair(tiles, n_slots),
        vmem(n_slots, 4 * tiles, dtype=BF16),
        vmem(n_slots, 4 * tiles, dtype=BF16),
        vmem(4 * tiles, tile, dtype=BF16),
        *pair(tiles, tile),
        *pair(tiles, tile),
        *pair(n_slots, tile),
        *pair(n_slots, tile),
        dma((6,)),
        dma((5,)),
        *[dma((4,)) for _ in range(6)],
        dma((2,)), dma((2,)),
        dma((PLANE,)), dma((PLANE,)),
        *[dma((2 * PLANE,)) for _ in range(4)],
    ]
    in_hbm = pl.BlockSpec(memory_space=pltpu.HBM)
    anywhere = pl.BlockSpec(memory_space=pl.ANY)
    in_vmem = pl.BlockSpec(memory_space=pltpu.VMEM)
    return pl.pallas_call(
        kernel,
        out_shape=(
            jax.ShapeDtypeStruct((tiles, tile), F32),
            jax.ShapeDtypeStruct((layers, rows, cols), F32),
            jax.ShapeDtypeStruct((rows, cols), F32),
        ),
        in_specs=[in_hbm] * 5 + [in_vmem] * 3,
        out_specs=[anywhere] * 3,
        scratch_shapes=scratch,
        compiler_params=pltpu.CompilerParams(
            collective_id=0, has_side_effects=True, vmem_limit_bytes=48 * 1024 * 1024
        ),
    )


def solution(mesh):
    n_gx, n_gy = mesh.shape["gx"], mesh.shape["gy"]

    def local(temp, cond, adj, grad, obs, frame_index, source_map, source_weight):
        layers, rows, cols = temp.shape
        call = make_kernel(n_gx, n_gy, layers, rows, cols, obs.shape[0], source_map.shape[1])
        operands = (
            temp, cond, adj, grad, obs, frame_index[None, :], source_map.T, source_weight.T
        )
        return call(*(pltpu.with_memory_space_constraint(x, pltpu.HBM) for x in operands))

    placed = (
        P(None, "gx", "gy"),
        P("gx", "gy"),
        P(None, "gx", "gy"),
        P("gx", "gy"),
        P(None, ("gx", "gy"), None),
        P(("gx", "gy")),
        P(("gx", "gy"), None),
        P(("gx", "gy"), None),
    )
    return jax.shard_map(
        local,
        mesh=mesh,
        in_specs=placed,
        out_specs=(P(("gx", "gy"), None), P(None, "gx", "gy"), P("gx", "gy")),
        check_vma=False,
    )
```

time: 407 us -> 87.3 us (0.21); the launches traced: 402 us -> 87.2 us
  waiting for transfers between devices: 326 us -> 0 us
  Pallas kernels: 0 us -> 83.8 us
  starting transfers between devices: 18 us -> 0 us
  matrix products: 16.5 us -> 0 us
  other arithmetic: 16.5 us -> 0 us
  between operations: 14.4 us -> 0.64 us
  local copies, waits for them, and re-layouts: 11 us -> 2.73 us
    reduce_scatter x1 -> x0, waiting for transfers between devices: 202 us -> none  [local(): lax.psum_scatter(jnp.dot(select.T, misfit, precision=lax.Precision.HIGHES...]
    all_gather x1 -> x0, waiting for transfers between devices: 114 us -> none  [local(): piece = lax.all_gather(top_tiles, 'gx', axis=0, tiled=True)]
    pallas_call x0 -> x1, Pallas kernels: none -> 83.8 us  [local(): call(*(pltpu.with_memory_space_constraint(x, pltpu.HBM) for x in operands))]
    ppermute x8 -> x0, starting transfers between devices: 18 us -> none  [the longest x4 12.8 us: extended(): lax.ppermute(lax.slice_in_dim(block, block.shape[dim] - width, None, axis...]
    dot_general x2 -> x0, matrix products: 16.5 us -> none  [the longest x1 8.99 us: local(): jnp.dot(select.T, misfit, precision=lax.Precision.HIGHEST, preferred_elem...]
    ppermute x8 -> x0, waiting for transfers between devices: 10.4 us -> none  [the longest x4 8.16 us: extended(): lax.ppermute(lax.slice_in_dim(block, 0, width, axis=dim), axis, backward)]
    reduce_sum x3 -> x0, other arithmetic: 8.65 us -> none  [the longest x1 6.91 us: face_grad(): return jnp.sum(total, axis=0)]
    add x3 -> x0, other arithmetic: 5.16 us -> none  [the longest x1 4.41 us: local(): adjoint_next + RATE_PLANE * plane_term(adj_pad, kpad)]
  transfers between devices with their start and end apart: 10 -> 0, of which waited for: 7 -> 0; matrix products, arithmetic and copies ran while one was open for 1% -> 0% of each run, Pallas kernels for 0% -> 0%
where the time goes in v1:
time: 87.3 us; the launch traced here: 87.2 us
  Pallas kernels  83.8 us (96%)
  local copies, waits for them, and re-layouts  2.73 us (3%)
    pallas_call x1, Pallas kernels, local(): call(*(pltpu.with_memory_space_constraint(x, pltpu.HBM) for x in operands))  83.8 us
    unnamed x3, local copies, waits for them, and re-layouts  2.73 us

profile of v1, /device:TPU:0, one launch (start us, length us, event | category | flops | bytes accessed | tf_op | source)
XLA Modules:
  0.0 87.2 jit_solution(2380812136690446889)
XLA Ops:
  0.6 83.8 %shard_map.103 = (f32[64,1024]{1,0:T(8,128)S(1)}, f32[8,64,1024]{2,1,0:T(8,128)S(1)}, f32[64,1024]{1,0:T(8,128)S(1)}) custom-call(f32[8,64,1024]{2,1,0:T(8,128)} %temp.1, f32[64,1024]{1,0:T(8,128)} %cond.1, f32[8,64,1024]{2,1,0:T(8,128)} %adj.1, f32[64,1024]{1,0:T(8,128)} %grad.1, f32[4,64,1024]{2,1,0:T(8,128)} %obs.1, s32[1,64]{1,0:T(1,128)} %bitcast.5, ...), custom_call_target="tpu_custom_call" | custom-call | tf_op jit(solution)/shard_map/pallas_call | solution.py:560
  84.5 0.7 copy.14
  85.2 1.3 %copy.15 = f32[8,64,1024]{2,1,0:T(8,128)} copy(f32[8,64,1024]{2,1,0:T(8,128)S(1)} %get-tuple-element.7) | data formatting | bytes 4194304
  86.5 0.7 copy.16

commit v2 on v1

--- a/solution.py
+++ b/solution.py
@@ -36,12 +36,7 @@
 
 RING = 4
 PLANE = RING * RING
-ORDER = (
-    ((2, 2), (2, 2)), ((2, 0), (0, 2)), ((0, 2), (2, 0)),
-    ((2, 1), (2, 3)), ((1, 2), (3, 2)), ((2, 3), (2, 1)), ((3, 2), (1, 2)),
-    ((1, 1), (3, 3)), ((1, 3), (3, 1)), ((3, 3), (1, 1)), ((3, 1), (1, 3)),
-    ((0, 1), (0, 3)), ((1, 0), (3, 0)), ((0, 3), (0, 1)), ((3, 0), (1, 0)),
-)
+FARTHEST_FIRST = (2, 1, 3)
 
 
 def make_kernel(n_gx, n_gy, layers, rows, cols, frames, k_blocks):
@@ -55,22 +50,23 @@
     top = layers - 1
     per_group = LANES // CAP
     groups = PLANE // per_group
-    order = [tuple(dz * RING + dy for dz, dy in pair) for pair in ORDER]
     others = range(1, PLANE)
+    wide = cols // 2
 
     def kernel(
         temp, cond, adj, grad, obs, frame_ref, map_ref, weight_ref,
         misfit_out, adj_out, grad_out,
-        tpad, apad, kpad, gin, obs_v, coef, gacc, outv, misv, gradv,
+        tpad, apad, kpad, gin, obs_v, coef, gacc, outv, gradv,
         ns0_send, ns0_recv, ew0_send, ew0_recv,
         ns_send, ns_recv, ew_send, ew_recv,
         ns2_send, ns2_recv, ew2_send, ew2_recv,
-        req_send, req_recv, tiles3, wsel, onehot, lhs1, lhs2, rhs,
+        req_send, req_recv, tiles3, onehot, lhs1, rhs, rhs2,
+        wsend, wblk, wcat, lhs2,
         x_send, x_recv, xa_send, xa_recv,
-        send1, recv1, send2, recv2,
+        send1, recv1, part, part_recv, mis, mis_recv, send2, recv2,
         in_sem, out_sem,
         rim0_ss, rim0_rs, rim_ss, rim_rs, rim2_ss, rim2_rs, x_ss, x_rs,
-        req_ss, req_rs, a1_ss, a1_rs, a2_ss, a2_rs,
+        req_ss, req_rs, w_ss, w_rs, s1_ss, s1_rs, p_ss, p_rs, m_ss, m_rs, s2_ss, s2_rs,
     ):
         gx = lax.axis_index("gx")
         gy = lax.axis_index("gy")
@@ -82,18 +78,29 @@
         sides = ({"gx": north}, {"gx": south}, {"gy": west}, {"gy": east})
         partner = {"gx": gx + RING - 2 * RING * gx_x}
 
-        core = lax.rem(gy, 2)
-
-        def peer(q, sign):
-            dz, dy = q // RING, lax.rem(q, RING)
-            if sign < 0:
-                dz, dy = RING - dz, RING - dy
-            z = lax.rem(gx_z + dz, RING)
-            y = lax.rem(gx_y + dy, RING)
+        def along(dz, dy):
+            z = lax.rem(gx_z + dz % RING, RING)
+            y = lax.rem(gx_y + dy % RING, RING)
             return {"gx": z * (2 * RING) + gx_x * RING + y}
 
+        def slot_peer(h, d):
+            return along(0, d) if h == 0 else along(d, 0)
+
+        def dense_peer(h, d):
+            return along(d, 0) if h == 0 else along(0, d)
+
+        def send(src, dst, ss, rs, device):
+            return pltpu.make_async_remote_copy(
+                src_ref=src,
+                dst_ref=dst,
+                send_sem=ss,
+                recv_sem=rs,
+                device_id=device,
+                device_id_type=MESH,
+            )
+
         barrier = pltpu.get_barrier_semaphore()
-        greeted = [peer(q, 1) for q in others] + [partner] + list(sides)
+        greeted = [along(b % RING, b // RING) for b in others] + [partner] + list(sides)
         for device in greeted:
             pl.semaphore_signal(barrier, inc=1, device_id=device, device_id_type=MESH)
 
@@ -125,8 +132,8 @@
         lane_slot = iota((tiles, n_slots), 1)
         below = jnp.where(iota((tiles, tiles), 0) > iota((tiles, tiles), 1), 1.0, 0.0)
         base = jnp.zeros((1, LANES), F32)
-        weights = jnp.zeros((tiles, n_slots), F32)
         wanted = jnp.zeros((tiles, n_slots), F32)
+        weights = [jnp.zeros((tiles, n_slots), F32) for _ in range(2)]
         for k in range(k_blocks):
             code = as_column(map_ref[k : k + 1, :].astype(F32)).astype(jnp.int32)
             weight = as_column(weight_ref[k : k + 1, :])
@@ -134,16 +141,21 @@
             far = ((plate ^ gx) >> 2) & 1
             dz = ((plate >> 3) - gx_z) & 3
             dy = (plate - gx) & 3
-            block = far * PLANE + dz * RING + dy
+            block = far * PLANE + dy * RING + dz
             local = code & (tiles - 1)
             hit = jnp.where(block == lane, 1.0, 0.0)
             before = jnp.dot(below, hit, preferred_element_type=F32) + base
             base = base + jnp.sum(hit, axis=0, keepdims=True)
-            rank = jnp.sum(hit * before, axis=1, keepdims=True)
-            here = block * CAP + rank.astype(jnp.int32) == lane_slot
-            weights = weights + jnp.where(here, weight, 0.0)
+            rank = jnp.sum(hit * before, axis=1, keepdims=True).astype(jnp.int32)
+            here = block * CAP + rank == lane_slot
             wanted = wanted + jnp.where(here, (local + 1).astype(F32), 0.0)
-        wsel[...] = weights
+            for h, (dense, slot) in enumerate(((dz, dy), (dy, dz))):
+                at = dense * LANES + far * (LANES // 2) + slot * CAP + rank
+                weights[h] = weights[h] + jnp.where(at == lane_slot, weight, 0.0)
+        for h in range(2):
+            for d in range(RING):
+                wsend[h, d] = weights[h][:, d * LANES : (d + 1) * LANES]
+            wblk[h, 0] = weights[h][:, 0:LANES]
         asked = jnp.sum(wanted, axis=0, keepdims=True)
         for g in range(groups):
             for f in range(2):
@@ -187,17 +199,25 @@
             copy.start()
 
         req_copies = []
-        for q in others:
-            copy = pltpu.make_async_remote_copy(
-                src_ref=req_send.at[q // per_group],
-                dst_ref=req_recv.at[q],
-                send_sem=req_ss.at[q],
-                recv_sem=req_rs.at[q],
-                device_id=peer(q, 1),
-                device_id_type=MESH,
+        for b in others:
+            copy = send(
+                req_send.at[b // per_group],
+                req_recv.at[b],
+                req_ss.at[b],
+                req_rs.at[b],
+                along(b % RING, b // RING),
             )
             copy.start()
             req_copies.append(copy)
+        w_copies = []
+        for h in range(2):
+            for d in range(1, RING):
+                i = h * RING + d
+                copy = send(
+                    wsend.at[h, d], wblk.at[h, d], w_ss.at[i], w_rs.at[i], dense_peer(h, d)
+                )
+                copy.start()
+                w_copies.append(copy)
         req_recv[0] = req_send[0]
 
         has_north = jnp.where(gx > 0, 1.0, 0.0)
@@ -245,19 +265,9 @@
             for u in range(tile_cols):
                 tiles3[r * tile_cols + u] = value[:, u * TC : (u + 1) * TC]
 
-        def partner_copy(src, dst, i):
-            return pltpu.make_async_remote_copy(
-                src_ref=src,
-                dst_ref=dst,
-                send_sem=x_ss.at[i],
-                recv_sem=x_rs.at[i],
-                device_id=partner,
-                device_id_type=MESH,
-            )
-
         for rr in range(TR):
             x_send[:, rr * TC : (rr + 1) * TC] = tiles3[:, rr, :]
-        x_copy = partner_copy(x_send, x_recv, 0)
+        x_copy = send(x_send, x_recv, x_ss.at[0], x_rs.at[0], partner)
         x_copy.start()
 
         for copy in req_copies:
@@ -279,42 +289,42 @@
             lhs1[f * half : (f + 1) * half, 0 : 2 * tiles] = turned
             lhs1[f * half : (f + 1) * half, 2 * tiles : 4 * tiles] = turned
 
-        def block_copy(src, dst, ss, rs, sign, f, q):
-            b = f * PLANE + q
-            at = pl.ds(pl.multiple_of(b * CAP, CAP), CAP)
-            return pltpu.make_async_remote_copy(
-                src_ref=src.at[at],
-                dst_ref=dst.at[at],
-                send_sem=ss.at[b],
-                recv_sem=rs.at[b],
-                device_id=peer(q, sign),
-                device_id_type=MESH,
-            )
-
-        def exchange(*args):
-            starts, waits = [[], []], [[], []]
+        def plane_rows(ref, h, f, d):
+            return ref.at[0, f, d] if h == 0 else ref.at[1, f, :, d]
+
+        slots1 = {}
+        for h in range(2):
             for f in range(2):
-                for one, two in order:
-                    starts[f].append(block_copy(*args, f, one + core * (two - one)))
-                for q in others:
-                    waits[f].append(block_copy(*args, f, q))
-            return starts, waits
-
-        def pack_and_send(lhs, src, dst, copies, f):
-            at = slice(f * half, (f + 1) * half)
-            src[at] = jnp.dot(lhs[at], rhs[...], preferred_element_type=F32)
-            for copy in copies[f]:
-                copy.start()
-            dst[f * half : f * half + CAP] = src[f * half : f * half + CAP]
+                for d in range(1, RING):
+                    i = (h * 2 + f) * RING + d
+                    slots1[h, f, d] = send(
+                        plane_rows(send1, h, f, d),
+                        recv1.at[h, :, f, d],
+                        s1_ss.at[i],
+                        s1_rs.at[i],
+                        slot_peer(h, -d),
+                    )
 
         def fill_tiles(source):
-            for i, part in enumerate(three_parts(source)):
-                rhs[i * tiles : (i + 1) * tiles] = part
+            for i, three in enumerate(three_parts(source)):
+                rhs[i * tiles : (i + 1) * tiles] = three
             rhs[3 * tiles : 4 * tiles] = jnp.zeros((tiles, cols), BF16)
 
-        starts1, copies1 = exchange(send1, recv1, a1_ss, a1_rs, -1)
+        def pack_tiles(f):
+            for h in range(2):
+                packed = jnp.dot(
+                    lhs1[f * half : (f + 1) * half],
+                    rhs[:, h * wide : (h + 1) * wide],
+                    preferred_element_type=F32,
+                )
+                send1[h, f] = packed.reshape(RING, RING, CAP, wide)
+                for d in FARTHEST_FIRST:
+                    slots1[h, f, d].start()
+            recv1[0, :, f, 0] = send1[0, f, 0]
+            recv1[1, :, f, 0] = send1[1, f, :, 0]
+
         fill_tiles(x_send[...])
-        pack_and_send(lhs1, send1, recv1, starts1, 0)
+        pack_tiles(0)
 
         for load in loads[2:4]:
             load.wait()
@@ -333,10 +343,19 @@
         for copy in rims:
             copy.start()
 
-        halves = jnp.concatenate(two_parts(wsel[...]), axis=0).astype(F32)
-        turned = jnp.transpose(halves).astype(BF16)
-        lhs2[:, 0 : 2 * tiles] = turned
-        lhs2[:, 2 * tiles : 4 * tiles] = turned
+        for copy in w_copies:
+            copy.wait_recv()
+        for h in range(2):
+            for d in range(RING):
+                wh, wl = two_parts(wblk[h, d])
+                for f in range(2):
+                    at = slice(f * (LANES // 2), (f + 1) * (LANES // 2))
+                    wcat[h, d, f] = jnp.concatenate(
+                        [wh[:, at], wl[:, at], wh[:, at], wl[:, at]], axis=1
+                    )
+                turned = jnp.transpose(jnp.concatenate([wh, wl], axis=0).astype(F32))
+                lhs2[h, d, :, 0 : 2 * tiles] = turned.astype(BF16)
+                lhs2[h, d, :, 2 * tiles : 4 * tiles] = turned.astype(BF16)
 
         for copy in rims:
             copy.wait_recv()
@@ -372,68 +391,139 @@
 
             gacc[strip] = lax.fori_loop(0, top, body, jnp.zeros((TR, cols), F32))
 
-        for r in range(strips // 2):
+        for r in range(0, 2):
             inner_layers(r)
 
         x_copy.wait_recv()
         fill_tiles(x_recv[...])
-        pack_and_send(lhs1, send1, recv1, starts1, 1)
-
-        for r in range(strips // 2, strips):
+        pack_tiles(1)
+
+        for r in range(2, 4):
+            inner_layers(r)
+
+        loads[4].wait()
+        loads[5].wait()
+        frame = as_column(frame_ref[...].astype(F32)).astype(jnp.int32)
+        for h in range(2):
+            seen = jnp.zeros((tiles, wide), F32)
+            for f in range(frames):
+                seen = jnp.where(frame == f, obs_v[f, :, h * wide : (h + 1) * wide], seen)
+            mis[h] = -seen
+
+        def weigh(h, f, d):
+            rh, rl = two_parts(recv1[h, d, f].reshape(RING * CAP, wide))
+            return jnp.dot(
+                wcat[h, d, f],
+                jnp.concatenate([rh, rh, rl, rl], axis=0),
+                preferred_element_type=F32,
+            )
+
+        parts = {}
+        for h in range(2):
+            for d in range(1, RING):
+                i = h * RING + d
+                parts[h, d] = send(
+                    part.at[h, d], part_recv.at[h, d], p_ss.at[i], p_rs.at[i], dense_peer(h, -d)
+                )
+        for f in range(2):
+            for h in range(2):
+                for d in range(1, RING):
+                    slots1[h, f, d].wait_recv()
+                for d in FARTHEST_FIRST + (0,):
+                    if f == 0:
+                        part[h, d] = weigh(h, f, d)
+                    else:
+                        part[h, d] += weigh(h, f, d)
+                        if d:
+                            parts[h, d].start()
+
+        for r in range(4, 6):
+            inner_layers(r)
+
+        spread = {}
+        for h in range(2):
+            for d in range(1, RING):
+                i = h * RING + d
+                spread[h, d] = send(
+                    mis.at[h], mis_recv.at[h, d], m_ss.at[i], m_rs.at[i], dense_peer(h, d)
+                )
+        mis_copies = []
+        for h in range(2):
+            for d in range(1, RING):
+                parts[h, d].wait_recv()
+            mis[h] += (part[h, 0] + part_recv[h, 1]) + (part_recv[h, 2] + part_recv[h, 3])
+            for d in FARTHEST_FIRST:
+                spread[h, d].start()
+            copy = pltpu.make_async_copy(
+                mis.at[h], misfit_out.at[:, h * wide : (h + 1) * wide], out_sem.at[5 + h]
+            )
+            copy.start()
+            mis_copies.append(copy)
+
+        for r in range(6, 7):
+            inner_layers(r)
+
+        slots2 = {}
+        for h in range(2):
+            for f in range(2):
+                for d in range(1, RING):
+                    i = (h * 2 + f) * RING + d
+                    slots2[h, f, d] = send(
+                        send2.at[h, :, f, d],
+                        plane_rows(recv2, h, f, d),
+                        s2_ss.at[i],
+                        s2_rs.at[i],
+                        slot_peer(h, d),
+                    )
+        n_half = LANES // 2
+        for f in (1, 0):
+            for h in range(2):
+                for d in range(RING):
+                    if f == 1:
+                        if d:
+                            spread[h, d].wait_recv()
+                        mh, ml = two_parts(mis_recv[h, d] if d else mis[h])
+                        at = slice(h * wide, (h + 1) * wide)
+                        for i, piece in enumerate((mh, mh, ml, ml)):
+                            rhs2[d, i * tiles : (i + 1) * tiles, at] = piece
+                    packed = jnp.dot(
+                        lhs2[h, d, f * n_half : (f + 1) * n_half],
+                        rhs2[d, :, h * wide : (h + 1) * wide],
+                        preferred_element_type=F32,
+                    )
+                    send2[h, d, f] = packed.reshape(RING, CAP, wide)
+                for d in FARTHEST_FIRST:
+                    slots2[h, f, d].start()
+            recv2[0, f, 0] = send2[0, :, f, 0]
+            recv2[1, f, :, 0] = send2[1, :, f, 0]
+
+        for r in range(7, strips):
             inner_layers(r)
         early = pltpu.make_async_copy(
             outv.at[0 : top - 1], adj_out.at[0 : top - 1], out_sem.at[0]
         )
         early.start()
 
-        loads[4].wait()
-        loads[5].wait()
-        frame = as_column(frame_ref[...].astype(F32)).astype(jnp.int32)
-        seen = jnp.zeros((tiles, cols), F32)
-        for f in range(frames):
-            seen = jnp.where(frame == f, obs_v[f], seen)
-        misv[...] = -seen
-
-        for f in range(2):
-            for copy in copies1[f]:
-                copy.wait_recv()
-            at = slice(f * half, (f + 1) * half)
-            wh, wl = two_parts(wsel[:, at])
-            rh, rl = two_parts(recv1[at])
-            misv[...] += jnp.dot(
-                jnp.concatenate([wh, wl, wh], axis=1),
-                jnp.concatenate([rh, rh, rl], axis=0),
-                preferred_element_type=F32,
-            )
-        mis_copy = pltpu.make_async_copy(misv, misfit_out, out_sem.at[1])
-        mis_copy.start()
-
-        mh, ml = two_parts(misv[...])
-        rhs[0:tiles] = mh
-        rhs[tiles : 2 * tiles] = mh
-        rhs[2 * tiles : 3 * tiles] = ml
-        rhs[3 * tiles : 4 * tiles] = ml
-        starts2, copies2 = exchange(send2, recv2, a2_ss, a2_rs, 1)
-        for f in (1, 0):
-            pack_and_send(lhs2, send2, recv2, starts2, f)
-
-        def gathered(f):
-            for copy in copies2[f]:
-                copy.wait_recv()
-            at = slice(f * half, (f + 1) * half)
-            pick = onehot[:, at].astype(BF16)
+        def gathered(h, f):
+            for d in range(1, RING):
+                slots2[h, f, d].wait_recv()
+            pick = onehot[:, f * half : (f + 1) * half].astype(BF16)
             return jnp.dot(
                 jnp.concatenate([pick, pick, pick], axis=1),
-                jnp.concatenate(three_parts(recv2[at]), axis=0),
+                jnp.concatenate(three_parts(recv2[h, f].reshape(half, wide)), axis=0),
                 preferred_element_type=F32,
             )
 
-        xa_send[...] = gathered(1)
-        xa_copy = partner_copy(xa_send, xa_recv, 1)
-        xa_copy.start()
-        added = gathered(0)
-        xa_copy.wait_recv()
-        added = added + xa_recv[...]
+        xa_copies = []
+        for h in range(2):
+            xa_send[h] = gathered(h, 1)
+            copy = send(xa_send.at[h], xa_recv.at[h], x_ss.at[1 + h], x_rs.at[1 + h], partner)
+            copy.start()
+            xa_copies.append(copy)
+        sums = [gathered(h, 0) for h in range(2)]
+        for h in range(2):
+            xa_copies[h].wait_recv()
+        added = jnp.concatenate([sums[h] + xa_recv[h] for h in range(2)], axis=1)
         for rr in range(TR):
             tiles3[:, rr, :] = added[:, rr * TC : (rr + 1) * TC]
         for r in range(strips):
@@ -479,10 +569,12 @@
         ]
         for copy in last_copies:
             copy.start()
-        sent = rims0 + rims + rims2 + req_copies + [x_copy, xa_copy]
-        for copy in sent + copies1[0] + copies1[1] + copies2[0] + copies2[1]:
+        sent = rims0 + rims + rims2 + req_copies + w_copies + [x_copy] + xa_copies
+        for group in (slots1, parts, spread, slots2):
+            sent.extend(group.values())
+        for copy in sent:
             copy.wait_send()
-        for copy in [early, mis_copy, late] + last_copies:
+        for copy in [early, late] + mis_copies + last_copies:
             copy.wait()
 
     dma = pltpu.SemaphoreType.DMA
@@ -503,7 +595,6 @@
         vmem(4, rows, cols),
         vmem(rows, cols),
         vmem(layers, rows, cols),
-        vmem(tiles, tile),
         vmem(rows, cols),
         *pair(2, 2, cols),
         *pair(2, rows, LANES),
@@ -514,20 +605,32 @@
         vmem(groups, 8, LANES),
         vmem(PLANE, 8, LANES),
         vmem(tiles, TR, TC),
-        *pair(tiles, n_slots),
-        vmem(n_slots, 4 * tiles, dtype=BF16),
+        vmem(tiles, n_slots),
         vmem(n_slots, 4 * tiles, dtype=BF16),
         vmem(4 * tiles, tile, dtype=BF16),
+        vmem(RING, 4 * tiles, tile, dtype=BF16),
+        *pair(2, RING, tiles, LANES),
+        vmem(2, RING, 2, tiles, 4 * tiles, dtype=BF16),
+        vmem(2, RING, LANES, 4 * tiles, dtype=BF16),
         *pair(tiles, tile),
-        *pair(tiles, tile),
-        *pair(n_slots, tile),
-        *pair(n_slots, tile),
+        *pair(2, tiles, tile // 2),
+        vmem(2, 2, RING, RING, CAP, tile // 2),
+        vmem(2, RING, 2, RING, CAP, tile // 2),
+        *pair(2, RING, tiles, tile // 2),
+        vmem(2, tiles, tile // 2),
+        vmem(2, RING, tiles, tile // 2),
+        vmem(2, RING, 2, RING, CAP, tile // 2),
+        vmem(2, 2, RING, RING, CAP, tile // 2),
         dma((6,)),
-        dma((5,)),
+        dma((7,)),
         *[dma((4,)) for _ in range(6)],
-        dma((2,)), dma((2,)),
+        dma((3,)), dma((3,)),
         dma((PLANE,)), dma((PLANE,)),
-        *[dma((2 * PLANE,)) for _ in range(4)],
+        dma((2 * RING,)), dma((2 * RING,)),
+        dma((4 * RING,)), dma((4 * RING,)),
+        dma((2 * RING,)), dma((2 * RING,)),
+        dma((2 * RING,)), dma((2 * RING,)),
+        dma((4 * RING,)), dma((4 * RING,)),
     ]
     in_hbm = pl.BlockSpec(memory_space=pltpu.HBM)
     anywhere = pl.BlockSpec(memory_space=pl.ANY)

time: 87.3 us -> 78.9 us (0.904)
  Pallas kernels: 83.8 us -> 74.9 us
    pallas_call x1, Pallas kernels: 83.8 us -> 74.9 us  [local(): call(*(pltpu.with_memory_space_constraint(x, pltpu.HBM) for x in operands))]
where the time goes in v2:
time: 78.9 us; the launch traced here: 78.3 us
  Pallas kernels  74.9 us (95%)
  local copies, waits for them, and re-layouts  2.73 us (3%)
    pallas_call x1, Pallas kernels, local(): call(*(pltpu.with_memory_space_constraint(x, pltpu.HBM) for x in operands))  74.9 us
    unnamed x3, local copies, waits for them, and re-layouts  2.73 us

profile of v2, /device:TPU:0, one launch (start us, length us, event | category | flops | bytes accessed | tf_op | source)
XLA Modules:
  0.0 78.3 jit_solution(10930906281678428788)
XLA Ops:
  0.6 74.9 %shard_map.103 = (f32[64,1024]{1,0:T(8,128)S(1)}, f32[8,64,1024]{2,1,0:T(8,128)S(1)}, f32[64,1024]{1,0:T(8,128)S(1)}) custom-call(f32[8,64,1024]{2,1,0:T(8,128)} %temp.1, f32[64,1024]{1,0:T(8,128)} %cond.1, f32[8,64,1024]{2,1,0:T(8,128)} %adj.1, f32[64,1024]{1,0:T(8,128)} %grad.1, f32[4,64,1024]{2,1,0:T(8,128)} %obs.1, s32[1,64]{1,0:T(1,128)} %bitcast.5, ...), custom_call_target="tpu_custom_call" | custom-call | tf_op jit(solution)/shard_map/pallas_call | solution.py:663
  75.6 0.7 copy.14
  76.3 1.3 %copy.15 = f32[8,64,1024]{2,1,0:T(8,128)} copy(f32[8,64,1024]{2,1,0:T(8,128)S(1)} %get-tuple-element.7) | data formatting | bytes 4194304
  77.6 0.7 copy.16

commit v3 on v2

v3 whole, which is shorter than its diff:
```python
import jax
import jax.numpy as jnp
from jax import lax
from jax.experimental import pallas as pl
from jax.experimental.pallas import tpu as pltpu
from jax.sharding import PartitionSpec as P

TR = 8
TC = 128
LANES = 128
RATE_PLANE = 0.2
RATE_VERTICAL = 0.08
MESH = pl.DeviceIdType.MESH
F32 = jnp.float32
BF16 = jnp.bfloat16


def iota(shape, dim):
    return lax.broadcasted_iota(jnp.int32, shape, dim)


def two_parts(x):
    hi = x.astype(BF16)
    lo = (x - hi.astype(F32)).astype(BF16)
    return hi, lo


RING = 4
FARTHEST_FIRST = (2, 1, 3)


def make_kernel(n_gx, n_gy, layers, rows, cols, frames, k_blocks):
    tiles = (rows // TR) * (cols // TC)
    row0, col0 = TR, LANES
    row1, col1 = row0 + rows, col0 + cols
    strips = rows // TR
    tile_cols = cols // TC
    top = layers - 1
    n_chunks = 4
    wide = cols // n_chunks
    ring = RING * tiles

    def kernel(
        temp, cond, adj, grad, obs, frame_ref, map_ref, weight_ref,
        misfit_out, adj_out, grad_out,
        tpad, apad, kpad, gin, obs_v, coef, gacc, outv, gradv,
        ns0_send, ns0_recv, ew0_send, ew0_recv,
        ns_send, ns_recv, ew_send, ew_recv,
        ns2_send, ns2_recv, ew2_send, ew2_recv,
        small, tiles3, wfull, lhs1, lhs2,
        gat, part, part_recv, mis, con, con_recv, xa_send, xa_recv,
        in_sem, out_sem,
        rim0_ss, rim0_rs, rim_ss, rim_rs, rim2_ss, rim2_rs, x_ss, x_rs,
        w_ss, w_rs, s1_ss, s1_rs, p_ss, p_rs, m_ss, m_rs, s2_ss, s2_rs,
    ):
        gx = lax.axis_index("gx")
        gy = lax.axis_index("gy")
        gx_y = lax.rem(gx, RING)
        gx_x = lax.rem(gx // RING, 2)
        gx_z = gx // (2 * RING)
        north, south = lax.rem(gx + n_gx - 1, n_gx), lax.rem(gx + 1, n_gx)
        west, east = lax.rem(gy + n_gy - 1, n_gy), lax.rem(gy + 1, n_gy)
        sides = ({"gx": north}, {"gx": south}, {"gy": west}, {"gy": east})
        partner = {"gx": gx + RING - 2 * RING * gx_x}

        def along(dz, dy):
            z = lax.rem(gx_z + dz % RING, RING)
            y = lax.rem(gx_y + dy % RING, RING)
            return {"gx": z * (2 * RING) + gx_x * RING + y}

        def plate_peer(c, d):
            return along(0, d) if c % 2 == 0 else along(d, 0)

        def camera_peer(c, d):
            return along(d, 0) if c % 2 == 0 else along(0, d)

        def send(src, dst, ss, rs, device):
            return pltpu.make_async_remote_copy(
                src_ref=src,
                dst_ref=dst,
                send_sem=ss,
                recv_sem=rs,
                device_id=device,
                device_id_type=MESH,
            )

        barrier = pltpu.get_barrier_semaphore()
        greeted = [along(d, 0) for d in range(1, RING)] + [along(0, d) for d in range(1, RING)]
        greeted += [partner] + list(sides)
        for device in greeted:
            pl.semaphore_signal(barrier, inc=1, device_id=device, device_id_type=MESH)

        body_at = (slice(row0, row1), slice(col0, col1))
        loads = [
            pltpu.make_async_copy(
                temp.at[top - 1 : layers],
                tpad.at[(slice(top - 1, layers), *body_at)],
                in_sem.at[0],
            ),
            pltpu.make_async_copy(cond, kpad.at[body_at], in_sem.at[1]),
            pltpu.make_async_copy(
                temp.at[0 : top - 1], tpad.at[(slice(0, top - 1), *body_at)], in_sem.at[2]
            ),
            pltpu.make_async_copy(adj, apad.at[(slice(None), *body_at)], in_sem.at[3]),
            pltpu.make_async_copy(grad, gin, in_sem.at[4]),
            pltpu.make_async_copy(obs, obs_v, in_sem.at[5]),
        ]
        for load in loads:
            load.start()

        for load in loads[:2]:
            load.wait()
        first, last = row0, row1 - 1
        rim_lane = iota((rows, LANES), 1)
        for side, row in ((0, first), (1, last)):
            ns0_send[side, 0:1] = tpad[top, row : row + 1, col0:col1]
            ns0_send[side, 1:2] = kpad[row : row + 1, col0:col1]
        for side, col in ((0, col0), (1, col1 - 1)):
            ew0_send[side] = jnp.where(
                rim_lane == 0,
                tpad[top, row0:row1, col : col + 1],
                kpad[row0:row1, col : col + 1],
            )

        small[0, 0:k_blocks, 0:tiles] = map_ref[...].astype(F32)
        small[0, k_blocks : 2 * k_blocks, 0:tiles] = weight_ref[...]
        small[2 * RING - 1, 0:1, 0:tiles] = frame_ref[...].astype(F32)

        pl.semaphore_wait(barrier, len(greeted))

        def rim_copies(ns_s, ns_r, ew_s, ew_r, ss, rs):
            copies = []
            for i in range(4):
                src, dst = (ns_s, ns_r) if i < 2 else (ew_s, ew_r)
                copies.append(
                    pltpu.make_async_remote_copy(
                        src_ref=src.at[i % 2],
                        dst_ref=dst.at[1 - i % 2],
                        send_sem=ss.at[i],
                        recv_sem=rs.at[i],
                        device_id=sides[i],
                        device_id_type=MESH,
                    )
                )
            return copies

        rims0 = rim_copies(ns0_send, ns0_recv, ew0_send, ew0_recv, rim0_ss, rim0_rs)
        for copy in rims0:
            copy.start()

        w_copies = []
        for h in range(2):
            for d in range(1, RING):
                i = h * (RING - 1) + d
                copy = send(
                    small.at[0], small.at[i], w_ss.at[i], w_rs.at[i], camera_peer(h, d)
                )
                copy.start()
                w_copies.append(copy)

        has_north = jnp.where(gx > 0, 1.0, 0.0)
        has_south = jnp.where(gx < n_gx - 1, 1.0, 0.0)
        has_west = jnp.where(gy > 0, 1.0, 0.0)
        has_east = jnp.where(gy < n_gy - 1, 1.0, 0.0)

        def column_rims(pad, index, source, lane_at):
            for side, has, at in ((0, has_west, 0), (1, has_east, col1)):
                value = source[side, :, lane_at : lane_at + 1] * has
                pad[(*index, slice(row0, row1), slice(at, at + LANES))] = jnp.broadcast_to(
                    value, (rows, LANES)
                )

        for copy in rims0:
            copy.wait_recv()
        kpad[first - 1 : first, col0:col1] = ns0_recv[0, 1:2] * has_north
        kpad[last + 1 : last + 2, col0:col1] = ns0_recv[1, 1:2] * has_south
        column_rims(kpad, (), ew0_recv, 1)
        tpad[top, first - 1 : first, col0:col1] = ns0_recv[0, 0:1] * has_north
        tpad[top, last + 1 : last + 2, col0:col1] = ns0_recv[1, 0:1] * has_south
        column_rims(tpad, (top,), ew0_recv, 0)

        def around(pad, index, r):
            a, b = row0 + r * TR, row0 + (r + 1) * TR
            return (
                pad[(*index, slice(a, b), slice(col0, col1))],
                pad[(*index, slice(a, b), slice(col0 + 1, col1 + 1))],
                pad[(*index, slice(a, b), slice(col0 - 1, col1 - 1))],
                pad[(*index, slice(a - 1, b - 1), slice(col0, col1))],
                pad[(*index, slice(a + 1, b + 1), slice(col0, col1))],
            )

        for r in range(strips):
            kc, ke, kw, kn, ks = around(kpad, (), r)
            strip = slice(r * TR, (r + 1) * TR)
            faces = [0.5 * RATE_PLANE * (kc + other) for other in (ke, kw, kn, ks)]
            for i in range(4):
                coef[i, strip] = faces[i]
            tc, te, tw, tn, ts = around(tpad, (top,), r)
            under = tpad[top - 1, row0 + r * TR : row0 + (r + 1) * TR, col0:col1]
            value = tc + RATE_VERTICAL * (under - tc)
            for face, other in zip(faces, (te, tw, tn, ts)):
                value = value + face * (other - tc)
            for u in range(tile_cols):
                tiles3[r * tile_cols + u] = value[:, u * TC : (u + 1) * TC]

        x_copies, slots1 = [], {}
        for c in range(n_chunks):
            for rr in range(wide // TC):
                gat[c, 0, 0, :, rr * TC : (rr + 1) * TC] = tiles3[:, c * (wide // TC) + rr, :]
            x_copies.append(
                send(gat.at[c, 0, 0], gat.at[c, 1, 0], x_ss.at[c], x_rs.at[c], partner)
            )
            for f in range(2):
                for d in range(1, RING):
                    i = (c * 2 + f) * RING + d
                    slots1[c, f, d] = send(
                        gat.at[c, f, 0], gat.at[c, f, d], s1_ss.at[i], s1_rs.at[i], plate_peer(c, -d)
                    )
            x_copies[c].start()
            for d in FARTHEST_FIRST:
                slots1[c, 0, d].start()

        def pass_far(c):
            x_copies[c].wait_recv()
            for d in FARTHEST_FIRST:
                slots1[c, 1, d].start()

        for load in loads[2:4]:
            load.wait()
        for side, row in ((0, first), (1, last)):
            ns_send[side, 0:top] = tpad[0:top, row, col0:col1]
            ns_send[side, layers : layers + top] = apad[0:top, row, col0:col1]
        for side, col in ((0, col0), (1, col1 - 1)):
            packed = jnp.zeros((rows, LANES), F32)
            for l in range(top):
                packed = jnp.where(rim_lane == l, tpad[l, row0:row1, col : col + 1], packed)
                packed = jnp.where(
                    rim_lane == layers + l, apad[l, row0:row1, col : col + 1], packed
                )
            ew_send[side] = packed
        rims = rim_copies(ns_send, ns_recv, ew_send, ew_recv, rim_ss, rim_rs)
        for copy in rims:
            copy.start()


        pass_far(0)
        for copy in w_copies:
            copy.wait_recv()
        turned = jnp.transpose(small[...].reshape(2 * RING * TR, LANES))[0:tiles]
        lane_tile = iota((tiles, 2 * ring), 1)

        def weigh_matrix(h):
            for d in range(RING):
                i = (h * (RING - 1) + d) * TR if d else 0
                code = turned[:, i : i + k_blocks].astype(jnp.int32)
                weight = turned[:, i + k_blocks : i + 2 * k_blocks]
                plate = code >> ((tiles * n_gy).bit_length() - 1)
                far = ((plate ^ gx) >> 2) & 1
                dz = ((plate >> 3) - gx_z) & 3
                dy = (plate - gx) & 3
                here, step = (dz, dy) if h == 0 else (dy, dz)
                at = jnp.where(here == 0, far * ring + step * tiles + (code & (tiles - 1)), -1)
                total = jnp.zeros((tiles, 2 * ring), F32)
                for k in range(k_blocks):
                    hit = at[:, k : k + 1] == lane_tile
                    total = total + jnp.where(hit, weight[:, k : k + 1], 0.0)
                wfull[h, d * tiles : (d + 1) * tiles] = total
                for i, piece in enumerate(two_parts(total)):
                    for f in range(2):
                        lhs1[h, f, i * ring + d * tiles : i * ring + (d + 1) * tiles] = piece[
                            :, f * ring : (f + 1) * ring
                        ]

        weigh_matrix(0)
        pass_far(1)
        weigh_matrix(1)
        pass_far(2)
        pass_far(3)

        def weigh(lhs, value):
            hi, lo = two_parts(value)
            both = jnp.dot(lhs[...], hi, preferred_element_type=F32)
            more = jnp.dot(lhs[0:ring], lo, preferred_element_type=F32)
            return both[0:ring] + (both[ring : 2 * ring] + more)

        for h in range(2):
            for i, piece in enumerate(two_parts(jnp.transpose(wfull[h]))):
                for f in range(2):
                    lhs2[h, f, i * ring : (i + 1) * ring] = piece[f * ring : (f + 1) * ring]

        edge = jnp.zeros((rows, LANES), F32)
        apad[top, row0:row1, 0:col0] = edge
        apad[top, row0:row1, col1 : col1 + LANES] = edge
        apad[top, first - 1 : first, col0:col1] = jnp.zeros((1, cols), F32)
        apad[top, last + 1 : last + 2, col0:col1] = jnp.zeros((1, cols), F32)

        for copy in rims:
            copy.wait_recv()
        for l in range(top):
            column_rims(tpad, (l,), ew_recv, l)
            column_rims(apad, (l,), ew_recv, layers + l)
        tpad[0:top, first - 1, col0:col1] = ns_recv[0, 0:top] * has_north
        tpad[0:top, last + 1, col0:col1] = ns_recv[1, 0:top] * has_south
        apad[0:top, first - 1, col0:col1] = ns_recv[0, layers : layers + top] * has_north
        apad[0:top, last + 1, col0:col1] = ns_recv[1, layers : layers + top] * has_south

        def layer_step(l, r, total):
            strip = slice(r * TR, (r + 1) * TR)
            tc, *t_near = around(tpad, (l,), r)
            ac, *a_near = around(apad, (l,), r)
            flow = jnp.zeros_like(ac)
            for i in range(4):
                step = a_near[i] - ac
                flow = flow + coef[i, strip] * step
                total = total + (t_near[i] - tc) * step
            return ac + flow, ac, total

        def inner_layers(r):
            strip = slice(r * TR, (r + 1) * TR)
            inner = slice(row0 + r * TR, row0 + (r + 1) * TR)

            def body(l, total):
                value, ac, total = layer_step(l, r, total)
                above = apad[l + 1, inner, col0:col1]
                under = apad[jnp.maximum(l - 1, 0), inner, col0:col1]
                outv[l, strip] = value + RATE_VERTICAL * ((above - ac) + (under - ac))
                return total

            gacc[strip] = lax.fori_loop(0, top, body, jnp.zeros((TR, cols), F32))

        for r in range(0, 2):
            inner_layers(r)

        loads[4].wait()
        loads[5].wait()
        i = (2 * RING - 1) * TR
        frame = turned[:, i : i + 1].astype(jnp.int32)

        def columns(c):
            return slice(c * wide, (c + 1) * wide)

        for c in range(n_chunks):
            seen = jnp.zeros((tiles, wide), F32)
            for f in range(frames):
                seen = jnp.where(frame == f, obs_v[f, :, columns(c)], seen)
            mis[c, 0] = -seen

        parts, spread = {}, {}
        for c in range(n_chunks):
            for d in range(1, RING):
                i = c * RING + d
                parts[c, d] = send(
                    part.at[c, d], part_recv.at[c, d], p_ss.at[i], p_rs.at[i], camera_peer(c, -d)
                )
                spread[c, d] = send(
                    mis.at[c, 0], mis.at[c, d], m_ss.at[i], m_rs.at[i], camera_peer(c, d)
                )
        for f in range(2):
            for c in range(n_chunks):
                for d in range(1, RING):
                    slots1[c, f, d].wait_recv()
                value = weigh(lhs1.at[c % 2, f], gat[c, f].reshape(ring, wide))
                value = value.reshape(RING, tiles, wide)
                if f == 0:
                    part[c] = value
                else:
                    part[c] += value
                    for d in FARTHEST_FIRST:
                        parts[c, d].start()

        inner_layers(2)

        mis_copies = []
        for c in range(n_chunks):
            for d in range(1, RING):
                parts[c, d].wait_recv()
            mis[c, 0] += (part[c, 0] + part_recv[c, 1]) + (part_recv[c, 2] + part_recv[c, 3])
            for d in FARTHEST_FIRST:
                spread[c, d].start()
            copy = pltpu.make_async_copy(
                mis.at[c, 0], misfit_out.at[:, columns(c)], out_sem.at[4 + c]
            )
            copy.start()
            mis_copies.append(copy)

        inner_layers(3)

        back = {}
        for f in (1, 0):
            for c in range(n_chunks):
                if f == 1:
                    for d in range(1, RING):
                        spread[c, d].wait_recv()
                value = weigh(lhs2.at[c % 2, f], mis[c].reshape(ring, wide))
                con[c, f] = value.reshape(RING, tiles, wide)
                for d in FARTHEST_FIRST:
                    i = (c * 2 + f) * RING + d
                    back[c, f, d] = send(
                        con.at[c, f, d], con_recv.at[c, f, d], s2_ss.at[i], s2_rs.at[i], plate_peer(c, d)
                    )
                    back[c, f, d].start()

        for r in range(4, strips):
            inner_layers(r)
        early = pltpu.make_async_copy(
            outv.at[0 : top - 1], adj_out.at[0 : top - 1], out_sem.at[0]
        )
        early.start()
        sent = rims0 + rims + w_copies + x_copies
        for group in (slots1, parts, spread):
            sent.extend(group.values())
        for copy in sent:
            copy.wait_send()

        def gathered(c, f):
            for d in range(1, RING):
                back[c, f, d].wait_recv()
            return (con[c, f, 0] + con_recv[c, f, 1]) + (con_recv[c, f, 2] + con_recv[c, f, 3])

        xa_copies = []
        for c in range(n_chunks):
            xa_send[c] = gathered(c, 1)
            i = n_chunks + c
            copy = send(xa_send.at[c], xa_recv.at[c], x_ss.at[i], x_rs.at[i], partner)
            copy.start()
            xa_copies.append(copy)
        for c in range(n_chunks):
            near = gathered(c, 0)
            xa_copies[c].wait_recv()
            added = near + xa_recv[c]
            for rr in range(wide // TC):
                tiles3[:, c * (wide // TC) + rr, :] = added[:, rr * TC : (rr + 1) * TC]
        for r in range(strips):
            strip = slice(r * TR, (r + 1) * TR)
            inner = slice(row0 + r * TR, row0 + (r + 1) * TR)
            extra = jnp.concatenate(
                [tiles3[r * tile_cols + u] for u in range(tile_cols)], axis=1
            )
            apad[top, inner, col0:col1] += extra
            outv[top - 1, strip] += RATE_VERTICAL * extra

        for side, row in ((0, first), (1, last)):
            ns2_send[side] = apad[top, row : row + 1, col0:col1]
        for side, col in ((0, col0), (1, col1 - 1)):
            ew2_send[side] = jnp.broadcast_to(
                apad[top, row0:row1, col : col + 1], (rows, LANES)
            )
        rims2 = rim_copies(ns2_send, ns2_recv, ew2_send, ew2_recv, rim2_ss, rim2_rs)
        for copy in rims2:
            copy.start()
        late = pltpu.make_async_copy(
            outv.at[top - 1], adj_out.at[top - 1], out_sem.at[2]
        )
        late.start()
        for r in range(strips):
            strip = slice(r * TR, (r + 1) * TR)
            inner = slice(row0 + r * TR, row0 + (r + 1) * TR)
            value, ac, total = layer_step(top, r, gacc[strip])
            under = apad[top - 1, inner, col0:col1]
            outv[top, strip] = value + RATE_VERTICAL * (under - ac)
            gradv[strip] = gin[strip] - (0.5 * RATE_PLANE) * total
        for copy in list(back.values()) + xa_copies:
            copy.wait_send()

        for copy in rims2:
            copy.wait_recv()
        for side, has, row, beyond in ((0, has_north, 0, first - 1), (1, has_south, rows - 1, last + 1)):
            at = slice(row, row + 1)
            rim = ns2_recv[side] * has
            slope = tpad[top, beyond : beyond + 1, col0:col1] - tpad[
                top, row0 + row : row0 + row + 1, col0:col1
            ]
            outv[top, at] += coef[2 + side, at] * rim
            gradv[at] -= (0.5 * RATE_PLANE) * slope * rim
        for side, has, face, at, beyond, edge_lane in (
            (0, has_west, 1, 0, 0, 0),
            (1, has_east, 0, cols - LANES, col1, LANES - 1),
        ):
            at = slice(at, at + LANES)
            rim = jnp.where(rim_lane == edge_lane, ew2_recv[side] * has, 0.0)
            slope = tpad[top, row0:row1, beyond : beyond + LANES] - tpad[
                top, row0:row1, col0 + at.start : col0 + at.stop
            ]
            outv[top, :, at] += coef[face, :, at] * rim
            gradv[:, at] -= (0.5 * RATE_PLANE) * slope * rim

        last_copies = [
            pltpu.make_async_copy(outv.at[top], adj_out.at[top], out_sem.at[3]),
            pltpu.make_async_copy(gradv, grad_out, out_sem.at[1]),
        ]
        for copy in last_copies:
            copy.start()
        for copy in rims2:
            copy.wait_send()
        for copy in [early, late] + mis_copies + last_copies:
            copy.wait()

    dma = pltpu.SemaphoreType.DMA

    def vmem(*shape, dtype=F32):
        return pltpu.VMEM(shape, dtype)

    def pair(*shape):
        return [vmem(*shape), vmem(*shape)]

    tile = TR * TC
    scratch = [
        vmem(layers, rows + 2 * TR, cols + 2 * LANES),
        vmem(layers, rows + 2 * TR, cols + 2 * LANES),
        vmem(rows + 2 * TR, cols + 2 * LANES),
        vmem(rows, cols),
        vmem(frames, tiles, tile),
        vmem(4, rows, cols),
        vmem(rows, cols),
        vmem(layers, rows, cols),
        vmem(rows, cols),
        *pair(2, 2, cols),
        *pair(2, rows, LANES),
        *pair(2, 2 * layers, cols),
        *pair(2, rows, LANES),
        *pair(2, 1, cols),
        *pair(2, rows, LANES),
        vmem(2 * RING, TR, LANES),
        vmem(tiles, TR, TC),
        vmem(2, ring, 2 * ring),
        vmem(2, 2, 2 * ring, ring, dtype=BF16),
        vmem(2, 2, 2 * ring, ring, dtype=BF16),
        vmem(n_chunks, 2, RING, tiles, wide),
        *pair(n_chunks, RING, tiles, wide),
        vmem(n_chunks, RING, tiles, wide),
        *pair(n_chunks, 2, RING, tiles, wide),
        *pair(n_chunks, tiles, wide),
        dma((6,)),
        dma((4 + n_chunks,)),
        *[dma((4,)) for _ in range(6)],
        dma((2 * n_chunks,)), dma((2 * n_chunks,)),
        dma((2 * RING,)), dma((2 * RING,)),
        dma((2 * n_chunks * RING,)), dma((2 * n_chunks * RING,)),
        dma((n_chunks * RING,)), dma((n_chunks * RING,)),
        dma((n_chunks * RING,)), dma((n_chunks * RING,)),
        dma((2 * n_chunks * RING,)), dma((2 * n_chunks * RING,)),
    ]
    in_hbm = pl.BlockSpec(memory_space=pltpu.HBM)
    anywhere = pl.BlockSpec(memory_space=pl.ANY)
    in_vmem = pl.BlockSpec(memory_space=pltpu.VMEM)
    return pl.pallas_call(
        kernel,
        out_shape=(
            jax.ShapeDtypeStruct((tiles, tile), F32),
            jax.ShapeDtypeStruct((layers, rows, cols), F32),
            jax.ShapeDtypeStruct((rows, cols), F32),
        ),
        in_specs=[in_hbm] * 5 + [in_vmem] * 3,
        out_specs=[anywhere] * 3,
        scratch_shapes=scratch,
        compiler_params=pltpu.CompilerParams(
            collective_id=0, has_side_effects=True, vmem_limit_bytes=48 * 1024 * 1024
        ),
    )


def solution(mesh):
    n_gx, n_gy = mesh.shape["gx"], mesh.shape["gy"]

    def local(temp, cond, adj, grad, obs, frame_index, source_map, source_weight):
        layers, rows, cols = temp.shape
        call = make_kernel(n_gx, n_gy, layers, rows, cols, obs.shape[0], source_map.shape[1])
        operands = (
            temp, cond, adj, grad, obs, frame_index[None, :], source_map.T, source_weight.T
        )
        return call(*(pltpu.with_memory_space_constraint(x, pltpu.HBM) for x in operands))

    placed = (
        P(None, "gx", "gy"),
        P("gx", "gy"),
        P(None, "gx", "gy"),
        P("gx", "gy"),
        P(None, ("gx", "gy"), None),
        P(("gx", "gy")),
        P(("gx", "gy"), None),
        P(("gx", "gy"), None),
    )
    return jax.shard_map(
        local,
        mesh=mesh,
        in_specs=placed,
        out_specs=(P(("gx", "gy"), None), P(None, "gx", "gy"), P("gx", "gy")),
        check_vma=False,
    )
```

time: 78.9 us -> 71.7 us (0.909)
  Pallas kernels: 74.9 us -> 68.2 us
    pallas_call x1, Pallas kernels: 74.9 us -> 68.2 us  [local(): call(*(pltpu.with_memory_space_constraint(x, pltpu.HBM) for x in operands))]
where the time goes in v3:
time: 71.7 us; the launch traced here: 71.5 us
  Pallas kernels  68.2 us (95%)
  local copies, waits for them, and re-layouts  2.73 us (4%)
    pallas_call x1, Pallas kernels, local(): call(*(pltpu.with_memory_space_constraint(x, pltpu.HBM) for x in operands))  68.2 us
    unnamed x3, local copies, waits for them, and re-layouts  2.73 us

profile of v3, /device:TPU:0, one launch (start us, length us, event | category | flops | bytes accessed | tf_op | source)
XLA Modules:
  0.0 71.5 jit_solution(3940858422862800667)
XLA Ops:
  0.6 68.2 %shard_map.103 = (f32[64,1024]{1,0:T(8,128)S(1)}, f32[8,64,1024]{2,1,0:T(8,128)S(1)}, f32[64,1024]{1,0:T(8,128)S(1)}) custom-call(f32[8,64,1024]{2,1,0:T(8,128)} %temp.1, f32[64,1024]{1,0:T(8,128)} %cond.1, f32[8,64,1024]{2,1,0:T(8,128)} %adj.1, f32[64,1024]{1,0:T(8,128)} %grad.1, f32[4,64,1024]{2,1,0:T(8,128)} %obs.1, s32[1,64]{1,0:T(1,128)} %bitcast.5, ...), custom_call_target="tpu_custom_call" | custom-call | tf_op jit(solution)/shard_map/pallas_call | solution.py:571
  68.8 0.7 copy.14
  69.5 1.3 %copy.15 = f32[8,64,1024]{2,1,0:T(8,128)} copy(f32[8,64,1024]{2,1,0:T(8,128)S(1)} %get-tuple-element.7) | data formatting | bytes 4194304
  70.8 0.7 copy.16

commit v4 on v3

--- a/solution.py
+++ b/solution.py
@@ -7,6 +7,7 @@
 
 TR = 8
 TC = 128
+CAP = 16
 LANES = 128
 RATE_PLANE = 0.2
 RATE_VERTICAL = 0.08
@@ -26,32 +27,39 @@
 
 
 RING = 4
+PLANE = RING * RING
 FARTHEST_FIRST = (2, 1, 3)
 
 
 def make_kernel(n_gx, n_gy, layers, rows, cols, frames, k_blocks):
     tiles = (rows // TR) * (cols // TC)
+    half = PLANE * CAP
+    n_slots = 2 * half
     row0, col0 = TR, LANES
     row1, col1 = row0 + rows, col0 + cols
     strips = rows // TR
     tile_cols = cols // TC
     top = layers - 1
+    per_group = LANES // CAP
+    groups = PLANE // per_group
+    others = range(1, PLANE)
     n_chunks = 4
     wide = cols // n_chunks
-    ring = RING * tiles
 
     def kernel(
-        temp, cond, adj, grad, obs, frame_ref, map_ref, weight_ref,
-        misfit_out, adj_out, grad_out,
-        tpad, apad, kpad, gin, obs_v, coef, gacc, outv, gradv,
+        temp, cond, adj, grad, obs, frame_in, map_in, weight_in,
+        misfit_out, outv, gradv,
+        tpad, apad, kpad, gin, obs_v, coef, gacc, map_v, weight_v, frame_v,
         ns0_send, ns0_recv, ew0_send, ew0_recv,
         ns_send, ns_recv, ew_send, ew_recv,
         ns2_send, ns2_recv, ew2_send, ew2_recv,
-        small, tiles3, wfull, lhs1, lhs2,
-        gat, part, part_recv, mis, con, con_recv, xa_send, xa_recv,
-        in_sem, out_sem,
+        small, req_send, req_recv, tiles3, onehot, lhs1, rhs,
+        wsend, wblk, wcat, lhs2,
+        x_send, x_recv, xa_send, xa_recv,
+        send1, recv1, part, part_recv, mis, mis_recv, send2, recv2,
+        in_sem,
         rim0_ss, rim0_rs, rim_ss, rim_rs, rim2_ss, rim2_rs, x_ss, x_rs,
-        w_ss, w_rs, s1_ss, s1_rs, p_ss, p_rs, m_ss, m_rs, s2_ss, s2_rs,
+        req_ss, req_rs, w_ss, w_rs, s1_ss, s1_rs, p_ss, p_rs, m_ss, m_rs, s2_ss, s2_rs,
     ):
         gx = lax.axis_index("gx")
         gy = lax.axis_index("gy")
@@ -68,11 +76,11 @@
             y = lax.rem(gx_y + dy % RING, RING)
             return {"gx": z * (2 * RING) + gx_x * RING + y}
 
-        def plate_peer(c, d):
-            return along(0, d) if c % 2 == 0 else along(d, 0)
-
-        def camera_peer(c, d):
-            return along(d, 0) if c % 2 == 0 else along(0, d)
+        def slot_peer(h, d):
+            return along(0, d) if h == 0 else along(d, 0)
+
+        def dense_peer(h, d):
+            return along(d, 0) if h == 0 else along(0, d)
 
         def send(src, dst, ss, rs, device):
             return pltpu.make_async_remote_copy(
@@ -83,12 +91,6 @@
                 device_id=device,
                 device_id_type=MESH,
             )
-
-        barrier = pltpu.get_barrier_semaphore()
-        greeted = [along(d, 0) for d in range(1, RING)] + [along(0, d) for d in range(1, RING)]
-        greeted += [partner] + list(sides)
-        for device in greeted:
-            pl.semaphore_signal(barrier, inc=1, device_id=device, device_id_type=MESH)
 
         body_at = (slice(row0, row1), slice(col0, col1))
         loads = [
@@ -104,8 +106,19 @@
             pltpu.make_async_copy(adj, apad.at[(slice(None), *body_at)], in_sem.at[3]),
             pltpu.make_async_copy(grad, gin, in_sem.at[4]),
             pltpu.make_async_copy(obs, obs_v, in_sem.at[5]),
+            pltpu.make_async_copy(map_in, map_v, in_sem.at[6]),
+            pltpu.make_async_copy(weight_in, weight_v, in_sem.at[7]),
+            pltpu.make_async_copy(frame_in, frame_v, in_sem.at[8]),
         ]
-        for load in loads:
+        for load in loads[:2]:
+            load.start()
+
+        barrier = pltpu.get_barrier_semaphore()
+        greeted = [along(b % RING, b // RING) for b in others] + [partner] + list(sides)
+        for device in greeted:
+            pl.semaphore_signal(barrier, inc=1, device_id=device, device_id_type=MESH)
+
+        for load in loads[6:] + loads[2:6]:
             load.start()
 
         for load in loads[:2]:
@@ -122,10 +135,6 @@
                 kpad[row0:row1, col : col + 1],
             )
 
-        small[0, 0:k_blocks, 0:tiles] = map_ref[...].astype(F32)
-        small[0, k_blocks : 2 * k_blocks, 0:tiles] = weight_ref[...]
-        small[2 * RING - 1, 0:1, 0:tiles] = frame_ref[...].astype(F32)
-
         pl.semaphore_wait(barrier, len(greeted))
 
         def rim_copies(ns_s, ns_r, ew_s, ew_r, ss, rs):
@@ -148,15 +157,69 @@
         for copy in rims0:
             copy.start()
 
+        for load in loads[6:]:
+            load.wait()
+        small[0:k_blocks, 0:tiles] = map_v[...].astype(F32)
+        small[k_blocks : 2 * k_blocks, 0:tiles] = weight_v[...]
+        small[2 * k_blocks : 2 * k_blocks + 1, 0:tiles] = frame_v[...].astype(F32)
+        columns_of = jnp.transpose(small[...])[0:tiles]
+        weight = columns_of[:, k_blocks : 2 * k_blocks]
+        code = columns_of[:, 0:k_blocks].astype(jnp.int32)
+        plate = code >> ((tiles * n_gy).bit_length() - 1)
+        far = ((plate ^ gx) >> 2) & 1
+        dz = ((plate >> 3) - gx_z) & 3
+        dy = (plate - gx) & 3
+        block = far * PLANE + dy * RING + dz
+        wish = ((code & (tiles - 1)) + 1).astype(F32)
+        lane = iota((tiles, LANES), 1)
+        lane_slot = iota((tiles, n_slots), 1)
+        below = jnp.where(iota((tiles, tiles), 0) > iota((tiles, tiles), 1), 1.0, 0.0)
+        hits = [jnp.where(block[:, k : k + 1] == lane, 1.0, 0.0) for k in range(k_blocks)]
+        before = jnp.dot(below, jnp.concatenate(hits, axis=1), preferred_element_type=F32)
+        base = jnp.zeros((1, LANES), F32)
+        wanted = jnp.zeros((tiles, n_slots), F32)
+        weights = [jnp.zeros((tiles, n_slots), F32) for _ in range(2)]
+        for k in range(k_blocks):
+            earlier = before[:, k * LANES : (k + 1) * LANES] + base
+            base = base + jnp.sum(hits[k], axis=0, keepdims=True)
+            rank = jnp.sum(hits[k] * earlier, axis=1, keepdims=True).astype(jnp.int32)
+            col = slice(k, k + 1)
+            here = block[:, col] * CAP + rank == lane_slot
+            wanted = wanted + jnp.where(here, wish[:, col], 0.0)
+            for h, (dense, slot) in enumerate(((dz, dy), (dy, dz))):
+                at = (dense * LANES + far * (LANES // 2) + slot * CAP)[:, col] + rank
+                weights[h] = weights[h] + jnp.where(at == lane_slot, weight[:, col], 0.0)
+        for h in range(2):
+            for d in range(RING):
+                wsend[h, d] = weights[h][:, d * LANES : (d + 1) * LANES]
+            wblk[h, 0] = weights[h][:, 0:LANES]
+        asked = jnp.sum(wanted, axis=0, keepdims=True)
+        for g in range(groups):
+            for f in range(2):
+                at = f * half + g * LANES
+                req_send[g, f : f + 1] = asked[:, at : at + LANES]
+
+        req_copies = []
+        for b in others:
+            copy = send(
+                req_send.at[b // per_group],
+                req_recv.at[b],
+                req_ss.at[b],
+                req_rs.at[b],
+                along(b % RING, b // RING),
+            )
+            copy.start()
+            req_copies.append(copy)
         w_copies = []
         for h in range(2):
             for d in range(1, RING):
-                i = h * (RING - 1) + d
+                i = h * RING + d
                 copy = send(
-                    small.at[0], small.at[i], w_ss.at[i], w_rs.at[i], camera_peer(h, d)
+                    wsend.at[h, d], wblk.at[h, d], w_ss.at[i], w_rs.at[i], dense_peer(h, d)
                 )
                 copy.start()
                 w_copies.append(copy)
+        req_recv[0] = req_send[0]
 
         has_north = jnp.where(gx > 0, 1.0, 0.0)
         has_south = jnp.where(gx < n_gx - 1, 1.0, 0.0)
@@ -203,27 +266,67 @@
             for u in range(tile_cols):
                 tiles3[r * tile_cols + u] = value[:, u * TC : (u + 1) * TC]
 
-        x_copies, slots1 = [], {}
-        for c in range(n_chunks):
-            for rr in range(wide // TC):
-                gat[c, 0, 0, :, rr * TC : (rr + 1) * TC] = tiles3[:, c * (wide // TC) + rr, :]
-            x_copies.append(
-                send(gat.at[c, 0, 0], gat.at[c, 1, 0], x_ss.at[c], x_rs.at[c], partner)
-            )
+        x_copies = []
+        for i in range(2):
+            for rr in range(TR // 2):
+                x_send[i, :, rr * TC : (rr + 1) * TC] = tiles3[:, i * (TR // 2) + rr, :]
+            copy = send(x_send.at[i], x_recv.at[i], x_ss.at[i], x_rs.at[i], partner)
+            copy.start()
+            x_copies.append(copy)
+
+        for copy in req_copies:
+            copy.wait_recv()
+        group_lane = iota((per_group, LANES), 1) // CAP
+        group_row = iota((per_group, LANES), 0)
+        tile_row = iota((tiles, LANES), 0).astype(F32)
+        for f in range(2):
+            picks = []
+            for g in range(groups):
+                block = req_recv[g * per_group : (g + 1) * per_group, f, :]
+                line = jnp.sum(
+                    jnp.where(group_lane == group_row, block, 0.0), axis=0, keepdims=True
+                )
+                picks.append(jnp.where(line - 1.0 == tile_row, 1.0, 0.0))
+            pick = jnp.concatenate(picks, axis=1)
+            onehot[:, f * half : (f + 1) * half] = pick
+            turned = jnp.transpose(jnp.concatenate([pick, pick], axis=0)).astype(BF16)
+            lhs1[f * half : (f + 1) * half] = turned
+
+        def plane_rows(ref, c, f, d):
+            return ref.at[c, f, d] if c % 2 == 0 else ref.at[c, f, :, d]
+
+        slots1 = {}
+        for c in range(n_chunks):
             for f in range(2):
                 for d in range(1, RING):
                     i = (c * 2 + f) * RING + d
                     slots1[c, f, d] = send(
-                        gat.at[c, f, 0], gat.at[c, f, d], s1_ss.at[i], s1_rs.at[i], plate_peer(c, -d)
+                        plane_rows(send1, c, f, d),
+                        recv1.at[c, :, f, d],
+                        s1_ss.at[i],
+                        s1_rs.at[i],
+                        slot_peer(c % 2, -d),
                     )
-            x_copies[c].start()
-            for d in FARTHEST_FIRST:
-                slots1[c, 0, d].start()
-
-        def pass_far(c):
-            x_copies[c].wait_recv()
-            for d in FARTHEST_FIRST:
-                slots1[c, 1, d].start()
+
+        def columns(c, count=1):
+            return slice(c * wide, (c + count) * wide)
+
+        def pack_tiles(f, pair, source):
+            for i, piece in enumerate(two_parts(source)):
+                rhs[i * tiles : (i + 1) * tiles, columns(pair, 2)] = piece
+            for c in (pair, pair + 1):
+                packed = jnp.dot(
+                    lhs1[f * half : (f + 1) * half],
+                    rhs[:, columns(c)],
+                    preferred_element_type=F32,
+                )
+                send1[c, f] = packed.reshape(RING, RING, CAP, wide)
+                for d in FARTHEST_FIRST:
+                    slots1[c, f, d].start()
+                recv1[c, :, f, 0] = send1[c, f, 0] if c % 2 == 0 else send1[c, f, :, 0]
+
+        for pair in (0, 2):
+            pack_tiles(0, pair, x_send[pair // 2])
 
         for load in loads[2:4]:
             load.wait()
@@ -242,51 +345,25 @@
         for copy in rims:
             copy.start()
 
-
-        pass_far(0)
         for copy in w_copies:
             copy.wait_recv()
-        turned = jnp.transpose(small[...].reshape(2 * RING * TR, LANES))[0:tiles]
-        lane_tile = iota((tiles, 2 * ring), 1)
-
-        def weigh_matrix(h):
+        for h in range(2):
             for d in range(RING):
-                i = (h * (RING - 1) + d) * TR if d else 0
-                code = turned[:, i : i + k_blocks].astype(jnp.int32)
-                weight = turned[:, i + k_blocks : i + 2 * k_blocks]
-                plate = code >> ((tiles * n_gy).bit_length() - 1)
-                far = ((plate ^ gx) >> 2) & 1
-                dz = ((plate >> 3) - gx_z) & 3
-                dy = (plate - gx) & 3
-                here, step = (dz, dy) if h == 0 else (dy, dz)
-                at = jnp.where(here == 0, far * ring + step * tiles + (code & (tiles - 1)), -1)
-                total = jnp.zeros((tiles, 2 * ring), F32)
-                for k in range(k_blocks):
-                    hit = at[:, k : k + 1] == lane_tile
-                    total = total + jnp.where(hit, weight[:, k : k + 1], 0.0)
-                wfull[h, d * tiles : (d + 1) * tiles] = total
-                for i, piece in enumerate(two_parts(total)):
-                    for f in range(2):
-                        lhs1[h, f, i * ring + d * tiles : i * ring + (d + 1) * tiles] = piece[
-                            :, f * ring : (f + 1) * ring
-                        ]
-
-        weigh_matrix(0)
-        pass_far(1)
-        weigh_matrix(1)
-        pass_far(2)
-        pass_far(3)
-
-        def weigh(lhs, value):
-            hi, lo = two_parts(value)
-            both = jnp.dot(lhs[...], hi, preferred_element_type=F32)
-            more = jnp.dot(lhs[0:ring], lo, preferred_element_type=F32)
-            return both[0:ring] + (both[ring : 2 * ring] + more)
+                for i, piece in enumerate(two_parts(wblk[h, d])):
+                    wcat[h, d, i * tiles : (i + 1) * tiles] = jnp.concatenate(
+                        [piece, piece], axis=1
+                    )
+
+        for pair in (0, 2):
+            x_copies[pair // 2].wait_recv()
+            pack_tiles(1, pair, x_recv[pair // 2])
 
         for h in range(2):
-            for i, piece in enumerate(two_parts(jnp.transpose(wfull[h]))):
-                for f in range(2):
-                    lhs2[h, f, i * ring : (i + 1) * ring] = piece[f * ring : (f + 1) * ring]
+            for d in range(RING):
+                parts_of = jnp.concatenate(two_parts(wblk[h, d]), axis=0).astype(F32)
+                turned = jnp.transpose(parts_of).astype(BF16)
+                lhs2[h, d, :, 0 : 2 * tiles] = turned
+                lhs2[h, d, :, 2 * tiles : 4 * tiles] = turned
 
         edge = jnp.zeros((rows, LANES), F32)
         apad[top, row0:row1, 0:col0] = edge
@@ -333,80 +410,94 @@
 
         loads[4].wait()
         loads[5].wait()
-        i = (2 * RING - 1) * TR
-        frame = turned[:, i : i + 1].astype(jnp.int32)
-
-        def columns(c):
-            return slice(c * wide, (c + 1) * wide)
-
+        frame = columns_of[:, 2 * k_blocks : 2 * k_blocks + 1].astype(jnp.int32)
         for c in range(n_chunks):
             seen = jnp.zeros((tiles, wide), F32)
             for f in range(frames):
                 seen = jnp.where(frame == f, obs_v[f, :, columns(c)], seen)
-            mis[c, 0] = -seen
+            mis[c] = -seen
+
+        def weigh(c, d):
+            both = jnp.dot(
+                wcat[c % 2, d],
+                jnp.concatenate(two_parts(recv1[c, d].reshape(LANES, wide)), axis=0),
+                preferred_element_type=F32,
+            )
+            return both[0:tiles] + both[tiles : 2 * tiles]
 
         parts, spread = {}, {}
         for c in range(n_chunks):
             for d in range(1, RING):
                 i = c * RING + d
                 parts[c, d] = send(
-                    part.at[c, d], part_recv.at[c, d], p_ss.at[i], p_rs.at[i], camera_peer(c, -d)
+                    part.at[c, d],
+                    part_recv.at[c, d],
+                    p_ss.at[i],
+                    p_rs.at[i],
+                    dense_peer(c % 2, -d),
                 )
                 spread[c, d] = send(
-                    mis.at[c, 0], mis.at[c, d], m_ss.at[i], m_rs.at[i], camera_peer(c, d)
-                )
-        for f in range(2):
-            for c in range(n_chunks):
+                    mis.at[c], mis_recv.at[c, d], m_ss.at[i], m_rs.at[i], dense_peer(c % 2, d)
+                )
+        for c in range(n_chunks):
+            for f in range(2):
                 for d in range(1, RING):
                     slots1[c, f, d].wait_recv()
-                value = weigh(lhs1.at[c % 2, f], gat[c, f].reshape(ring, wide))
-                value = value.reshape(RING, tiles, wide)
-                if f == 0:
-                    part[c] = value
-                else:
-                    part[c] += value
-                    for d in FARTHEST_FIRST:
-                        parts[c, d].start()
+            for d in FARTHEST_FIRST:
+                part[c, d] = weigh(c, d)
+                parts[c, d].start()
+            mis[c] += weigh(c, 0)
 
         inner_layers(2)
 
-        mis_copies = []
         for c in range(n_chunks):
             for d in range(1, RING):
                 parts[c, d].wait_recv()
-            mis[c, 0] += (part[c, 0] + part_recv[c, 1]) + (part_recv[c, 2] + part_recv[c, 3])
+            mis[c] += part_recv[c, 1] + (part_recv[c, 2] + part_recv[c, 3])
             for d in FARTHEST_FIRST:
                 spread[c, d].start()
-            copy = pltpu.make_async_copy(
-                mis.at[c, 0], misfit_out.at[:, columns(c)], out_sem.at[4 + c]
-            )
-            copy.start()
-            mis_copies.append(copy)
+            misfit_out[:, columns(c)] = mis[c]
 
         inner_layers(3)
 
-        back = {}
-        for f in (1, 0):
-            for c in range(n_chunks):
-                if f == 1:
-                    for d in range(1, RING):
-                        spread[c, d].wait_recv()
-                value = weigh(lhs2.at[c % 2, f], mis[c].reshape(ring, wide))
-                con[c, f] = value.reshape(RING, tiles, wide)
-                for d in FARTHEST_FIRST:
+        slots2 = {}
+        for c in range(n_chunks):
+            for f in range(2):
+                for d in range(1, RING):
                     i = (c * 2 + f) * RING + d
-                    back[c, f, d] = send(
-                        con.at[c, f, d], con_recv.at[c, f, d], s2_ss.at[i], s2_rs.at[i], plate_peer(c, d)
+                    slots2[c, f, d] = send(
+                        send2.at[c, :, f, d],
+                        plane_rows(recv2, c, f, d),
+                        s2_ss.at[i],
+                        s2_rs.at[i],
+                        slot_peer(c % 2, d),
                     )
-                    back[c, f, d].start()
+        for c in range(n_chunks):
+            for d in range(RING):
+                if d:
+                    spread[c, d].wait_recv()
+                mh, ml = two_parts(mis_recv[c, d] if d else mis[c])
+                packed = jnp.dot(
+                    lhs2[c % 2, d],
+                    jnp.concatenate([mh, mh, ml, ml], axis=0),
+                    preferred_element_type=F32,
+                )
+                send2[c, d] = packed.reshape(2, RING, CAP, wide)
+            for d in FARTHEST_FIRST:
+                slots2[c, 1, d].start()
+        for c in range(n_chunks):
+            for d in FARTHEST_FIRST:
+                slots2[c, 0, d].start()
+        for c in range(n_chunks):
+            for f in range(2):
+                if c % 2 == 0:
+                    recv2[c, f, 0] = send2[c, :, f, 0]
+                else:
+                    recv2[c, f, :, 0] = send2[c, :, f, 0]
 
         for r in range(4, strips):
             inner_layers(r)
-        early = pltpu.make_async_copy(
-            outv.at[0 : top - 1], adj_out.at[0 : top - 1], out_sem.at[0]
-        )
-        early.start()
-        sent = rims0 + rims + w_copies + x_copies
+        sent = rims0 + rims + req_copies + w_copies + x_copies
         for group in (slots1, parts, spread):
             sent.extend(group.values())
         for copy in sent:
@@ -414,22 +505,26 @@
 
         def gathered(c, f):
             for d in range(1, RING):
-                back[c, f, d].wait_recv()
-            return (con[c, f, 0] + con_recv[c, f, 1]) + (con_recv[c, f, 2] + con_recv[c, f, 3])
+                slots2[c, f, d].wait_recv()
+            pick = onehot[:, f * half : (f + 1) * half].astype(BF16)
+            return jnp.dot(
+                jnp.concatenate([pick, pick], axis=1),
+                jnp.concatenate(two_parts(recv2[c, f].reshape(half, wide)), axis=0),
+                preferred_element_type=F32,
+            )
 
         xa_copies = []
         for c in range(n_chunks):
             xa_send[c] = gathered(c, 1)
-            i = n_chunks + c
-            copy = send(xa_send.at[c], xa_recv.at[c], x_ss.at[i], x_rs.at[i], partner)
+            copy = send(xa_send.at[c], xa_recv.at[c], x_ss.at[2 + c], x_rs.at[2 + c], partner)
             copy.start()
             xa_copies.append(copy)
-        for c in range(n_chunks):
-            near = gathered(c, 0)
-            xa_copies[c].wait_recv()
-            added = near + xa_recv[c]
-            for rr in range(wide // TC):
-                tiles3[:, c * (wide // TC) + rr, :] = added[:, rr * TC : (rr + 1) * TC]
+        sums = [gathered(c, 0) for c in range(n_chunks)]
+        for copy in xa_copies:
+            copy.wait_recv()
+        added = jnp.concatenate([sums[c] + xa_recv[c] for c in range(n_chunks)], axis=1)
+        for rr in range(TR):
+            tiles3[:, rr, :] = added[:, rr * TC : (rr + 1) * TC]
         for r in range(strips):
             strip = slice(r * TR, (r + 1) * TR)
             inner = slice(row0 + r * TR, row0 + (r + 1) * TR)
@@ -448,10 +543,6 @@
         rims2 = rim_copies(ns2_send, ns2_recv, ew2_send, ew2_recv, rim2_ss, rim2_rs)
         for copy in rims2:
             copy.start()
-        late = pltpu.make_async_copy(
-            outv.at[top - 1], adj_out.at[top - 1], out_sem.at[2]
-        )
-        late.start()
         for r in range(strips):
             strip = slice(r * TR, (r + 1) * TR)
             inner = slice(row0 + r * TR, row0 + (r + 1) * TR)
@@ -459,7 +550,7 @@
             under = apad[top - 1, inner, col0:col1]
             outv[top, strip] = value + RATE_VERTICAL * (under - ac)
             gradv[strip] = gin[strip] - (0.5 * RATE_PLANE) * total
-        for copy in list(back.values()) + xa_copies:
+        for copy in list(slots2.values()) + xa_copies:
             copy.wait_send()
 
         for copy in rims2:
@@ -484,16 +575,8 @@
             outv[top, :, at] += coef[face, :, at] * rim
             gradv[:, at] -= (0.5 * RATE_PLANE) * slope * rim
 
-        last_copies = [
-            pltpu.make_async_copy(outv.at[top], adj_out.at[top], out_sem.at[3]),
-            pltpu.make_async_copy(gradv, grad_out, out_sem.at[1]),
-        ]
-        for copy in last_copies:
-            copy.start()
         for copy in rims2:
             copy.wait_send()
-        for copy in [early, late] + mis_copies + last_copies:
-            copy.wait()
 
     dma = pltpu.SemaphoreType.DMA
 
@@ -512,28 +595,38 @@
         vmem(frames, tiles, tile),
         vmem(4, rows, cols),
         vmem(rows, cols),
-        vmem(layers, rows, cols),
-        vmem(rows, cols),
+        vmem(k_blocks, tiles, dtype=jnp.int32),
+        vmem(k_blocks, tiles),
+        vmem(1, tiles, dtype=jnp.int32),
         *pair(2, 2, cols),
         *pair(2, rows, LANES),
         *pair(2, 2 * layers, cols),
         *pair(2, rows, LANES),
         *pair(2, 1, cols),
         *pair(2, rows, LANES),
-        vmem(2 * RING, TR, LANES),
+        vmem(2 * TR, LANES),
+        vmem(groups, 8, LANES),
+        vmem(PLANE, 8, LANES),
         vmem(tiles, TR, TC),
-        vmem(2, ring, 2 * ring),
-        vmem(2, 2, 2 * ring, ring, dtype=BF16),
-        vmem(2, 2, 2 * ring, ring, dtype=BF16),
-        vmem(n_chunks, 2, RING, tiles, wide),
+        vmem(tiles, n_slots),
+        vmem(n_slots, 2 * tiles, dtype=BF16),
+        vmem(2 * tiles, tile, dtype=BF16),
+        *pair(2, RING, tiles, LANES),
+        vmem(2, RING, 2 * tiles, 4 * tiles, dtype=BF16),
+        vmem(2, RING, LANES, 4 * tiles, dtype=BF16),
+        *pair(2, tiles, tile // 2),
+        *pair(n_chunks, tiles, wide),
+        vmem(n_chunks, 2, RING, RING, CAP, wide),
+        vmem(n_chunks, RING, 2, RING, CAP, wide),
         *pair(n_chunks, RING, tiles, wide),
+        vmem(n_chunks, tiles, wide),
         vmem(n_chunks, RING, tiles, wide),
-        *pair(n_chunks, 2, RING, tiles, wide),
-        *pair(n_chunks, tiles, wide),
-        dma((6,)),
-        dma((4 + n_chunks,)),
+        vmem(n_chunks, RING, 2, RING, CAP, wide),
+        vmem(n_chunks, 2, RING, RING, CAP, wide),
+        dma((9,)),
         *[dma((4,)) for _ in range(6)],
-        dma((2 * n_chunks,)), dma((2 * n_chunks,)),
+        dma((2 + n_chunks,)), dma((2 + n_chunks,)),
+        dma((PLANE,)), dma((PLANE,)),
         dma((2 * RING,)), dma((2 * RING,)),
         dma((2 * n_chunks * RING,)), dma((2 * n_chunks * RING,)),
         dma((n_chunks * RING,)), dma((n_chunks * RING,)),
@@ -541,7 +634,6 @@
         dma((2 * n_chunks * RING,)), dma((2 * n_chunks * RING,)),
     ]
     in_hbm = pl.BlockSpec(memory_space=pltpu.HBM)
-    anywhere = pl.BlockSpec(memory_space=pl.ANY)
     in_vmem = pl.BlockSpec(memory_space=pltpu.VMEM)
     return pl.pallas_call(
         kernel,
@@ -550,13 +642,35 @@
             jax.ShapeDtypeStruct((layers, rows, cols), F32),
             jax.ShapeDtypeStruct((rows, cols), F32),
         ),
-        in_specs=[in_hbm] * 5 + [in_vmem] * 3,
-        out_specs=[anywhere] * 3,
+        in_specs=[in_hbm] * 8,
+        out_specs=[in_vmem] * 3,
         scratch_shapes=scratch,
         compiler_params=pltpu.CompilerParams(
             collective_id=0, has_side_effects=True, vmem_limit_bytes=48 * 1024 * 1024
         ),
     )
+
+
+def write_out(results):
+    count = len(results)
+
+    def kernel(*refs):
+        copies = [
+            pltpu.make_async_copy(refs[i], refs[count + i], refs[-1].at[i]) for i in range(count)
+        ]
+        for copy in copies:
+            copy.start()
+        for copy in copies:
+            copy.wait()
+
+    return pl.pallas_call(
+        kernel,
+        out_shape=tuple(jax.ShapeDtypeStruct(x.shape, x.dtype) for x in results),
+        in_specs=[pl.BlockSpec(memory_space=pltpu.VMEM)] * count,
+        out_specs=[pl.BlockSpec(memory_space=pl.ANY)] * count,
+        scratch_shapes=[pltpu.SemaphoreType.DMA((count,))],
+        compiler_params=pltpu.CompilerParams(vmem_limit_bytes=8 * 1024 * 1024),
+    )(*results)
 
 
 def solution(mesh):
@@ -568,7 +682,8 @@
         operands = (
             temp, cond, adj, grad, obs, frame_index[None, :], source_map.T, source_weight.T
         )
-        return call(*(pltpu.with_memory_space_constraint(x, pltpu.HBM) for x in operands))
+        results = call(*(pltpu.with_memory_space_constraint(x, pltpu.HBM) for x in operands))
+        return write_out(results)
 
     placed = (
         P(None, "gx", "gy"),

time: 71.7 us -> 67.3 us (0.939)
  local copies, waits for them, and re-layouts: 2.73 us -> 0 us
  Pallas kernels: 68.2 us -> 66.4 us
    pallas_call x1, Pallas kernels: 68.2 us -> 64.9 us  [local(): call(*(pltpu.with_memory_space_constraint(x, pltpu.HBM) for x in operands))]
    unnamed x3 -> x0, local copies, waits for them, and re-layouts: 2.73 us -> none
    pallas_call x0 -> x1, Pallas kernels: none -> 1.51 us  [write_out(): pl.pallas_call(kernel, out_shape=tuple((jax.ShapeDtypeStruct(x.shape, x.d...]
where the time goes in v4:
time: 67.3 us; the launch traced here: 67 us
  Pallas kernels  66.4 us (99%)
    pallas_call x1, Pallas kernels, local(): call(*(pltpu.with_memory_space_constraint(x, pltpu.HBM) for x in operands))  64.9 us
    pallas_call x1, Pallas kernels, write_out(): pl.pallas_call(kernel, out_shape=tuple((jax.ShapeDtypeStruct(x.shape, x.d...  1.51 us

profile of v4, /device:TPU:0, one launch (start us, length us, event | category | flops | bytes accessed | tf_op | source)
XLA Modules:
  0.0 67.0 jit_solution(5282774025098473435)
XLA Ops:
  0.6 64.9 %shard_map.103 = (f32[64,1024]{1,0:T(8,128)S(1)}, f32[8,64,1024]{2,1,0:T(8,128)S(1)}, f32[64,1024]{1,0:T(8,128)S(1)}) custom-call(f32[8,64,1024]{2,1,0:T(8,128)} %temp.1, f32[64,1024]{1,0:T(8,128)} %cond.1, f32[8,64,1024]{2,1,0:T(8,128)} %adj.1, f32[64,1024]{1,0:T(8,128)} %grad.1, f32[4,64,1024]{2,1,0:T(8,128)} %obs.1, s32[1,64]{1,0:T(1,128)} %bitcast.5, ...), custom_call_target="tpu_custom_call" | custom-call | tf_op jit(solution)/shard_map/pallas_call | solution.py:685
  65.5 1.5 %shard_map.104 = (f32[64,1024]{1,0:T(8,128)}, f32[8,64,1024]{2,1,0:T(8,128)}, f32[64,1024]{1,0:T(8,128)}) custom-call(f32[64,1024]{1,0:T(8,128)S(1)} %get-tuple-element.6.refs_0_, f32[8,64,1024]{2,1,0:T(8,128)S(1)} %get-tuple-element.7.refs_1_, f32[64,1024]{1,0:T(8,128)S(1)} %get-tuple-element.8.refs_2_), custom_call_target="tpu_custom_call" | custom-call | tf_op jit(solution)/shard_map/pallas_call | solution.py:666

commit v5 on v3

--- a/solution.py
+++ b/solution.py
@@ -41,17 +41,17 @@
     ring = RING * tiles
 
     def kernel(
-        temp, cond, adj, grad, obs, frame_ref, map_ref, weight_ref,
-        misfit_out, adj_out, grad_out,
-        tpad, apad, kpad, gin, obs_v, coef, gacc, outv, gradv,
+        temp, cond, adj, grad, obs, frame_in, map_in, weight_in,
+        misfit_out, outv, gradv,
+        tpad, apad, kpad, gin, obs_v, coef, gacc, map_v, weight_v, frame_v,
         ns0_send, ns0_recv, ew0_send, ew0_recv,
         ns_send, ns_recv, ew_send, ew_recv,
         ns2_send, ns2_recv, ew2_send, ew2_recv,
         small, tiles3, wfull, lhs1, lhs2,
-        gat, part, part_recv, mis, con, con_recv, xa_send, xa_recv,
-        in_sem, out_sem,
+        gat, part, part_recv, mis, con, con_recv, over_recv, xa_send, xa_recv,
+        in_sem,
         rim0_ss, rim0_rs, rim_ss, rim_rs, rim2_ss, rim2_rs, x_ss, x_rs,
-        w_ss, w_rs, s1_ss, s1_rs, p_ss, p_rs, m_ss, m_rs, s2_ss, s2_rs,
+        w_ss, w_rs, s1_ss, s1_rs, p_ss, p_rs, m_ss, m_rs, s2_ss, s2_rs, o_ss, o_rs,
     ):
         gx = lax.axis_index("gx")
         gy = lax.axis_index("gy")
@@ -83,12 +83,6 @@
                 device_id=device,
                 device_id_type=MESH,
             )
-
-        barrier = pltpu.get_barrier_semaphore()
-        greeted = [along(d, 0) for d in range(1, RING)] + [along(0, d) for d in range(1, RING)]
-        greeted += [partner] + list(sides)
-        for device in greeted:
-            pl.semaphore_signal(barrier, inc=1, device_id=device, device_id_type=MESH)
 
         body_at = (slice(row0, row1), slice(col0, col1))
         loads = [
@@ -104,8 +98,20 @@
             pltpu.make_async_copy(adj, apad.at[(slice(None), *body_at)], in_sem.at[3]),
             pltpu.make_async_copy(grad, gin, in_sem.at[4]),
             pltpu.make_async_copy(obs, obs_v, in_sem.at[5]),
+            pltpu.make_async_copy(map_in, map_v, in_sem.at[6]),
+            pltpu.make_async_copy(weight_in, weight_v, in_sem.at[7]),
+            pltpu.make_async_copy(frame_in, frame_v, in_sem.at[8]),
         ]
-        for load in loads:
+        for load in loads[:2]:
+            load.start()
+
+        barrier = pltpu.get_barrier_semaphore()
+        greeted = [along(d, 0) for d in range(1, RING)] + [along(0, d) for d in range(1, RING)]
+        greeted += [partner] + list(sides)
+        for device in greeted:
+            pl.semaphore_signal(barrier, inc=1, device_id=device, device_id_type=MESH)
+
+        for load in loads[6:] + loads[2:6]:
             load.start()
 
         for load in loads[:2]:
@@ -122,9 +128,11 @@
                 kpad[row0:row1, col : col + 1],
             )
 
-        small[0, 0:k_blocks, 0:tiles] = map_ref[...].astype(F32)
-        small[0, k_blocks : 2 * k_blocks, 0:tiles] = weight_ref[...]
-        small[2 * RING - 1, 0:1, 0:tiles] = frame_ref[...].astype(F32)
+        for load in loads[6:]:
+            load.wait()
+        small[0, 0:k_blocks, 0:tiles] = map_v[...].astype(F32)
+        small[0, k_blocks : 2 * k_blocks, 0:tiles] = weight_v[...]
+        small[2 * RING - 1, 0:1, 0:tiles] = frame_v[...].astype(F32)
 
         pl.semaphore_wait(barrier, len(greeted))
 
@@ -210,20 +218,26 @@
             x_copies.append(
                 send(gat.at[c, 0, 0], gat.at[c, 1, 0], x_ss.at[c], x_rs.at[c], partner)
             )
-            for f in range(2):
-                for d in range(1, RING):
-                    i = (c * 2 + f) * RING + d
-                    slots1[c, f, d] = send(
-                        gat.at[c, f, 0], gat.at[c, f, d], s1_ss.at[i], s1_rs.at[i], plate_peer(c, -d)
-                    )
+            for f, d in ((0, 2), (0, 1), (0, 3), (1, 1), (1, 3)):
+                i = (c * 2 + f) * RING + d
+                slots1[c, f, d] = send(
+                    gat.at[c, f, 0], gat.at[c, f, d], s1_ss.at[i], s1_rs.at[i], plate_peer(c, -d)
+                )
             x_copies[c].start()
             for d in FARTHEST_FIRST:
                 slots1[c, 0, d].start()
 
+        over1 = [
+            send(gat.at[c, 0, 2], gat.at[c, 1, 2], o_ss.at[c], o_rs.at[c], partner)
+            for c in range(n_chunks)
+        ]
+
         def pass_far(c):
             x_copies[c].wait_recv()
-            for d in FARTHEST_FIRST:
+            for d in (1, 3):
                 slots1[c, 1, d].start()
+            slots1[c, 0, 2].wait_recv()
+            over1[c].start()
 
         for load in loads[2:4]:
             load.wait()
@@ -357,8 +371,10 @@
                 )
         for f in range(2):
             for c in range(n_chunks):
-                for d in range(1, RING):
+                for d in (1, 3):
                     slots1[c, f, d].wait_recv()
+                if f == 1:
+                    over1[c].wait_recv()
                 value = weigh(lhs1.at[c % 2, f], gat[c, f].reshape(ring, wide))
                 value = value.reshape(RING, tiles, wide)
                 if f == 0:
@@ -370,22 +386,27 @@
 
         inner_layers(2)
 
-        mis_copies = []
         for c in range(n_chunks):
             for d in range(1, RING):
                 parts[c, d].wait_recv()
             mis[c, 0] += (part[c, 0] + part_recv[c, 1]) + (part_recv[c, 2] + part_recv[c, 3])
             for d in FARTHEST_FIRST:
                 spread[c, d].start()
-            copy = pltpu.make_async_copy(
-                mis.at[c, 0], misfit_out.at[:, columns(c)], out_sem.at[4 + c]
+            misfit_out[:, columns(c)] = mis[c, 0]
+
+        inner_layers(3)
+
+        back = {}
+        over2 = [
+            send(
+                con.at[c, 1, 2],
+                over_recv.at[c],
+                o_ss.at[n_chunks + c],
+                o_rs.at[n_chunks + c],
+                partner,
             )
-            copy.start()
-            mis_copies.append(copy)
-
-        inner_layers(3)
-
-        back = {}
+            for c in range(n_chunks)
+        ]
         for f in (1, 0):
             for c in range(n_chunks):
                 if f == 1:
@@ -393,8 +414,14 @@
                         spread[c, d].wait_recv()
                 value = weigh(lhs2.at[c % 2, f], mis[c].reshape(ring, wide))
                 con[c, f] = value.reshape(RING, tiles, wide)
-                for d in FARTHEST_FIRST:
+                for d in (1, 3, 2):
                     i = (c * 2 + f) * RING + d
+                    if f == 1 and d == 2:
+                        over2[c].start()
+                        continue
+                    if d == 2:
+                        over2[c].wait_recv()
+                        con[c, 0, 2] += over_recv[c]
                     back[c, f, d] = send(
                         con.at[c, f, d], con_recv.at[c, f, d], s2_ss.at[i], s2_rs.at[i], plate_peer(c, d)
                     )
@@ -402,20 +429,20 @@
 
         for r in range(4, strips):
             inner_layers(r)
-        early = pltpu.make_async_copy(
-            outv.at[0 : top - 1], adj_out.at[0 : top - 1], out_sem.at[0]
-        )
-        early.start()
-        sent = rims0 + rims + w_copies + x_copies
+        sent = rims0 + rims + w_copies + x_copies + over1
         for group in (slots1, parts, spread):
             sent.extend(group.values())
         for copy in sent:
             copy.wait_send()
 
         def gathered(c, f):
-            for d in range(1, RING):
+            for d in (1, 3):
                 back[c, f, d].wait_recv()
-            return (con[c, f, 0] + con_recv[c, f, 1]) + (con_recv[c, f, 2] + con_recv[c, f, 3])
+            total = con[c, f, 0] + (con_recv[c, f, 1] + con_recv[c, f, 3])
+            if f == 0:
+                back[c, f, 2].wait_recv()
+                total = total + con_recv[c, f, 2]
+            return total
 
         xa_copies = []
         for c in range(n_chunks):
@@ -448,10 +475,6 @@
         rims2 = rim_copies(ns2_send, ns2_recv, ew2_send, ew2_recv, rim2_ss, rim2_rs)
         for copy in rims2:
             copy.start()
-        late = pltpu.make_async_copy(
-            outv.at[top - 1], adj_out.at[top - 1], out_sem.at[2]
-        )
-        late.start()
         for r in range(strips):
             strip = slice(r * TR, (r + 1) * TR)
             inner = slice(row0 + r * TR, row0 + (r + 1) * TR)
@@ -459,7 +482,7 @@
             under = apad[top - 1, inner, col0:col1]
             outv[top, strip] = value + RATE_VERTICAL * (under - ac)
             gradv[strip] = gin[strip] - (0.5 * RATE_PLANE) * total
-        for copy in list(back.values()) + xa_copies:
+        for copy in list(back.values()) + over2 + xa_copies:
             copy.wait_send()
 
         for copy in rims2:
@@ -484,16 +507,8 @@
             outv[top, :, at] += coef[face, :, at] * rim
             gradv[:, at] -= (0.5 * RATE_PLANE) * slope * rim
 
-        last_copies = [
-            pltpu.make_async_copy(outv.at[top], adj_out.at[top], out_sem.at[3]),
-            pltpu.make_async_copy(gradv, grad_out, out_sem.at[1]),
-        ]
-        for copy in last_copies:
-            copy.start()
         for copy in rims2:
             copy.wait_send()
-        for copy in [early, late] + mis_copies + last_copies:
-            copy.wait()
 
     dma = pltpu.SemaphoreType.DMA
 
@@ -512,8 +527,9 @@
         vmem(frames, tiles, tile),
         vmem(4, rows, cols),
         vmem(rows, cols),
-        vmem(layers, rows, cols),
-        vmem(rows, cols),
+        vmem(k_blocks, tiles, dtype=jnp.int32),
+        vmem(k_blocks, tiles),
+        vmem(1, tiles, dtype=jnp.int32),
         *pair(2, 2, cols),
         *pair(2, rows, LANES),
         *pair(2, 2 * layers, cols),
@@ -529,9 +545,9 @@
         *pair(n_chunks, RING, tiles, wide),
         vmem(n_chunks, RING, tiles, wide),
         *pair(n_chunks, 2, RING, tiles, wide),
+        vmem(n_chunks, tiles, wide),
         *pair(n_chunks, tiles, wide),
-        dma((6,)),
-        dma((4 + n_chunks,)),
+        dma((9,)),
         *[dma((4,)) for _ in range(6)],
         dma((2 * n_chunks,)), dma((2 * n_chunks,)),
         dma((2 * RING,)), dma((2 * RING,)),
@@ -539,9 +555,9 @@
         dma((n_chunks * RING,)), dma((n_chunks * RING,)),
         dma((n_chunks * RING,)), dma((n_chunks * RING,)),
         dma((2 * n_chunks * RING,)), dma((2 * n_chunks * RING,)),
+        dma((2 * n_chunks,)), dma((2 * n_chunks,)),
     ]
     in_hbm = pl.BlockSpec(memory_space=pltpu.HBM)
-    anywhere = pl.BlockSpec(memory_space=pl.ANY)
     in_vmem = pl.BlockSpec(memory_space=pltpu.VMEM)
     return pl.pallas_call(
         kernel,
@@ -550,13 +566,35 @@
             jax.ShapeDtypeStruct((layers, rows, cols), F32),
             jax.ShapeDtypeStruct((rows, cols), F32),
         ),
-        in_specs=[in_hbm] * 5 + [in_vmem] * 3,
-        out_specs=[anywhere] * 3,
+        in_specs=[in_hbm] * 8,
+        out_specs=[in_vmem] * 3,
         scratch_shapes=scratch,
         compiler_params=pltpu.CompilerParams(
             collective_id=0, has_side_effects=True, vmem_limit_bytes=48 * 1024 * 1024
         ),
     )
+
+
+def write_out(results):
+    count = len(results)
+
+    def kernel(*refs):
+        copies = [
+            pltpu.make_async_copy(refs[i], refs[count + i], refs[-1].at[i]) for i in range(count)
+        ]
+        for copy in copies:
+            copy.start()
+        for copy in copies:
+            copy.wait()
+
+    return pl.pallas_call(
+        kernel,
+        out_shape=tuple(jax.ShapeDtypeStruct(x.shape, x.dtype) for x in results),
+        in_specs=[pl.BlockSpec(memory_space=pltpu.VMEM)] * count,
+        out_specs=[pl.BlockSpec(memory_space=pl.ANY)] * count,
+        scratch_shapes=[pltpu.SemaphoreType.DMA((count,))],
+        compiler_params=pltpu.CompilerParams(vmem_limit_bytes=8 * 1024 * 1024),
+    )(*results)
 
 
 def solution(mesh):
@@ -568,7 +606,8 @@
         operands = (
             temp, cond, adj, grad, obs, frame_index[None, :], source_map.T, source_weight.T
         )
-        return call(*(pltpu.with_memory_space_constraint(x, pltpu.HBM) for x in operands))
+        results = call(*(pltpu.with_memory_space_constraint(x, pltpu.HBM) for x in operands))
+        return write_out(results)
 
     placed = (
         P(None, "gx", "gy"),

time: 71.7 us -> 73.9 us (1.031)
  Pallas kernels: 68.2 us -> 73.2 us
  local copies, waits for them, and re-layouts: 2.73 us -> 0 us
    pallas_call x1, Pallas kernels: 68.2 us -> 71.7 us  [local(): call(*(pltpu.with_memory_space_constraint(x, pltpu.HBM) for x in operands))]
    unnamed x3 -> x0, local copies, waits for them, and re-layouts: 2.73 us -> none
    pallas_call x0 -> x1, Pallas kernels: none -> 1.51 us  [write_out(): pl.pallas_call(kernel, out_shape=tuple((jax.ShapeDtypeStruct(x.shape, x.d...]
where the time goes in v5:
time: 73.9 us; the launch traced here: 73.8 us
  Pallas kernels  73.2 us (99%)
    pallas_call x1, Pallas kernels, local(): call(*(pltpu.with_memory_space_constraint(x, pltpu.HBM) for x in operands))  71.7 us
    pallas_call x1, Pallas kernels, write_out(): pl.pallas_call(kernel, out_shape=tuple((jax.ShapeDtypeStruct(x.shape, x.d...  1.51 us

profile of v5, /device:TPU:0, one launch (start us, length us, event | category | flops | bytes accessed | tf_op | source)
XLA Modules:
  0.0 73.8 jit_solution(2513675023225568280)
XLA Ops:
  0.6 71.7 %shard_map.103 = (f32[64,1024]{1,0:T(8,128)S(1)}, f32[8,64,1024]{2,1,0:T(8,128)S(1)}, f32[64,1024]{1,0:T(8,128)S(1)}) custom-call(f32[8,64,1024]{2,1,0:T(8,128)} %temp.1, f32[64,1024]{1,0:T(8,128)} %cond.1, f32[8,64,1024]{2,1,0:T(8,128)} %adj.1, f32[64,1024]{1,0:T(8,128)} %grad.1, f32[4,64,1024]{2,1,0:T(8,128)} %obs.1, s32[1,64]{1,0:T(1,128)} %bitcast.5, ...), custom_call_target="tpu_custom_call" | custom-call | tf_op jit(solution)/shard_map/pallas_call | solution.py:609
  72.3 1.5 %shard_map.104 = (f32[64,1024]{1,0:T(8,128)}, f32[8,64,1024]{2,1,0:T(8,128)}, f32[64,1024]{1,0:T(8,128)}) custom-call(f32[64,1024]{1,0:T(8,128)S(1)} %get-tuple-element.6.refs_0_, f32[8,64,1024]{2,1,0:T(8,128)S(1)} %get-tuple-element.7.refs_1_, f32[64,1024]{1,0:T(8,128)S(1)} %get-tuple-element.8.refs_2_), custom_call_target="tpu_custom_call" | custom-call | tf_op jit(solution)/shard_map/pallas_call | solution.py:590

commit v6 on v4

--- a/solution.py
+++ b/solution.py
@@ -35,8 +35,7 @@
     tiles = (rows // TR) * (cols // TC)
     half = PLANE * CAP
     n_slots = 2 * half
-    row0, col0 = TR, LANES
-    row1, col1 = row0 + rows, col0 + cols
+    row0, row1 = TR, TR + rows
     strips = rows // TR
     tile_cols = cols // TC
     top = layers - 1
@@ -92,25 +91,33 @@
                 device_id_type=MESH,
             )
 
-        body_at = (slice(row0, row1), slice(col0, col1))
-        loads = [
-            pltpu.make_async_copy(
-                temp.at[top - 1 : layers],
-                tpad.at[(slice(top - 1, layers), *body_at)],
-                in_sem.at[0],
-            ),
-            pltpu.make_async_copy(cond, kpad.at[body_at], in_sem.at[1]),
-            pltpu.make_async_copy(
-                temp.at[0 : top - 1], tpad.at[(slice(0, top - 1), *body_at)], in_sem.at[2]
-            ),
-            pltpu.make_async_copy(adj, apad.at[(slice(None), *body_at)], in_sem.at[3]),
+        def block_loads(src, src_layers, pad, pad_layers, sem):
+            return [
+                pltpu.make_async_copy(
+                    src.at[(*src_layers, slice(None), slice(u * TC, (u + 1) * TC))],
+                    pad.at[(*pad_layers, u + 1, slice(row0, row1))],
+                    in_sem.at[sem + u],
+                )
+                for u in range(tile_cols)
+            ]
+
+        both = (slice(top - 1, layers),)
+        rest = (slice(0, top - 1),)
+        all_layers = (slice(0, layers),)
+        first_loads = block_loads(temp, both, tpad, both, 9) + block_loads(
+            cond, (), kpad, (), 9 + tile_cols
+        )
+        rim_loads = block_loads(temp, rest, tpad, rest, 9 + 2 * tile_cols) + block_loads(
+            adj, all_layers, apad, all_layers, 9 + 3 * tile_cols
+        )
+        loads = [None] * 4 + [
             pltpu.make_async_copy(grad, gin, in_sem.at[4]),
             pltpu.make_async_copy(obs, obs_v, in_sem.at[5]),
             pltpu.make_async_copy(map_in, map_v, in_sem.at[6]),
             pltpu.make_async_copy(weight_in, weight_v, in_sem.at[7]),
             pltpu.make_async_copy(frame_in, frame_v, in_sem.at[8]),
         ]
-        for load in loads[:2]:
+        for load in first_loads:
             load.start()
 
         barrier = pltpu.get_barrier_semaphore()
@@ -118,21 +125,33 @@
         for device in greeted:
             pl.semaphore_signal(barrier, inc=1, device_id=device, device_id_type=MESH)
 
-        for load in loads[6:] + loads[2:6]:
+        for load in loads[6:] + rim_loads + loads[4:6]:
             load.start()
 
-        for load in loads[:2]:
+        for load in first_loads:
             load.wait()
         first, last = row0, row1 - 1
+
+        def across(pad, index, at):
+            return jnp.concatenate(
+                [pad[(*index, u, at, slice(None))] for u in range(1, tile_cols + 1)], axis=-1
+            )
+
+        def put_line(pad, index, at, value):
+            for u in range(tile_cols):
+                pad[(*index, u + 1, at, slice(None))] = value[..., u * TC : (u + 1) * TC]
+
+        def edge_column(pad, index, side):
+            u, at = ((1, 0), (tile_cols, TC - 1))[side]
+            return pad[(*index, u, slice(row0, row1), slice(at, at + 1))]
+
         rim_lane = iota((rows, LANES), 1)
         for side, row in ((0, first), (1, last)):
-            ns0_send[side, 0:1] = tpad[top, row : row + 1, col0:col1]
-            ns0_send[side, 1:2] = kpad[row : row + 1, col0:col1]
-        for side, col in ((0, col0), (1, col1 - 1)):
+            ns0_send[side, 0:1] = across(tpad, (top,), slice(row, row + 1))
+            ns0_send[side, 1:2] = across(kpad, (), slice(row, row + 1))
+        for side in range(2):
             ew0_send[side] = jnp.where(
-                rim_lane == 0,
-                tpad[top, row0:row1, col : col + 1],
-                kpad[row0:row1, col : col + 1],
+                rim_lane == 0, edge_column(tpad, (top,), side), edge_column(kpad, (), side)
             )
 
         pl.semaphore_wait(barrier, len(greeted))
@@ -173,9 +192,9 @@
         wish = ((code & (tiles - 1)) + 1).astype(F32)
         lane = iota((tiles, LANES), 1)
         lane_slot = iota((tiles, n_slots), 1)
-        below = jnp.where(iota((tiles, tiles), 0) > iota((tiles, tiles), 1), 1.0, 0.0)
+        lower = jnp.where(iota((tiles, tiles), 0) > iota((tiles, tiles), 1), 1.0, 0.0)
         hits = [jnp.where(block[:, k : k + 1] == lane, 1.0, 0.0) for k in range(k_blocks)]
-        before = jnp.dot(below, jnp.concatenate(hits, axis=1), preferred_element_type=F32)
+        before = jnp.dot(lower, jnp.concatenate(hits, axis=1), preferred_element_type=F32)
         base = jnp.zeros((1, LANES), F32)
         wanted = jnp.zeros((tiles, n_slots), F32)
         weights = [jnp.zeros((tiles, n_slots), F32) for _ in range(2)]
@@ -227,29 +246,41 @@
         has_east = jnp.where(gy < n_gy - 1, 1.0, 0.0)
 
         def column_rims(pad, index, source, lane_at):
-            for side, has, at in ((0, has_west, 0), (1, has_east, col1)):
+            for side, has, at in ((0, has_west, 0), (1, has_east, tile_cols + 1)):
                 value = source[side, :, lane_at : lane_at + 1] * has
-                pad[(*index, slice(row0, row1), slice(at, at + LANES))] = jnp.broadcast_to(
-                    value, (rows, LANES)
-                )
+                pad[(*index, at, slice(row0, row1))] = jnp.broadcast_to(value, (rows, LANES))
 
         for copy in rims0:
             copy.wait_recv()
-        kpad[first - 1 : first, col0:col1] = ns0_recv[0, 1:2] * has_north
-        kpad[last + 1 : last + 2, col0:col1] = ns0_recv[1, 1:2] * has_south
+        above, below = slice(first - 1, first), slice(last + 1, last + 2)
+        put_line(kpad, (), above, ns0_recv[0, 1:2] * has_north)
+        put_line(kpad, (), below, ns0_recv[1, 1:2] * has_south)
         column_rims(kpad, (), ew0_recv, 1)
-        tpad[top, first - 1 : first, col0:col1] = ns0_recv[0, 0:1] * has_north
-        tpad[top, last + 1 : last + 2, col0:col1] = ns0_recv[1, 0:1] * has_south
+        put_line(tpad, (top,), above, ns0_recv[0, 0:1] * has_north)
+        put_line(tpad, (top,), below, ns0_recv[1, 0:1] * has_south)
         column_rims(tpad, (top,), ew0_recv, 0)
+
+        strip_lane = iota((TR, TC), 1)
 
         def around(pad, index, r):
             a, b = row0 + r * TR, row0 + (r + 1) * TR
+            blocks = [pad[(*index, u, slice(a, b), slice(None))] for u in range(tile_cols + 2)]
+            inside = blocks[1:-1]
+            eastward = [pltpu.roll(x, TC - 1, 1) for x in inside] + blocks[-1:]
+            westward = blocks[:1] + [pltpu.roll(x, 1, 1) for x in inside]
+            e = [
+                jnp.where(strip_lane == TC - 1, eastward[u + 1], eastward[u])
+                for u in range(tile_cols)
+            ]
+            w = [
+                jnp.where(strip_lane == 0, westward[u], westward[u + 1]) for u in range(tile_cols)
+            ]
             return (
-                pad[(*index, slice(a, b), slice(col0, col1))],
-                pad[(*index, slice(a, b), slice(col0 + 1, col1 + 1))],
-                pad[(*index, slice(a, b), slice(col0 - 1, col1 - 1))],
-                pad[(*index, slice(a - 1, b - 1), slice(col0, col1))],
-                pad[(*index, slice(a + 1, b + 1), slice(col0, col1))],
+                jnp.concatenate(inside, axis=1),
+                jnp.concatenate(e, axis=1),
+                jnp.concatenate(w, axis=1),
+                across(pad, index, slice(a - 1, b - 1)),
+                across(pad, index, slice(a + 1, b + 1)),
             )
 
         for r in range(strips):
@@ -259,7 +290,7 @@
             for i in range(4):
                 coef[i, strip] = faces[i]
             tc, te, tw, tn, ts = around(tpad, (top,), r)
-            under = tpad[top - 1, row0 + r * TR : row0 + (r + 1) * TR, col0:col1]
+            under = across(tpad, (top - 1,), slice(row0 + r * TR, row0 + (r + 1) * TR))
             value = tc + RATE_VERTICAL * (under - tc)
             for face, other in zip(faces, (te, tw, tn, ts)):
                 value = value + face * (other - tc)
@@ -328,17 +359,19 @@
         for pair in (0, 2):
             pack_tiles(0, pair, x_send[pair // 2])
 
-        for load in loads[2:4]:
+        for load in rim_loads:
             load.wait()
         for side, row in ((0, first), (1, last)):
-            ns_send[side, 0:top] = tpad[0:top, row, col0:col1]
-            ns_send[side, layers : layers + top] = apad[0:top, row, col0:col1]
-        for side, col in ((0, col0), (1, col1 - 1)):
+            for u in range(tile_cols):
+                at = slice(u * TC, (u + 1) * TC)
+                ns_send[side, 0:top, at] = tpad[0:top, u + 1, row, :]
+                ns_send[side, layers : layers + top, at] = apad[0:top, u + 1, row, :]
+        for side in range(2):
             packed = jnp.zeros((rows, LANES), F32)
             for l in range(top):
-                packed = jnp.where(rim_lane == l, tpad[l, row0:row1, col : col + 1], packed)
+                packed = jnp.where(rim_lane == l, edge_column(tpad, (l,), side), packed)
                 packed = jnp.where(
-                    rim_lane == layers + l, apad[l, row0:row1, col : col + 1], packed
+                    rim_lane == layers + l, edge_column(apad, (l,), side), packed
                 )
             ew_send[side] = packed
         rims = rim_copies(ns_send, ns_recv, ew_send, ew_recv, rim_ss, rim_rs)
@@ -366,20 +399,21 @@
                 lhs2[h, d, :, 2 * tiles : 4 * tiles] = turned
 
         edge = jnp.zeros((rows, LANES), F32)
-        apad[top, row0:row1, 0:col0] = edge
-        apad[top, row0:row1, col1 : col1 + LANES] = edge
-        apad[top, first - 1 : first, col0:col1] = jnp.zeros((1, cols), F32)
-        apad[top, last + 1 : last + 2, col0:col1] = jnp.zeros((1, cols), F32)
+        apad[top, 0, row0:row1] = edge
+        apad[top, tile_cols + 1, row0:row1] = edge
+        put_line(apad, (top,), above, jnp.zeros((1, cols), F32))
+        put_line(apad, (top,), below, jnp.zeros((1, cols), F32))
 
         for copy in rims:
             copy.wait_recv()
         for l in range(top):
             column_rims(tpad, (l,), ew_recv, l)
             column_rims(apad, (l,), ew_recv, layers + l)
-        tpad[0:top, first - 1, col0:col1] = ns_recv[0, 0:top] * has_north
-        tpad[0:top, last + 1, col0:col1] = ns_recv[1, 0:top] * has_south
-        apad[0:top, first - 1, col0:col1] = ns_recv[0, layers : layers + top] * has_north
-        apad[0:top, last + 1, col0:col1] = ns_recv[1, layers : layers + top] * has_south
+        for side, has, at in ((0, has_north, first - 1), (1, has_south, last + 1)):
+            for u in range(tile_cols):
+                cut = slice(u * TC, (u + 1) * TC)
+                tpad[0:top, u + 1, at, :] = ns_recv[side, 0:top, cut] * has
+                apad[0:top, u + 1, at, :] = ns_recv[side, layers : layers + top, cut] * has
 
         def layer_step(l, r, total):
             strip = slice(r * TR, (r + 1) * TR)
@@ -398,9 +432,9 @@
 
             def body(l, total):
                 value, ac, total = layer_step(l, r, total)
-                above = apad[l + 1, inner, col0:col1]
-                under = apad[jnp.maximum(l - 1, 0), inner, col0:col1]
-                outv[l, strip] = value + RATE_VERTICAL * ((above - ac) + (under - ac))
+                over = across(apad, (l + 1,), inner)
+                under = across(apad, (jnp.maximum(l - 1, 0),), inner)
+                outv[l, strip] = value + RATE_VERTICAL * ((over - ac) + (under - ac))
                 return total
 
             gacc[strip] = lax.fori_loop(0, top, body, jnp.zeros((TR, cols), F32))
@@ -531,15 +565,13 @@
             extra = jnp.concatenate(
                 [tiles3[r * tile_cols + u] for u in range(tile_cols)], axis=1
             )
-            apad[top, inner, col0:col1] += extra
+            put_line(apad, (top,), inner, across(apad, (top,), inner) + extra)
             outv[top - 1, strip] += RATE_VERTICAL * extra
 
         for side, row in ((0, first), (1, last)):
-            ns2_send[side] = apad[top, row : row + 1, col0:col1]
-        for side, col in ((0, col0), (1, col1 - 1)):
-            ew2_send[side] = jnp.broadcast_to(
-                apad[top, row0:row1, col : col + 1], (rows, LANES)
-            )
+            ns2_send[side] = across(apad, (top,), slice(row, row + 1))
+        for side in range(2):
+            ew2_send[side] = jnp.broadcast_to(edge_column(apad, (top,), side), (rows, LANES))
         rims2 = rim_copies(ns2_send, ns2_recv, ew2_send, ew2_recv, rim2_ss, rim2_rs)
         for copy in rims2:
             copy.start()
@@ -547,7 +579,7 @@
             strip = slice(r * TR, (r + 1) * TR)
             inner = slice(row0 + r * TR, row0 + (r + 1) * TR)
             value, ac, total = layer_step(top, r, gacc[strip])
-            under = apad[top - 1, inner, col0:col1]
+            under = across(apad, (top - 1,), inner)
             outv[top, strip] = value + RATE_VERTICAL * (under - ac)
             gradv[strip] = gin[strip] - (0.5 * RATE_PLANE) * total
         for copy in list(slots2.values()) + xa_copies:
@@ -558,20 +590,18 @@
         for side, has, row, beyond in ((0, has_north, 0, first - 1), (1, has_south, rows - 1, last + 1)):
             at = slice(row, row + 1)
             rim = ns2_recv[side] * has
-            slope = tpad[top, beyond : beyond + 1, col0:col1] - tpad[
-                top, row0 + row : row0 + row + 1, col0:col1
-            ]
+            slope = across(tpad, (top,), slice(beyond, beyond + 1)) - across(
+                tpad, (top,), slice(row0 + row, row0 + row + 1)
+            )
             outv[top, at] += coef[2 + side, at] * rim
             gradv[at] -= (0.5 * RATE_PLANE) * slope * rim
-        for side, has, face, at, beyond, edge_lane in (
-            (0, has_west, 1, 0, 0, 0),
-            (1, has_east, 0, cols - LANES, col1, LANES - 1),
+        for side, has, face, inside, beyond, edge_lane in (
+            (0, has_west, 1, 1, 0, 0),
+            (1, has_east, 0, tile_cols, tile_cols + 1, TC - 1),
         ):
-            at = slice(at, at + LANES)
+            at = slice((inside - 1) * TC, inside * TC)
             rim = jnp.where(rim_lane == edge_lane, ew2_recv[side] * has, 0.0)
-            slope = tpad[top, row0:row1, beyond : beyond + LANES] - tpad[
-                top, row0:row1, col0 + at.start : col0 + at.stop
-            ]
+            slope = tpad[top, beyond, row0:row1] - tpad[top, inside, row0:row1]
             outv[top, :, at] += coef[face, :, at] * rim
             gradv[:, at] -= (0.5 * RATE_PLANE) * slope * rim
 
@@ -588,9 +618,9 @@
 
     tile = TR * TC
     scratch = [
-        vmem(layers, rows + 2 * TR, cols + 2 * LANES),
-        vmem(layers, rows + 2 * TR, cols + 2 * LANES),
-        vmem(rows + 2 * TR, cols + 2 * LANES),
+        vmem(layers, tile_cols + 2, rows + 2 * TR, TC),
+        vmem(layers, tile_cols + 2, rows + 2 * TR, TC),
+        vmem(tile_cols + 2, rows + 2 * TR, TC),
         vmem(rows, cols),
         vmem(frames, tiles, tile),
         vmem(4, rows, cols),
@@ -623,7 +653,7 @@
         vmem(n_chunks, RING, tiles, wide),
         vmem(n_chunks, RING, 2, RING, CAP, wide),
         vmem(n_chunks, 2, RING, RING, CAP, wide),
-        dma((9,)),
+        dma((9 + 4 * tile_cols,)),
         *[dma((4,)) for _ in range(6)],
         dma((2 + n_chunks,)), dma((2 + n_chunks,)),
         dma((PLANE,)), dma((PLANE,)),

time: 67.3 us -> 65.2 us (0.969)
  Pallas kernels: 66.4 us -> 64.4 us
    pallas_call x1, Pallas kernels: 64.9 us -> 62.9 us  [local(): call(*(pltpu.with_memory_space_constraint(x, pltpu.HBM) for x in operands))]
where the time goes in v6:
time: 65.2 us; the launch traced here: 65 us
  Pallas kernels  64.4 us (99%)
    pallas_call x1, Pallas kernels, local(): call(*(pltpu.with_memory_space_constraint(x, pltpu.HBM) for x in operands))  62.9 us
    pallas_call x1, Pallas kernels, write_out(): pl.pallas_call(kernel, out_shape=tuple((jax.ShapeDtypeStruct(x.shape, x.d...  1.51 us

profile of v6, /device:TPU:0, one launch (start us, length us, event | category | flops | bytes accessed | tf_op | source)
XLA Modules:
  0.0 65.0 jit_solution(13709967336153015944)
XLA Ops:
  0.6 62.9 %shard_map.103 = (f32[64,1024]{1,0:T(8,128)S(1)}, f32[8,64,1024]{2,1,0:T(8,128)S(1)}, f32[64,1024]{1,0:T(8,128)S(1)}) custom-call(f32[8,64,1024]{2,1,0:T(8,128)} %temp.1, f32[64,1024]{1,0:T(8,128)} %cond.1, f32[8,64,1024]{2,1,0:T(8,128)} %adj.1, f32[64,1024]{1,0:T(8,128)} %grad.1, f32[4,64,1024]{2,1,0:T(8,128)} %obs.1, s32[1,64]{1,0:T(1,128)} %bitcast.5, ...), custom_call_target="tpu_custom_call" | custom-call | tf_op jit(solution)/shard_map/pallas_call | solution.py:715
  63.5 1.5 %shard_map.104 = (f32[64,1024]{1,0:T(8,128)}, f32[8,64,1024]{2,1,0:T(8,128)}, f32[64,1024]{1,0:T(8,128)}) custom-call(f32[64,1024]{1,0:T(8,128)S(1)} %get-tuple-element.6.refs_0_, f32[8,64,1024]{2,1,0:T(8,128)S(1)} %get-tuple-element.7.refs_1_, f32[64,1024]{1,0:T(8,128)S(1)} %get-tuple-element.8.refs_2_), custom_call_target="tpu_custom_call" | custom-call | tf_op jit(solution)/shard_map/pallas_call | solution.py:696

commit v7 on v6

--- a/solution.py
+++ b/solution.py
@@ -81,6 +81,9 @@
         def dense_peer(h, d):
             return along(d, 0) if h == 0 else along(0, d)
 
+        def wait_bytes(like, sem):
+            pltpu.make_async_copy(like, like, sem).wait()
+
         def send(src, dst, ss, rs, device):
             return pltpu.make_async_remote_copy(
                 src_ref=src,
@@ -164,8 +167,8 @@
                     pltpu.make_async_remote_copy(
                         src_ref=src.at[i % 2],
                         dst_ref=dst.at[1 - i % 2],
-                        send_sem=ss.at[i],
-                        recv_sem=rs.at[i],
+                        send_sem=ss.at[i // 2],
+                        recv_sem=rs.at[i // 2],
                         device_id=sides[i],
                         device_id_type=MESH,
                     )
@@ -198,46 +201,40 @@
         base = jnp.zeros((1, LANES), F32)
         wanted = jnp.zeros((tiles, n_slots), F32)
         weights = [jnp.zeros((tiles, n_slots), F32) for _ in range(2)]
+        ranks = []
         for k in range(k_blocks):
             earlier = before[:, k * LANES : (k + 1) * LANES] + base
             base = base + jnp.sum(hits[k], axis=0, keepdims=True)
-            rank = jnp.sum(hits[k] * earlier, axis=1, keepdims=True).astype(jnp.int32)
+            ranks.append(jnp.sum(hits[k] * earlier, axis=1, keepdims=True).astype(jnp.int32))
+            here = block[:, k : k + 1] * CAP + ranks[k] == lane_slot
+            wanted = wanted + jnp.where(here, wish[:, k : k + 1], 0.0)
+        asked = jnp.sum(wanted, axis=0, keepdims=True)
+        for g in range(groups):
+            for f in range(2):
+                at = f * half + g * LANES
+                req_send[g, f : f + 1] = asked[:, at : at + LANES]
+
+        for b in others:
+            send(
+                req_send.at[b // per_group],
+                req_recv.at[b],
+                req_ss.at[0],
+                req_rs.at[0],
+                along(b % RING, b // RING),
+            ).start()
+        for k in range(k_blocks):
             col = slice(k, k + 1)
-            here = block[:, col] * CAP + rank == lane_slot
-            wanted = wanted + jnp.where(here, wish[:, col], 0.0)
             for h, (dense, slot) in enumerate(((dz, dy), (dy, dz))):
-                at = (dense * LANES + far * (LANES // 2) + slot * CAP)[:, col] + rank
+                at = (dense * LANES + far * (LANES // 2) + slot * CAP)[:, col] + ranks[k]
                 weights[h] = weights[h] + jnp.where(at == lane_slot, weight[:, col], 0.0)
         for h in range(2):
             for d in range(RING):
                 wsend[h, d] = weights[h][:, d * LANES : (d + 1) * LANES]
             wblk[h, 0] = weights[h][:, 0:LANES]
-        asked = jnp.sum(wanted, axis=0, keepdims=True)
-        for g in range(groups):
-            for f in range(2):
-                at = f * half + g * LANES
-                req_send[g, f : f + 1] = asked[:, at : at + LANES]
-
-        req_copies = []
-        for b in others:
-            copy = send(
-                req_send.at[b // per_group],
-                req_recv.at[b],
-                req_ss.at[b],
-                req_rs.at[b],
-                along(b % RING, b // RING),
-            )
-            copy.start()
-            req_copies.append(copy)
-        w_copies = []
-        for h in range(2):
             for d in range(1, RING):
-                i = h * RING + d
-                copy = send(
-                    wsend.at[h, d], wblk.at[h, d], w_ss.at[i], w_rs.at[i], dense_peer(h, d)
-                )
-                copy.start()
-                w_copies.append(copy)
+                send(
+                    wsend.at[h, d], wblk.at[h, d], w_ss.at[0], w_rs.at[0], dense_peer(h, d)
+                ).start()
         req_recv[0] = req_send[0]
 
         has_north = jnp.where(gx > 0, 1.0, 0.0)
@@ -250,8 +247,8 @@
                 value = source[side, :, lane_at : lane_at + 1] * has
                 pad[(*index, at, slice(row0, row1))] = jnp.broadcast_to(value, (rows, LANES))
 
-        for copy in rims0:
-            copy.wait_recv()
+        wait_bytes(ns0_recv, rim0_rs.at[0])
+        wait_bytes(ew0_recv, rim0_rs.at[1])
         above, below = slice(first - 1, first), slice(last + 1, last + 2)
         put_line(kpad, (), above, ns0_recv[0, 1:2] * has_north)
         put_line(kpad, (), below, ns0_recv[1, 1:2] * has_south)
@@ -305,12 +302,11 @@
             copy.start()
             x_copies.append(copy)
 
-        for copy in req_copies:
-            copy.wait_recv()
+        wait_bytes(req_recv.at[1:PLANE], req_rs.at[0])
         group_lane = iota((per_group, LANES), 1) // CAP
         group_row = iota((per_group, LANES), 0)
         tile_row = iota((tiles, LANES), 0).astype(F32)
-        for f in range(2):
+        def make_picks(f):
             picks = []
             for g in range(groups):
                 block = req_recv[g * per_group : (g + 1) * per_group, f, :]
@@ -323,6 +319,8 @@
             turned = jnp.transpose(jnp.concatenate([pick, pick], axis=0)).astype(BF16)
             lhs1[f * half : (f + 1) * half] = turned
 
+        make_picks(0)
+
         def plane_rows(ref, c, f, d):
             return ref.at[c, f, d] if c % 2 == 0 else ref.at[c, f, :, d]
 
@@ -330,12 +328,11 @@
         for c in range(n_chunks):
             for f in range(2):
                 for d in range(1, RING):
-                    i = (c * 2 + f) * RING + d
                     slots1[c, f, d] = send(
                         plane_rows(send1, c, f, d),
                         recv1.at[c, :, f, d],
-                        s1_ss.at[i],
-                        s1_rs.at[i],
+                        s1_ss.at[0],
+                        s1_rs.at[c],
                         slot_peer(c % 2, -d),
                     )
 
@@ -358,6 +355,7 @@
 
         for pair in (0, 2):
             pack_tiles(0, pair, x_send[pair // 2])
+        make_picks(1)
 
         for load in rim_loads:
             load.wait()
@@ -378,8 +376,7 @@
         for copy in rims:
             copy.start()
 
-        for copy in w_copies:
-            copy.wait_recv()
+        wait_bytes(wblk.at[:, 1:RING], w_rs.at[0])
         for h in range(2):
             for d in range(RING):
                 for i, piece in enumerate(two_parts(wblk[h, d])):
@@ -404,8 +401,8 @@
         put_line(apad, (top,), above, jnp.zeros((1, cols), F32))
         put_line(apad, (top,), below, jnp.zeros((1, cols), F32))
 
-        for copy in rims:
-            copy.wait_recv()
+        wait_bytes(ns_recv, rim_rs.at[0])
+        wait_bytes(ew_recv, rim_rs.at[1])
         for l in range(top):
             column_rims(tpad, (l,), ew_recv, l)
             column_rims(apad, (l,), ew_recv, layers + l)
@@ -462,21 +459,18 @@
         parts, spread = {}, {}
         for c in range(n_chunks):
             for d in range(1, RING):
-                i = c * RING + d
                 parts[c, d] = send(
                     part.at[c, d],
                     part_recv.at[c, d],
-                    p_ss.at[i],
-                    p_rs.at[i],
+                    p_ss.at[0],
+                    p_rs.at[c],
                     dense_peer(c % 2, -d),
                 )
                 spread[c, d] = send(
-                    mis.at[c], mis_recv.at[c, d], m_ss.at[i], m_rs.at[i], dense_peer(c % 2, d)
+                    mis.at[c], mis_recv.at[c, d], m_ss.at[0], m_rs.at[c], dense_peer(c % 2, d)
                 )
         for c in range(n_chunks):
-            for f in range(2):
-                for d in range(1, RING):
-                    slots1[c, f, d].wait_recv()
+            wait_bytes(recv1.at[c, 0 : RING - 1], s1_rs.at[c])
             for d in FARTHEST_FIRST:
                 part[c, d] = weigh(c, d)
                 parts[c, d].start()
@@ -485,8 +479,7 @@
         inner_layers(2)
 
         for c in range(n_chunks):
-            for d in range(1, RING):
-                parts[c, d].wait_recv()
+            wait_bytes(part_recv.at[c, 1:RING], p_rs.at[c])
             mis[c] += part_recv[c, 1] + (part_recv[c, 2] + part_recv[c, 3])
             for d in FARTHEST_FIRST:
                 spread[c, d].start()
@@ -498,18 +491,16 @@
         for c in range(n_chunks):
             for f in range(2):
                 for d in range(1, RING):
-                    i = (c * 2 + f) * RING + d
                     slots2[c, f, d] = send(
                         send2.at[c, :, f, d],
                         plane_rows(recv2, c, f, d),
-                        s2_ss.at[i],
-                        s2_rs.at[i],
+                        s2_ss.at[0],
+                        s2_rs.at[2 * c + f],
                         slot_peer(c % 2, d),
                     )
         for c in range(n_chunks):
+            wait_bytes(mis_recv.at[c, 1:RING], m_rs.at[c])
             for d in range(RING):
-                if d:
-                    spread[c, d].wait_recv()
                 mh, ml = two_parts(mis_recv[c, d] if d else mis[c])
                 packed = jnp.dot(
                     lhs2[c % 2, d],
@@ -531,15 +522,23 @@
 
         for r in range(4, strips):
             inner_layers(r)
-        sent = rims0 + rims + req_copies + w_copies + x_copies
-        for group in (slots1, parts, spread):
-            sent.extend(group.values())
-        for copy in sent:
+        for like, sem in (
+            (ns0_recv, rim0_ss.at[0]),
+            (ew0_recv, rim0_ss.at[1]),
+            (ns_recv, rim_ss.at[0]),
+            (ew_recv, rim_ss.at[1]),
+            (req_recv.at[1:PLANE], req_ss.at[0]),
+            (wblk.at[:, 1:RING], w_ss.at[0]),
+            (recv1.at[:, 0 : RING - 1], s1_ss.at[0]),
+            (part.at[:, 1:RING], p_ss.at[0]),
+            (part.at[:, 1:RING], m_ss.at[0]),
+        ):
+            wait_bytes(like, sem)
+        for copy in x_copies:
             copy.wait_send()
 
         def gathered(c, f):
-            for d in range(1, RING):
-                slots2[c, f, d].wait_recv()
+            wait_bytes(recv2.at[c, f, 0 : RING - 1], s2_rs.at[2 * c + f])
             pick = onehot[:, f * half : (f + 1) * half].astype(BF16)
             return jnp.dot(
                 jnp.concatenate([pick, pick], axis=1),
@@ -582,11 +581,12 @@
             under = across(apad, (top - 1,), inner)
             outv[top, strip] = value + RATE_VERTICAL * (under - ac)
             gradv[strip] = gin[strip] - (0.5 * RATE_PLANE) * total
-        for copy in list(slots2.values()) + xa_copies:
+        wait_bytes(recv2.at[:, :, 0 : RING - 1], s2_ss.at[0])
+        for copy in xa_copies:
             copy.wait_send()
 
-        for copy in rims2:
-            copy.wait_recv()
+        wait_bytes(ns2_recv, rim2_rs.at[0])
+        wait_bytes(ew2_recv, rim2_rs.at[1])
         for side, has, row, beyond in ((0, has_north, 0, first - 1), (1, has_south, rows - 1, last + 1)):
             at = slice(row, row + 1)
             rim = ns2_recv[side] * has
@@ -605,8 +605,8 @@
             outv[top, :, at] += coef[face, :, at] * rim
             gradv[:, at] -= (0.5 * RATE_PLANE) * slope * rim
 
-        for copy in rims2:
-            copy.wait_send()
+        wait_bytes(ns2_recv, rim2_ss.at[0])
+        wait_bytes(ew2_recv, rim2_ss.at[1])
 
     dma = pltpu.SemaphoreType.DMA
 
@@ -654,14 +654,14 @@
         vmem(n_chunks, RING, 2, RING, CAP, wide),
         vmem(n_chunks, 2, RING, RING, CAP, wide),
         dma((9 + 4 * tile_cols,)),
-        *[dma((4,)) for _ in range(6)],
+        *[dma((2,)) for _ in range(6)],
         dma((2 + n_chunks,)), dma((2 + n_chunks,)),
-        dma((PLANE,)), dma((PLANE,)),
-        dma((2 * RING,)), dma((2 * RING,)),
-        dma((2 * n_chunks * RING,)), dma((2 * n_chunks * RING,)),
-        dma((n_chunks * RING,)), dma((n_chunks * RING,)),
-        dma((n_chunks * RING,)), dma((n_chunks * RING,)),
-        dma((2 * n_chunks * RING,)), dma((2 * n_chunks * RING,)),
+        dma((1,)), dma((1,)),
+        dma((1,)), dma((1,)),
+        dma((1,)), dma((n_chunks,)),
+        dma((1,)), dma((n_chunks,)),
+        dma((1,)), dma((n_chunks,)),
+        dma((1,)), dma((2 * n_chunks,)),
     ]
     in_hbm = pl.BlockSpec(memory_space=pltpu.HBM)
     in_vmem = pl.BlockSpec(memory_space=pltpu.VMEM)

time: 65.2 us -> 63 us (0.966)
  Pallas kernels: 64.4 us -> 62.2 us
    pallas_call x1, Pallas kernels: 62.9 us -> 60.7 us  [local(): call(*(pltpu.with_memory_space_constraint(x, pltpu.HBM) for x in operands))]
where the time goes in v7:
time: 63 us; the launch traced here: 62.9 us
  Pallas kernels  62.2 us (99%)
  between operations  0.64 us (1%)
    pallas_call x1, Pallas kernels, local(): call(*(pltpu.with_memory_space_constraint(x, pltpu.HBM) for x in operands))  60.7 us
    pallas_call x1, Pallas kernels, write_out(): pl.pallas_call(kernel, out_shape=tuple((jax.ShapeDtypeStruct(x.shape, x.d...  1.51 us

profile of v7, /device:TPU:0, one launch (start us, length us, event | category | flops | bytes accessed | tf_op | source)
XLA Modules:
  0.0 62.9 jit_solution(13048196838162094664)
XLA Ops:
  0.6 60.7 %shard_map.103 = (f32[64,1024]{1,0:T(8,128)S(1)}, f32[8,64,1024]{2,1,0:T(8,128)S(1)}, f32[64,1024]{1,0:T(8,128)S(1)}) custom-call(f32[8,64,1024]{2,1,0:T(8,128)} %temp.1, f32[64,1024]{1,0:T(8,128)} %cond.1, f32[8,64,1024]{2,1,0:T(8,128)} %adj.1, f32[64,1024]{1,0:T(8,128)} %grad.1, f32[4,64,1024]{2,1,0:T(8,128)} %obs.1, s32[1,64]{1,0:T(1,128)} %bitcast.5, ...), custom_call_target="tpu_custom_call" | custom-call | tf_op jit(solution)/shard_map/pallas_call | solution.py:715
  61.4 1.5 %shard_map.104 = (f32[64,1024]{1,0:T(8,128)}, f32[8,64,1024]{2,1,0:T(8,128)}, f32[64,1024]{1,0:T(8,128)}) custom-call(f32[64,1024]{1,0:T(8,128)S(1)} %get-tuple-element.6.refs_0_, f32[8,64,1024]{2,1,0:T(8,128)S(1)} %get-tuple-element.7.refs_1_, f32[64,1024]{1,0:T(8,128)S(1)} %get-tuple-element.8.refs_2_), custom_call_target="tpu_custom_call" | custom-call | tf_op jit(solution)/shard_map/pallas_call | solution.py:696

commit v8 on v7

--- a/solution.py
+++ b/solution.py
@@ -99,7 +99,7 @@
                 pltpu.make_async_copy(
                     src.at[(*src_layers, slice(None), slice(u * TC, (u + 1) * TC))],
                     pad.at[(*pad_layers, u + 1, slice(row0, row1))],
-                    in_sem.at[sem + u],
+                    in_sem.at[sem],
                 )
                 for u in range(tile_cols)
             ]
@@ -107,11 +107,9 @@
         both = (slice(top - 1, layers),)
         rest = (slice(0, top - 1),)
         all_layers = (slice(0, layers),)
-        first_loads = block_loads(temp, both, tpad, both, 9) + block_loads(
-            cond, (), kpad, (), 9 + tile_cols
-        )
-        rim_loads = block_loads(temp, rest, tpad, rest, 9 + 2 * tile_cols) + block_loads(
-            adj, all_layers, apad, all_layers, 9 + 3 * tile_cols
+        first_loads = block_loads(temp, both, tpad, both, 0) + block_loads(cond, (), kpad, (), 1)
+        rim_loads = block_loads(temp, rest, tpad, rest, 2) + block_loads(
+            adj, all_layers, apad, all_layers, 3
         )
         loads = [None] * 4 + [
             pltpu.make_async_copy(grad, gin, in_sem.at[4]),
@@ -131,8 +129,9 @@
         for load in loads[6:] + rim_loads + loads[4:6]:
             load.start()
 
-        for load in first_loads:
-            load.wait()
+        inside = (slice(1, tile_cols + 1), slice(row0, row1))
+        wait_bytes(tpad.at[(*both, *inside)], in_sem.at[0])
+        wait_bytes(kpad.at[inside], in_sem.at[1])
         first, last = row0, row1 - 1
 
         def across(pad, index, at):
@@ -322,19 +321,29 @@
         make_picks(0)
 
         def plane_rows(ref, c, f, d):
-            return ref.at[c, f, d] if c % 2 == 0 else ref.at[c, f, :, d]
+            return ref.at[0, c // 2, f, d] if c % 2 == 0 else ref.at[1, c // 2, f, :, d]
+
+        def near_rows(ref, h, d):
+            return ref.at[0, :, 0, d] if h == 0 else ref.at[1, :, 0, :, d]
 
         slots1 = {}
-        for c in range(n_chunks):
-            for f in range(2):
-                for d in range(1, RING):
-                    slots1[c, f, d] = send(
-                        plane_rows(send1, c, f, d),
-                        recv1.at[c, :, f, d],
-                        s1_ss.at[0],
-                        s1_rs.at[c],
-                        slot_peer(c % 2, -d),
-                    )
+        for d in range(1, RING):
+            for c in range(n_chunks):
+                slots1[c, 1, d] = send(
+                    plane_rows(send1, c, 1, d),
+                    recv1.at[c % 2, c // 2, :, 1, d],
+                    s1_ss.at[0],
+                    s1_rs.at[c],
+                    slot_peer(c % 2, -d),
+                )
+            for h in range(2):
+                slots1[h, 0, d] = send(
+                    near_rows(send1, h, d),
+                    recv1.at[h, :, :, 0, d],
+                    s1_ss.at[0],
+                    s1_rs.at[n_chunks + h],
+                    slot_peer(h, -d),
+                )
 
         def columns(c, count=1):
             return slice(c * wide, (c + count) * wide)
@@ -348,17 +357,21 @@
                     rhs[:, columns(c)],
                     preferred_element_type=F32,
                 )
-                send1[c, f] = packed.reshape(RING, RING, CAP, wide)
-                for d in FARTHEST_FIRST:
-                    slots1[c, f, d].start()
-                recv1[c, :, f, 0] = send1[c, f, 0] if c % 2 == 0 else send1[c, f, :, 0]
+                send1[c % 2, c // 2, f] = packed.reshape(RING, RING, CAP, wide)
+                if f == 1:
+                    for d in FARTHEST_FIRST:
+                        slots1[c, f, d].start()
+                recv1[c % 2, c // 2, :, f, 0] = send1[c % 2, c // 2, f, 0] if c % 2 == 0 else send1[c % 2, c // 2, f, :, 0]
 
         for pair in (0, 2):
             pack_tiles(0, pair, x_send[pair // 2])
+        for d in FARTHEST_FIRST:
+            for h in range(2):
+                slots1[h, 0, d].start()
         make_picks(1)
 
-        for load in rim_loads:
-            load.wait()
+        wait_bytes(tpad.at[(*rest, *inside)], in_sem.at[2])
+        wait_bytes(apad.at[(*all_layers, *inside)], in_sem.at[3])
         for side, row in ((0, first), (1, last)):
             for u in range(tile_cols):
                 at = slice(u * TC, (u + 1) * TC)
@@ -451,7 +464,7 @@
         def weigh(c, d):
             both = jnp.dot(
                 wcat[c % 2, d],
-                jnp.concatenate(two_parts(recv1[c, d].reshape(LANES, wide)), axis=0),
+                jnp.concatenate(two_parts(recv1[c % 2, c // 2, d].reshape(LANES, wide)), axis=0),
                 preferred_element_type=F32,
             )
             return both[0:tiles] + both[tiles : 2 * tiles]
@@ -470,7 +483,9 @@
                     mis.at[c], mis_recv.at[c, d], m_ss.at[0], m_rs.at[c], dense_peer(c % 2, d)
                 )
         for c in range(n_chunks):
-            wait_bytes(recv1.at[c, 0 : RING - 1], s1_rs.at[c])
+            if c < 2:
+                wait_bytes(recv1.at[c, :, 0 : RING - 1, 0], s1_rs.at[n_chunks + c])
+            wait_bytes(recv1.at[c % 2, c // 2, 0 : RING - 1, 1], s1_rs.at[c])
             for d in FARTHEST_FIRST:
                 part[c, d] = weigh(c, d)
                 parts[c, d].start()
@@ -488,16 +503,23 @@
         inner_layers(3)
 
         slots2 = {}
-        for c in range(n_chunks):
-            for f in range(2):
-                for d in range(1, RING):
-                    slots2[c, f, d] = send(
-                        send2.at[c, :, f, d],
-                        plane_rows(recv2, c, f, d),
-                        s2_ss.at[0],
-                        s2_rs.at[2 * c + f],
-                        slot_peer(c % 2, d),
-                    )
+        for d in range(1, RING):
+            for c in range(n_chunks):
+                slots2[c, 1, d] = send(
+                    send2.at[c % 2, c // 2, :, 1, d],
+                    plane_rows(recv2, c, 1, d),
+                    s2_ss.at[0],
+                    s2_rs.at[c],
+                    slot_peer(c % 2, d),
+                )
+            for h in range(2):
+                slots2[h, 0, d] = send(
+                    send2.at[h, :, :, 0, d],
+                    near_rows(recv2, h, d),
+                    s2_ss.at[0],
+                    s2_rs.at[n_chunks + h],
+                    slot_peer(h, d),
+                )
         for c in range(n_chunks):
             wait_bytes(mis_recv.at[c, 1:RING], m_rs.at[c])
             for d in range(RING):
@@ -507,18 +529,18 @@
                     jnp.concatenate([mh, mh, ml, ml], axis=0),
                     preferred_element_type=F32,
                 )
-                send2[c, d] = packed.reshape(2, RING, CAP, wide)
+                send2[c % 2, c // 2, d] = packed.reshape(2, RING, CAP, wide)
             for d in FARTHEST_FIRST:
                 slots2[c, 1, d].start()
-        for c in range(n_chunks):
-            for d in FARTHEST_FIRST:
-                slots2[c, 0, d].start()
+        for d in FARTHEST_FIRST:
+            for h in range(2):
+                slots2[h, 0, d].start()
         for c in range(n_chunks):
             for f in range(2):
                 if c % 2 == 0:
-                    recv2[c, f, 0] = send2[c, :, f, 0]
+                    recv2[c % 2, c // 2, f, 0] = send2[c % 2, c // 2, :, f, 0]
                 else:
-                    recv2[c, f, :, 0] = send2[c, :, f, 0]
+                    recv2[c % 2, c // 2, f, :, 0] = send2[c % 2, c // 2, :, f, 0]
 
         for r in range(4, strips):
             inner_layers(r)
@@ -529,7 +551,7 @@
             (ew_recv, rim_ss.at[1]),
             (req_recv.at[1:PLANE], req_ss.at[0]),
             (wblk.at[:, 1:RING], w_ss.at[0]),
-            (recv1.at[:, 0 : RING - 1], s1_ss.at[0]),
+            (recv1.at[:, :, 0 : RING - 1], s1_ss.at[0]),
             (part.at[:, 1:RING], p_ss.at[0]),
             (part.at[:, 1:RING], m_ss.at[0]),
         ):
@@ -538,11 +560,14 @@
             copy.wait_send()
 
         def gathered(c, f):
-            wait_bytes(recv2.at[c, f, 0 : RING - 1], s2_rs.at[2 * c + f])
+            if f == 1:
+                wait_bytes(recv2.at[c % 2, c // 2, 1, 0 : RING - 1], s2_rs.at[c])
+            elif c < 2:
+                wait_bytes(recv2.at[c, :, 0, 0 : RING - 1], s2_rs.at[n_chunks + c])
             pick = onehot[:, f * half : (f + 1) * half].astype(BF16)
             return jnp.dot(
                 jnp.concatenate([pick, pick], axis=1),
-                jnp.concatenate(two_parts(recv2[c, f].reshape(half, wide)), axis=0),
+                jnp.concatenate(two_parts(recv2[c % 2, c // 2, f].reshape(half, wide)), axis=0),
                 preferred_element_type=F32,
             )
 
@@ -581,7 +606,7 @@
             under = across(apad, (top - 1,), inner)
             outv[top, strip] = value + RATE_VERTICAL * (under - ac)
             gradv[strip] = gin[strip] - (0.5 * RATE_PLANE) * total
-        wait_bytes(recv2.at[:, :, 0 : RING - 1], s2_ss.at[0])
+        wait_bytes(recv2.at[:, :, :, 0 : RING - 1], s2_ss.at[0])
         for copy in xa_copies:
             copy.wait_send()
 
@@ -646,22 +671,22 @@
         vmem(2, RING, LANES, 4 * tiles, dtype=BF16),
         *pair(2, tiles, tile // 2),
         *pair(n_chunks, tiles, wide),
-        vmem(n_chunks, 2, RING, RING, CAP, wide),
-        vmem(n_chunks, RING, 2, RING, CAP, wide),
+        vmem(2, n_chunks // 2, 2, RING, RING, CAP, wide),
+        vmem(2, n_chunks // 2, RING, 2, RING, CAP, wide),
         *pair(n_chunks, RING, tiles, wide),
         vmem(n_chunks, tiles, wide),
         vmem(n_chunks, RING, tiles, wide),
-        vmem(n_chunks, RING, 2, RING, CAP, wide),
-        vmem(n_chunks, 2, RING, RING, CAP, wide),
-        dma((9 + 4 * tile_cols,)),
+        vmem(2, n_chunks // 2, RING, 2, RING, CAP, wide),
+        vmem(2, n_chunks // 2, 2, RING, RING, CAP, wide),
+        dma((9,)),
         *[dma((2,)) for _ in range(6)],
         dma((2 + n_chunks,)), dma((2 + n_chunks,)),
         dma((1,)), dma((1,)),
         dma((1,)), dma((1,)),
+        dma((1,)), dma((2 + n_chunks,)),
         dma((1,)), dma((n_chunks,)),
         dma((1,)), dma((n_chunks,)),
-        dma((1,)), dma((n_chunks,)),
-        dma((1,)), dma((2 * n_chunks,)),
+        dma((1,)), dma((2 + n_chunks,)),
     ]
     in_hbm = pl.BlockSpec(memory_space=pltpu.HBM)
     in_vmem = pl.BlockSpec(memory_space=pltpu.VMEM)

time: 63 us -> 63.1 us (level)
  no operation moved by 1% of the time
where the time goes in v8:
time: 63.1 us; the launch traced here: 63 us
  Pallas kernels  62.4 us (99%)
  between operations  0.64 us (1%)
    pallas_call x1, Pallas kernels, local(): call(*(pltpu.with_memory_space_constraint(x, pltpu.HBM) for x in operands))  60.8 us
    pallas_call x1, Pallas kernels, write_out(): pl.pallas_call(kernel, out_shape=tuple((jax.ShapeDtypeStruct(x.shape, x.d...  1.51 us

profile of v8, /device:TPU:0, one launch (start us, length us, event | category | flops | bytes accessed | tf_op | source)
XLA Modules:
  0.0 63.0 jit_solution(6323422099557927633)
XLA Ops:
  0.6 60.8 %shard_map.103 = (f32[64,1024]{1,0:T(8,128)S(1)}, f32[8,64,1024]{2,1,0:T(8,128)S(1)}, f32[64,1024]{1,0:T(8,128)S(1)}) custom-call(f32[8,64,1024]{2,1,0:T(8,128)} %temp.1, f32[64,1024]{1,0:T(8,128)} %cond.1, f32[8,64,1024]{2,1,0:T(8,128)} %adj.1, f32[64,1024]{1,0:T(8,128)} %grad.1, f32[4,64,1024]{2,1,0:T(8,128)} %obs.1, s32[1,64]{1,0:T(1,128)} %bitcast.5, ...), custom_call_target="tpu_custom_call" | custom-call | tf_op jit(solution)/shard_map/pallas_call | solution.py:740
  61.5 1.5 %shard_map.104 = (f32[64,1024]{1,0:T(8,128)}, f32[8,64,1024]{2,1,0:T(8,128)}, f32[64,1024]{1,0:T(8,128)}) custom-call(f32[64,1024]{1,0:T(8,128)S(1)} %get-tuple-element.6.refs_0_, f32[8,64,1024]{2,1,0:T(8,128)S(1)} %get-tuple-element.7.refs_1_, f32[64,1024]{1,0:T(8,128)S(1)} %get-tuple-element.8.refs_2_), custom_call_target="tpu_custom_call" | custom-call | tf_op jit(solution)/shard_map/pallas_call | solution.py:721

commit v9 on v8

--- a/solution.py
+++ b/solution.py
@@ -397,9 +397,8 @@
                         [piece, piece], axis=1
                     )
 
-        for pair in (0, 2):
-            x_copies[pair // 2].wait_recv()
-            pack_tiles(1, pair, x_recv[pair // 2])
+        x_copies[0].wait_recv()
+        pack_tiles(1, 0, x_recv[0])
 
         for h in range(2):
             for d in range(RING):
@@ -425,6 +424,18 @@
                 tpad[0:top, u + 1, at, :] = ns_recv[side, 0:top, cut] * has
                 apad[0:top, u + 1, at, :] = ns_recv[side, layers : layers + top, cut] * has
 
+        loads[4].wait()
+        loads[5].wait()
+        frame = columns_of[:, 2 * k_blocks : 2 * k_blocks + 1].astype(jnp.int32)
+        for c in range(n_chunks):
+            seen = jnp.zeros((tiles, wide), F32)
+            for f in range(frames):
+                seen = jnp.where(frame == f, obs_v[f, :, columns(c)], seen)
+            mis[c] = -seen
+
+        x_copies[1].wait_recv()
+        pack_tiles(1, 2, x_recv[1])
+
         def layer_step(l, r, total):
             strip = slice(r * TR, (r + 1) * TR)
             tc, *t_near = around(tpad, (l,), r)
@@ -449,17 +460,7 @@
 
             gacc[strip] = lax.fori_loop(0, top, body, jnp.zeros((TR, cols), F32))
 
-        for r in range(0, 2):
-            inner_layers(r)
-
-        loads[4].wait()
-        loads[5].wait()
-        frame = columns_of[:, 2 * k_blocks : 2 * k_blocks + 1].astype(jnp.int32)
-        for c in range(n_chunks):
-            seen = jnp.zeros((tiles, wide), F32)
-            for f in range(frames):
-                seen = jnp.where(frame == f, obs_v[f, :, columns(c)], seen)
-            mis[c] = -seen
+        inner_layers(0)
 
         def weigh(c, d):
             both = jnp.dot(
@@ -491,16 +492,14 @@
                 parts[c, d].start()
             mis[c] += weigh(c, 0)
 
-        inner_layers(2)
-
         for c in range(n_chunks):
             wait_bytes(part_recv.at[c, 1:RING], p_rs.at[c])
             mis[c] += part_recv[c, 1] + (part_recv[c, 2] + part_recv[c, 3])
             for d in FARTHEST_FIRST:
                 spread[c, d].start()
             misfit_out[:, columns(c)] = mis[c]
-
-        inner_layers(3)
+            if c % 2 == 1:
+                inner_layers(1 + c // 2)
 
         slots2 = {}
         for d in range(1, RING):
@@ -542,8 +541,7 @@
                 else:
                     recv2[c % 2, c // 2, f, :, 0] = send2[c % 2, c // 2, :, f, 0]
 
-        for r in range(4, strips):
-            inner_layers(r)
+        inner_layers(3)
         for like, sem in (
             (ns0_recv, rim0_ss.at[0]),
             (ew0_recv, rim0_ss.at[1]),
@@ -577,6 +575,9 @@
             copy = send(xa_send.at[c], xa_recv.at[c], x_ss.at[2 + c], x_rs.at[2 + c], partner)
             copy.start()
             xa_copies.append(copy)
+            if c % 2 == 1:
+                for r in range(3 + c, 5 + c):
+                    inner_layers(r)
         sums = [gathered(c, 0) for c in range(n_chunks)]
         for copy in xa_copies:
             copy.wait_recv()
@@ -708,10 +709,14 @@
 
 def write_out(results):
     count = len(results)
+    layers = results[1].shape[0]
 
     def kernel(*refs):
+        misfit, adjoint, grad, misfit_out, adjoint_out, grad_out, sems = refs
+        pairs = [(misfit, misfit_out), (grad, grad_out)]
+        pairs += [(adjoint.at[l], adjoint_out.at[l]) for l in range(layers)]
         copies = [
-            pltpu.make_async_copy(refs[i], refs[count + i], refs[-1].at[i]) for i in range(count)
+            pltpu.make_async_copy(src, dst, sems.at[i]) for i, (src, dst) in enumerate(pairs)
         ]
         for copy in copies:
             copy.start()
@@ -723,7 +728,7 @@
         out_shape=tuple(jax.ShapeDtypeStruct(x.shape, x.dtype) for x in results),
         in_specs=[pl.BlockSpec(memory_space=pltpu.VMEM)] * count,
         out_specs=[pl.BlockSpec(memory_space=pl.ANY)] * count,
-        scratch_shapes=[pltpu.SemaphoreType.DMA((count,))],
+        scratch_shapes=[pltpu.SemaphoreType.DMA((layers + 2,))],
         compiler_params=pltpu.CompilerParams(vmem_limit_bytes=8 * 1024 * 1024),
     )(*results)
 

time: 63.1 us -> 65.3 us (1.035)
  Pallas kernels: 62.4 us -> 64.6 us
    pallas_call x1, Pallas kernels: 60.8 us -> 63 us  [local(): call(*(pltpu.with_memory_space_constraint(x, pltpu.HBM) for x in operands))]
where the time goes in v9:
time: 65.3 us; the launch traced here: 65.2 us
  Pallas kernels  64.6 us (99%)
    pallas_call x1, Pallas kernels, local(): call(*(pltpu.with_memory_space_constraint(x, pltpu.HBM) for x in operands))  63 us
    pallas_call x1, Pallas kernels, write_out(): pl.pallas_call(kernel, out_shape=tuple((jax.ShapeDtypeStruct(x.shape, x.d...  1.57 us

profile of v9, /device:TPU:0, one launch (start us, length us, event | category | flops | bytes accessed | tf_op | source)
XLA Modules:
  0.0 65.2 jit_solution(6109679163049385890)
XLA Ops:
  0.6 63.0 %shard_map.103 = (f32[64,1024]{1,0:T(8,128)S(1)}, f32[8,64,1024]{2,1,0:T(8,128)S(1)}, f32[64,1024]{1,0:T(8,128)S(1)}) custom-call(f32[8,64,1024]{2,1,0:T(8,128)} %temp.1, f32[64,1024]{1,0:T(8,128)} %cond.1, f32[8,64,1024]{2,1,0:T(8,128)} %adj.1, f32[64,1024]{1,0:T(8,128)} %grad.1, f32[4,64,1024]{2,1,0:T(8,128)} %obs.1, s32[1,64]{1,0:T(1,128)} %bitcast.5, ...), custom_call_target="tpu_custom_call" | custom-call | tf_op jit(solution)/shard_map/pallas_call | solution.py:745
  63.6 1.6 %shard_map.104 = (f32[64,1024]{1,0:T(8,128)}, f32[8,64,1024]{2,1,0:T(8,128)}, f32[64,1024]{1,0:T(8,128)}) custom-call(f32[64,1024]{1,0:T(8,128)S(1)} %get-tuple-element.6.refs_0_, f32[8,64,1024]{2,1,0:T(8,128)S(1)} %get-tuple-element.7.refs_1_, f32[64,1024]{1,0:T(8,128)S(1)} %get-tuple-element.8.refs_2_), custom_call_target="tpu_custom_call" | custom-call | tf_op jit(solution)/shard_map/pallas_call | solution.py:726

commit v10 on v8

--- a/solution.py
+++ b/solution.py
@@ -449,7 +449,7 @@
 
             gacc[strip] = lax.fori_loop(0, top, body, jnp.zeros((TR, cols), F32))
 
-        for r in range(0, 2):
+        for r in range(0, 4):
             inner_layers(r)
 
         loads[4].wait()
@@ -491,7 +491,7 @@
                 parts[c, d].start()
             mis[c] += weigh(c, 0)
 
-        inner_layers(2)
+        inner_layers(4)
 
         for c in range(n_chunks):
             wait_bytes(part_recv.at[c, 1:RING], p_rs.at[c])
@@ -500,7 +500,7 @@
                 spread[c, d].start()
             misfit_out[:, columns(c)] = mis[c]
 
-        inner_layers(3)
+        inner_layers(5)
 
         slots2 = {}
         for d in range(1, RING):
@@ -542,7 +542,7 @@
                 else:
                     recv2[c % 2, c // 2, f, :, 0] = send2[c % 2, c // 2, :, f, 0]
 
-        for r in range(4, strips):
+        for r in range(6, strips):
             inner_layers(r)
         for like, sem in (
             (ns0_recv, rim0_ss.at[0]),

time: 63.1 us -> 63.1 us (level)
  no operation moved by 1% of the time
where the time goes in v10:
time: 63.1 us; the launch traced here: 63 us
  Pallas kernels  62.4 us (99%)
  between operations  0.64 us (1%)
    pallas_call x1, Pallas kernels, local(): call(*(pltpu.with_memory_space_constraint(x, pltpu.HBM) for x in operands))  60.9 us
    pallas_call x1, Pallas kernels, write_out(): pl.pallas_call(kernel, out_shape=tuple((jax.ShapeDtypeStruct(x.shape, x.d...  1.51 us

profile of v10, /device:TPU:0, one launch (start us, length us, event | category | flops | bytes accessed | tf_op | source)
XLA Modules:
  0.0 63.0 jit_solution(9575219159608033803)
XLA Ops:
  0.6 60.9 %shard_map.103 = (f32[64,1024]{1,0:T(8,128)S(1)}, f32[8,64,1024]{2,1,0:T(8,128)S(1)}, f32[64,1024]{1,0:T(8,128)S(1)}) custom-call(f32[8,64,1024]{2,1,0:T(8,128)} %temp.1, f32[64,1024]{1,0:T(8,128)} %cond.1, f32[8,64,1024]{2,1,0:T(8,128)} %adj.1, f32[64,1024]{1,0:T(8,128)} %grad.1, f32[4,64,1024]{2,1,0:T(8,128)} %obs.1, s32[1,64]{1,0:T(1,128)} %bitcast.5, ...), custom_call_target="tpu_custom_call" | custom-call | tf_op jit(solution)/shard_map/pallas_call | solution.py:740
  61.5 1.5 %shard_map.104 = (f32[64,1024]{1,0:T(8,128)}, f32[8,64,1024]{2,1,0:T(8,128)}, f32[64,1024]{1,0:T(8,128)}) custom-call(f32[64,1024]{1,0:T(8,128)S(1)} %get-tuple-element.6.refs_0_, f32[8,64,1024]{2,1,0:T(8,128)S(1)} %get-tuple-element.7.refs_1_, f32[64,1024]{1,0:T(8,128)S(1)} %get-tuple-element.8.refs_2_), custom_call_target="tpu_custom_call" | custom-call | tf_op jit(solution)/shard_map/pallas_call | solution.py:721

commit v11 on v8

--- a/solution.py
+++ b/solution.py
@@ -53,7 +53,7 @@
         ns_send, ns_recv, ew_send, ew_recv,
         ns2_send, ns2_recv, ew2_send, ew2_recv,
         small, req_send, req_recv, tiles3, onehot, lhs1, rhs,
-        wsend, wblk, wcat, lhs2,
+        wsend, wblk, wcol, wcat, lhs2,
         x_send, x_recv, xa_send, xa_recv,
         send1, recv1, part, part_recv, mis, mis_recv, send2, recv2,
         in_sem,
@@ -390,13 +390,6 @@
             copy.start()
 
         wait_bytes(wblk.at[:, 1:RING], w_rs.at[0])
-        for h in range(2):
-            for d in range(RING):
-                for i, piece in enumerate(two_parts(wblk[h, d])):
-                    wcat[h, d, i * tiles : (i + 1) * tiles] = jnp.concatenate(
-                        [piece, piece], axis=1
-                    )
-
         for pair in (0, 2):
             x_copies[pair // 2].wait_recv()
             pack_tiles(1, pair, x_recv[pair // 2])
@@ -407,6 +400,12 @@
                 turned = jnp.transpose(parts_of).astype(BF16)
                 lhs2[h, d, :, 0 : 2 * tiles] = turned
                 lhs2[h, d, :, 2 * tiles : 4 * tiles] = turned
+                slot_weight = jnp.sum(wblk[h, d], axis=0, keepdims=True)
+                wcol[h, d] = jnp.transpose(jnp.broadcast_to(slot_weight, (LANES, LANES)))
+                hit = jnp.where(wblk[h, d] != 0.0, 1.0, 0.0).astype(BF16)
+                for f in range(2):
+                    piece = hit[:, f * tiles : (f + 1) * tiles]
+                    wcat[h, d, f] = jnp.concatenate([piece, piece], axis=1)
 
         edge = jnp.zeros((rows, LANES), F32)
         apad[top, 0, row0:row1] = edge
@@ -461,13 +460,15 @@
                 seen = jnp.where(frame == f, obs_v[f, :, columns(c)], seen)
             mis[c] = -seen
 
-        def weigh(c, d):
-            both = jnp.dot(
-                wcat[c % 2, d],
-                jnp.concatenate(two_parts(recv1[c % 2, c // 2, d].reshape(LANES, wide)), axis=0),
+        def weigh(c, d, f):
+            scale = wcol[c % 2, d, f * tiles : (f + 1) * tiles]
+            value = recv1[c % 2, c // 2, d, f].reshape(tiles, wide)
+            value = value * jnp.concatenate([scale] * (wide // LANES), axis=1)
+            return jnp.dot(
+                wcat[c % 2, d, f],
+                jnp.concatenate(two_parts(value), axis=0),
                 preferred_element_type=F32,
             )
-            return both[0:tiles] + both[tiles : 2 * tiles]
 
         parts, spread = {}, {}
         for c in range(n_chunks):
@@ -485,11 +486,15 @@
         for c in range(n_chunks):
             if c < 2:
                 wait_bytes(recv1.at[c, :, 0 : RING - 1, 0], s1_rs.at[n_chunks + c])
+            for d in range(1, RING):
+                part[c, d] = weigh(c, d, 0)
+            mis[c] += weigh(c, 0, 0)
+        for c in range(n_chunks):
             wait_bytes(recv1.at[c % 2, c // 2, 0 : RING - 1, 1], s1_rs.at[c])
             for d in FARTHEST_FIRST:
-                part[c, d] = weigh(c, d)
+                part[c, d] += weigh(c, d, 1)
                 parts[c, d].start()
-            mis[c] += weigh(c, 0)
+            mis[c] += weigh(c, 0, 1)
 
         inner_layers(2)
 
@@ -667,7 +672,8 @@
         vmem(n_slots, 2 * tiles, dtype=BF16),
         vmem(2 * tiles, tile, dtype=BF16),
         *pair(2, RING, tiles, LANES),
-        vmem(2, RING, 2 * tiles, 4 * tiles, dtype=BF16),
+        vmem(2, RING, LANES, LANES),
+        vmem(2, RING, 2, tiles, 2 * tiles, dtype=BF16),
         vmem(2, RING, LANES, 4 * tiles, dtype=BF16),
         *pair(2, tiles, tile // 2),
         *pair(n_chunks, tiles, wide),

time: 63.1 us -> 63.8 us (1.011)
  Pallas kernels: 62.4 us -> 63.1 us
    pallas_call x1, Pallas kernels: 60.8 us -> 61.5 us  [local(): call(*(pltpu.with_memory_space_constraint(x, pltpu.HBM) for x in operands))]
where the time goes in v11:
time: 63.8 us; the launch traced here: 63.7 us
  Pallas kernels  63.1 us (99%)
  between operations  0.64 us (1%)
    pallas_call x1, Pallas kernels, local(): call(*(pltpu.with_memory_space_constraint(x, pltpu.HBM) for x in operands))  61.5 us
    pallas_call x1, Pallas kernels, write_out(): pl.pallas_call(kernel, out_shape=tuple((jax.ShapeDtypeStruct(x.shape, x.d...  1.51 us

profile of v11, /device:TPU:0, one launch (start us, length us, event | category | flops | bytes accessed | tf_op | source)
XLA Modules:
  0.0 63.7 jit_solution(320966193978019825)
XLA Ops:
  0.6 61.5 %shard_map.103 = (f32[64,1024]{1,0:T(8,128)S(1)}, f32[8,64,1024]{2,1,0:T(8,128)S(1)}, f32[64,1024]{1,0:T(8,128)S(1)}) custom-call(f32[8,64,1024]{2,1,0:T(8,128)} %temp.1, f32[64,1024]{1,0:T(8,128)} %cond.1, f32[8,64,1024]{2,1,0:T(8,128)} %adj.1, f32[64,1024]{1,0:T(8,128)} %grad.1, f32[4,64,1024]{2,1,0:T(8,128)} %obs.1, s32[1,64]{1,0:T(1,128)} %bitcast.5, ...), custom_call_target="tpu_custom_call" | custom-call | tf_op jit(solution)/shard_map/pallas_call | solution.py:746
  62.2 1.5 %shard_map.104 = (f32[64,1024]{1,0:T(8,128)}, f32[8,64,1024]{2,1,0:T(8,128)}, f32[64,1024]{1,0:T(8,128)}) custom-call(f32[64,1024]{1,0:T(8,128)S(1)} %get-tuple-element.6.refs_0_, f32[8,64,1024]{2,1,0:T(8,128)S(1)} %get-tuple-element.7.refs_1_, f32[64,1024]{1,0:T(8,128)S(1)} %get-tuple-element.8.refs_2_), custom_call_target="tpu_custom_call" | custom-call | tf_op jit(solution)/shard_map/pallas_call | solution.py:727

commit v12 on v8

--- a/solution.py
+++ b/solution.py
@@ -294,9 +294,10 @@
                 tiles3[r * tile_cols + u] = value[:, u * TC : (u + 1) * TC]
 
         x_copies = []
-        for i in range(2):
-            for rr in range(TR // 2):
-                x_send[i, :, rr * TC : (rr + 1) * TC] = tiles3[:, i * (TR // 2) + rr, :]
+        per_chunk = wide // TC
+        for i in range(n_chunks):
+            for rr in range(per_chunk):
+                x_send[i, :, rr * TC : (rr + 1) * TC] = tiles3[:, i * per_chunk + rr, :]
             copy = send(x_send.at[i], x_recv.at[i], x_ss.at[i], x_rs.at[i], partner)
             copy.start()
             x_copies.append(copy)
@@ -348,23 +349,22 @@
         def columns(c, count=1):
             return slice(c * wide, (c + count) * wide)
 
-        def pack_tiles(f, pair, source):
+        def pack_tiles(f, c, source):
             for i, piece in enumerate(two_parts(source)):
-                rhs[i * tiles : (i + 1) * tiles, columns(pair, 2)] = piece
-            for c in (pair, pair + 1):
-                packed = jnp.dot(
-                    lhs1[f * half : (f + 1) * half],
-                    rhs[:, columns(c)],
-                    preferred_element_type=F32,
-                )
-                send1[c % 2, c // 2, f] = packed.reshape(RING, RING, CAP, wide)
-                if f == 1:
-                    for d in FARTHEST_FIRST:
-                        slots1[c, f, d].start()
-                recv1[c % 2, c // 2, :, f, 0] = send1[c % 2, c // 2, f, 0] if c % 2 == 0 else send1[c % 2, c // 2, f, :, 0]
-
-        for pair in (0, 2):
-            pack_tiles(0, pair, x_send[pair // 2])
+                rhs[i * tiles : (i + 1) * tiles, columns(c)] = piece
+            packed = jnp.dot(
+                lhs1[f * half : (f + 1) * half],
+                rhs[:, columns(c)],
+                preferred_element_type=F32,
+            )
+            send1[c % 2, c // 2, f] = packed.reshape(RING, RING, CAP, wide)
+            if f == 1:
+                for d in FARTHEST_FIRST:
+                    slots1[c, f, d].start()
+            recv1[c % 2, c // 2, :, f, 0] = send1[c % 2, c // 2, f, 0] if c % 2 == 0 else send1[c % 2, c // 2, f, :, 0]
+
+        for c in range(n_chunks):
+            pack_tiles(0, c, x_send[c])
         for d in FARTHEST_FIRST:
             for h in range(2):
                 slots1[h, 0, d].start()
@@ -397,9 +397,9 @@
                         [piece, piece], axis=1
                     )
 
-        for pair in (0, 2):
-            x_copies[pair // 2].wait_recv()
-            pack_tiles(1, pair, x_recv[pair // 2])
+        for c in range(n_chunks):
+            x_copies[c].wait_recv()
+            pack_tiles(1, c, x_recv[c])
 
         for h in range(2):
             for d in range(RING):
@@ -574,7 +574,7 @@
         xa_copies = []
         for c in range(n_chunks):
             xa_send[c] = gathered(c, 1)
-            copy = send(xa_send.at[c], xa_recv.at[c], x_ss.at[2 + c], x_rs.at[2 + c], partner)
+            copy = send(xa_send.at[c], xa_recv.at[c], x_ss.at[n_chunks + c], x_rs.at[n_chunks + c], partner)
             copy.start()
             xa_copies.append(copy)
         sums = [gathered(c, 0) for c in range(n_chunks)]
@@ -669,7 +669,7 @@
         *pair(2, RING, tiles, LANES),
         vmem(2, RING, 2 * tiles, 4 * tiles, dtype=BF16),
         vmem(2, RING, LANES, 4 * tiles, dtype=BF16),
-        *pair(2, tiles, tile // 2),
+        *pair(n_chunks, tiles, wide),
         *pair(n_chunks, tiles, wide),
         vmem(2, n_chunks // 2, 2, RING, RING, CAP, wide),
         vmem(2, n_chunks // 2, RING, 2, RING, CAP, wide),
@@ -680,7 +680,7 @@
         vmem(2, n_chunks // 2, 2, RING, RING, CAP, wide),
         dma((9,)),
         *[dma((2,)) for _ in range(6)],
-        dma((2 + n_chunks,)), dma((2 + n_chunks,)),
+        dma((2 * n_chunks,)), dma((2 * n_chunks,)),
         dma((1,)), dma((1,)),
         dma((1,)), dma((1,)),
         dma((1,)), dma((2 + n_chunks,)),

time: 63.1 us -> 63.1 us (level)
  no operation moved by 1% of the time
where the time goes in v12:
time: 63.1 us; the launch traced here: 63 us
  Pallas kernels  62.4 us (99%)
  between operations  0.64 us (1%)
    pallas_call x1, Pallas kernels, local(): call(*(pltpu.with_memory_space_constraint(x, pltpu.HBM) for x in operands))  60.9 us
    pallas_call x1, Pallas kernels, write_out(): pl.pallas_call(kernel, out_shape=tuple((jax.ShapeDtypeStruct(x.shape, x.d...  1.51 us

profile of v12, /device:TPU:0, one launch (start us, length us, event | category | flops | bytes accessed | tf_op | source)
XLA Modules:
  0.0 63.0 jit_solution(14790539207547842504)
XLA Ops:
  0.6 60.9 %shard_map.103 = (f32[64,1024]{1,0:T(8,128)S(1)}, f32[8,64,1024]{2,1,0:T(8,128)S(1)}, f32[64,1024]{1,0:T(8,128)S(1)}) custom-call(f32[8,64,1024]{2,1,0:T(8,128)} %temp.1, f32[64,1024]{1,0:T(8,128)} %cond.1, f32[8,64,1024]{2,1,0:T(8,128)} %adj.1, f32[64,1024]{1,0:T(8,128)} %grad.1, f32[4,64,1024]{2,1,0:T(8,128)} %obs.1, s32[1,64]{1,0:T(1,128)} %bitcast.5, ...), custom_call_target="tpu_custom_call" | custom-call | tf_op jit(solution)/shard_map/pallas_call | solution.py:740
  61.5 1.5 %shard_map.104 = (f32[64,1024]{1,0:T(8,128)}, f32[8,64,1024]{2,1,0:T(8,128)}, f32[64,1024]{1,0:T(8,128)}) custom-call(f32[64,1024]{1,0:T(8,128)S(1)} %get-tuple-element.6.refs_0_, f32[8,64,1024]{2,1,0:T(8,128)S(1)} %get-tuple-element.7.refs_1_, f32[64,1024]{1,0:T(8,128)S(1)} %get-tuple-element.8.refs_2_), custom_call_target="tpu_custom_call" | custom-call | tf_op jit(solution)/shard_map/pallas_call | solution.py:721
